TPU v7x, 32 devices: a whole 2x2x4 slice. The times are simulated.
32 devices in a mesh: comp: 4 (over y, x), dom: 8 (over z, core).
Axes of the slice: x: 2, y: 2, z: 4, core: 2. Of those that a mesh axis runs over, the one named last changes fastest.
Arguments:
- atm_state: float32 [4, 4, 128, 16, 1024], P('comp', None, None, None, 'dom'), may hold values from -6 to 6
- elem_nbr: int32 [4, 4, 1024], P('comp', None, 'dom'), may hold values from 0 to 3071, as said below
- elem_metric: float32 [4, 16, 1024], P('comp', None, 'dom'), may hold values from 0.02 to 0.2
- bulk_coef: float32 [4, 16, 1024], P('comp', None, 'dom'), may hold values from 0.2 to 2
- stiffness: float32 [16, 16], replicated, may hold values from -1.5 to 1.5
- coupling: float32 [4, 16, 16], replicated, may hold values from -1.5 to 1.5
- atm_vertical: float32 [128, 128], replicated, may hold values from -0.25 to 0.25
- ocean_state: float32 [4, 4, 80, 8192], P('comp', None, None, 'dom'), may hold values from -6 to 6
- cell_nbr: int32 [4, 6, 8192], P('comp', None, 'dom'), may hold values from 0 to 8191, as said below
- cell_diff: float32 [4, 6, 8192], P('comp', None, 'dom'), may hold values from 0.01 to 0.12
- ocean_vertical: float32 [80, 80], replicated, may hold values from -0.3125 to 0.3125
- sea_mask: int32 [4, 8192], P('comp', 'dom'), may hold values 0 or 1
- pair_owner: int32 [4, 256, 1], P('comp', 'dom'), may hold values from 0 to 7, as said below
- pair_block: int32 [4, 256], P('comp', 'dom'), may hold values from 0 to 7
- pair_src: int32 [4, 256], P('comp', 'dom'), may hold values from 0 to 15
- remap_weight: float32 [4, 256, 128, 128], P('comp', 'dom'), may hold values from -0.5 to 0.5
Outputs:
- atm_next: float32 [4, 4, 128, 16, 1024], P('comp', None, None, None, 'dom')
- ocean_next: float32 [4, 4, 80, 8192], P('comp', None, None, 'dom')
Inputs may be any that keep to these rules, and one draw needn't show every extreme that they name: `elem_nbr`: each entry of the slabs c < 3 differs from its own element index c * 1024 + e by 1 to 8; the last slab repeats the first. `cell_nbr`: each entry differs from its own cell index by 1 to 128; all slabs are equal. `pair_owner`: within the rows of one device (aligned blocks of 32 rows) no owner is named by more than 8 rows; the owners one below and one above that device's index of dom (counted round) are each named by exactly 8 rows.
All inputs are finite; a program needn't handle non-finite values. No bound on the sum of `sea_mask` on one device may be relied on, other than what follows from the above.
Results may differ from a plain program's by a relative error of at most 0.0001.
Values sent between devices are 32-bit elements; how exact they have to be, the bound alone decides.
No kernel may reach another device: no remote copies, remote signals or barrier semaphores. Data moves between devices by JAX's collectives and lax.ppermute only.
A program may use at most 128 MiB of HBM per device.

v0:
```python
import jax
import jax.numpy as jnp
from jax import lax
from jax.sharding import PartitionSpec as P

RIM = 8
BLK = 128
HALO_O = 128


highest = lax.Precision.HIGHEST


def extended_2(shard, sides, width):
    for axis, dim in sides:
        devices, length = (lax.axis_size(axis), shard.shape[dim])
        up = [(i, (i + 1) % devices) for i in range(devices - 1)]
        down = [(j, i) for i, j in up]
        last = lax.slice_in_dim(shard, length - width, length, axis=dim)
        initial = lax.slice_in_dim(shard, 0, width, axis=dim)
        before = lax.ppermute(last, axis, up)
        after = lax.ppermute(initial, axis, down)
        shard = jnp.concatenate([before, shard, after], axis=dim)
    return shard


def slot_table(position, total, sender, target):
    match = (jnp.arange(total, dtype=jnp.int32)[:, None] == position[None, :]) & sender
    table = match.astype(jnp.float32)
    labels = jnp.sum(jnp.where(match, target[None, :] + 1, 0), axis=1) - 1
    return (table, labels)


def dynamics(current, extended, index, metric, flux, stiffness, coupling, atm_vertical):
    levels = current.shape[1]
    tend = jnp.einsum("pq,flqe->flpe", stiffness, current, precision=highest)
    tend = tend + jnp.einsum("lm,fmpe->flpe", atm_vertical, current, precision=highest)
    for side in range(4):
        beside = jnp.take(extended, index[side], axis=3)
        tend = tend + jnp.einsum("pq,flqe->flpe", coupling[side], beside, precision=highest)
    updated = current + metric[None, None] * tend
    return updated.at[:, levels - 1].add(-0.5 * flux)


def local(
    atm_state,
    elem_nbr,
    elem_metric,
    bulk_coef,
    stiffness,
    coupling,
    atm_vertical,
    ocean_state,
    cell_nbr,
    cell_diff,
    ocean_vertical,
    sea_mask,
    pair_owner,
    pair_block,
    pair_src,
    remap_weight,
):
    n_comp = lax.axis_size("comp")
    n_dom = lax.axis_size("dom")
    comp_index = lax.axis_index("comp")
    dom_index = lax.axis_index("dom")
    is_ocean = comp_index == n_comp - 1
    sender = jnp.logical_not(is_ocean)
    state = atm_state[0]
    fields, levels, points, elems = state.shape
    ocean = ocean_state[0]
    cells = ocean.shape[2]
    pairs = pair_block.shape[1]
    capacity = max(2, 2 * pairs // n_dom)
    owner = pair_owner[0, :, 0]
    target = pair_block[0]
    source = pair_src[0]
    weights = remap_weight[0]
    order = jnp.arange(pairs, dtype=jnp.int32)
    earlier = (owner[None, :] == owner[:, None]) & (order[None, :] < order[:, None])
    rank = jnp.sum(earlier.astype(jnp.int32), axis=1)
    total = n_comp * n_dom * capacity
    peer_pos = ((n_comp - 1) * n_dom + owner) * capacity + rank
    request_table, request_ids = slot_table(peer_pos, total, sender, target)
    ocean_blocks = cells // BLK
    top_blocks = jnp.transpose(ocean[:, 0, :].reshape(fields, ocean_blocks, BLK), (1, 0, 2))
    wanted = lax.all_to_all(
        request_ids.reshape(n_comp * n_dom, capacity),
        ("comp", "dom"),
        split_axis=0,
        concat_axis=0,
        tiled=True,
    )
    looked = jnp.take(top_blocks, jnp.maximum(wanted, 0), axis=0)
    looked = jnp.where((wanted >= 0)[:, :, None, None], looked, 0.0)
    replies = lax.all_to_all(looked, ("comp", "dom"), split_axis=0, concat_axis=0, tiled=True)
    replies = replies.reshape(total, fields, BLK)
    pair_surface = jnp.einsum("sp,sfo->pfo", request_table, replies, precision=highest)
    contrib = jnp.einsum("pfo,pao->pfa", pair_surface, weights, precision=highest)
    atm_blocks = points * elems // BLK
    block_pick = (source[:, None] == jnp.arange(atm_blocks, dtype=jnp.int32)[None, :]).astype(
        jnp.float32
    )
    surf_blocks = jnp.einsum("pb,pfa->bfa", block_pick, contrib, precision=highest)
    surface = jnp.transpose(
        surf_blocks.reshape(points, elems // BLK, fields, BLK), (2, 0, 1, 3)
    ).reshape(fields, points, elems)
    flux = bulk_coef[0][None] * (state[:, levels - 1] - surface)
    flux_blocks = jnp.transpose(
        flux.reshape(fields, points, elems // BLK, BLK), (1, 2, 0, 3)
    ).reshape(atm_blocks, fields, BLK)
    pair_flux = jnp.einsum("pb,bfa->pfa", block_pick, flux_blocks, precision=highest)
    sent = jnp.einsum("pfa,pao->pfo", pair_flux, weights, precision=highest)
    values = jnp.einsum("sp,pfo->sfo", request_table, sent, precision=highest)
    arrived, arrived_ids = (
        lax.all_to_all(values, ("comp", "dom"), split_axis=0, concat_axis=0, tiled=True),
        lax.all_to_all(request_ids, ("comp", "dom"), split_axis=0, concat_axis=0, tiled=True),
    )
    joined = comp_index * n_dom + dom_index
    element_index = elem_nbr[0] - joined * elems + RIM
    metric = elem_metric[0]
    for step in range(2):
        current = state
        extended = extended_2(current, ((("comp", "dom"), 3),), RIM)

        def atmosphere_work():
            return dynamics(
                current, extended, element_index, metric, flux, stiffness, coupling, atm_vertical
            )

        state = lax.cond(sender, atmosphere_work, lambda: jnp.zeros_like(current))
    ocean_ext = extended_2(ocean, (("dom", 2),), HALO_O)
    cell_index = cell_nbr[0] - dom_index * cells + HALO_O

    def ocean_work():
        receive = (
            arrived_ids[None, :] == jnp.arange(ocean_blocks, dtype=jnp.int32)[:, None]
        ).astype(jnp.float32)
        block_flux = jnp.einsum("bs,sfo->bfo", receive, arrived, precision=highest)
        oflux = jnp.transpose(block_flux, (1, 0, 2)).reshape(fields, cells)
        lap = jnp.zeros_like(ocean)
        for side in range(cell_index.shape[0]):
            lap = lap + cell_diff[0, side][None, None] * (
                jnp.take(ocean_ext, cell_index[side], axis=2) - ocean
            )
        fresh = ocean + lap + jnp.einsum("lm,fmc->flc", ocean_vertical, ocean, precision=highest)
        fresh = fresh.at[:, 0].add(0.5 * oflux)
        return jnp.where(sea_mask[0][None, None] == 1, fresh, ocean)

    ocean_next = lax.cond(is_ocean, ocean_work, lambda: jnp.zeros_like(ocean))
    return (state[None], ocean_next[None])


def solution(mesh):
    in_specs = (
        P("comp", None, None, None, "dom"),
        P("comp", None, "dom"),
        P("comp", None, "dom"),
        P("comp", None, "dom"),
        P(),
        P(),
        P(),
        P("comp", None, None, "dom"),
        P("comp", None, "dom"),
        P("comp", None, "dom"),
        P(),
        P("comp", "dom"),
        P("comp", "dom", None),
        P("comp", "dom"),
        P("comp", "dom"),
        P("comp", "dom", None, None),
    )
    out_specs = (P("comp", None, None, None, "dom"), P("comp", None, None, "dom"))
    return jax.shard_map(local, mesh=mesh, in_specs=in_specs, out_specs=out_specs, check_vma=False)
```

profile of v0, /device:TPU:4, one launch (start us, length us, event | category | flops | bytes accessed | tf_op | source)
XLA Modules:
  0.0 359.1 jit_solution(3530712865904206979)
XLA Ops:
  3.8 6.1 %all-to-all-start = ((s32[32,1,8]{2,1,0:T(1,128)}), s32[32,1,8]{2,1,0:T(1,128)S(1)}, u32[]{:S(2)}, u32[]{:S(2)}) async-start(s32[32,1,8]{2,1,0:T(1,128)} %bitcast.101), calls=%async_computation | async-start | bytes 32768 | tf_op jit(solution)/shard_map/all_to_all | solution.py:87
  10.8 5.0 %all-to-all-done = s32[32,1,8]{2,1,0:T(1,128)S(1)} async-done(((s32[32,1,8]{2,1,0:T(1,128)}), s32[32,1,8]{2,1,0:T(1,128)S(1)}, u32[]{:S(2)}, u32[]{:S(2)}) %all-to-all-start) | async-done | bytes 1056 | tf_op jit(solution)/shard_map/all_to_all | solution.py:87
  18.2 3.7 %all-to-all-start.1 = ((f32[32,8,4,128]{3,1,2,0:T(8,128)}), f32[32,8,4,128]{3,1,2,0:T(8,128)S(1)}, u32[]{:S(2)}, u32[]{:S(2)}) async-start(f32[32,8,4,128]{3,1,2,0:T(8,128)} %fusion.75), calls=%async_computation.1 | async-start | bytes 1048576 | tf_op jit(solution)/shard_map/all_to_all | solution.py:96
  21.8 2.7 copy.284
  24.6 4.7 %fusion.107 = (f32[4,128,16,8]{3,2,0,1:T(8,128)}, f32[4,128,16,8]{3,2,0,1:T(8,128)}) fusion(f32[4,128,16,128]{3,2,0,1:T(8,128)S(1)} %bitcast.334), kind=kLoop, calls=%fused_computation.204 | loop fusion | bytes 1048576 | tf_op jit(solution)/shard_map/slice | solution.py:19
  29.3 3.7 %copy.207 = f32[4,128,16,8]{1,3,2,0:T(8,128)S(1)} copy(f32[4,128,16,8]{3,2,0,1:T(8,128)} %get-tuple-element.321) | data formatting | bytes 524288 | tf_op jit(solution)/shard_map/slice | solution.py:19
  33.0 2.1 collective-permute-start
  35.1 3.7 %copy.208 = f32[4,128,16,8]{1,3,2,0:T(8,128)S(1)} copy(f32[4,128,16,8]{3,2,0,1:T(8,128)} %get-tuple-element.322) | data formatting | bytes 524288 | tf_op jit(solution)/shard_map/slice | solution.py:20
  38.8 7.1 %collective-permute-start.1 = (f32[4,128,16,8]{1,3,2,0:T(8,128)S(1)}, f32[4,128,16,8]{1,3,2,0:T(8,128)}, u32[]{:S(2)}, u32[]{:S(2)}) collective-permute-start(f32[4,128,16,8]{1,3,2,0:T(8,128)S(1)} %copy.208), channel_id=1, source_target_pairs={{1,0},{2,1},{3,2},{4,3},{5,4},{6,5},{7,6},{8,7},{9,8},{10,9},{11,1... | collective-permute-start | bytes 786440 | tf_op jit(solution)/shard_map/ppermute | solution.py:22
  45.9 1.7 fusion.108
  47.7 2.0 collective-permute-start.4
  49.6 1.3 collective-permute-start.5
  51.6 4.4 %copy.209 = f32[4,128,16,8]{3,2,0,1:T(8,128)} copy(f32[4,128,16,8]{1,3,2,0:T(8,128)S(1)} %collective-permute-done) | data formatting | bytes 524288 | tf_op jit(solution)/shard_map/ppermute | solution.py:21
  56.0 5.3 %copy.210 = f32[4,128,16,8]{3,2,0,1:T(8,128)} copy(f32[4,128,16,8]{1,3,2,0:T(8,128)} %collective-permute-done.1) | data formatting | bytes 524288 | tf_op jit(solution)/shard_map/ppermute | solution.py:22
  61.4 5.1 %all-to-all-start.2 = ((s32[32,8,1]{1,2,0:T(1,128)}), s32[32,8,1]{1,2,0:T(1,128)S(1)}, u32[]{:S(2)}, u32[]{:S(2)}) async-start(s32[32,8,1]{1,2,0:T(1,128)} %bitcast.113), calls=%async_computation.2 | async-start | bytes 32768 | tf_op jit(solution)/shard_map/all_to_all | solution.py:117
  66.8 3.4 fusion.70
  72.1 1.9 fusion.68
  75.6 5.8 %all-to-all-start.3 = ((f32[256,4,128]{2,1,0:T(4,128)}), f32[256,4,128]{2,1,0:T(4,128)S(1)}, u32[]{:S(2)}, u32[]{:S(2)}) async-start(f32[256,4,128]{2,1,0:T(4,128)} %copy.230), calls=%async_computation.3 | async-start | bytes 1048576 | tf_op jit(solution)/shard_map/all_to_all | solution.py:116
  81.4 8.8 %pad_maximum_fusion = f32[4,128,16,144]{3,2,0,1:T(8,128)} fusion(f32[4,128,16,8]{3,2,0,1:T(8,128)} %copy.210, f32[4,128,16,128]{3,2,0,1:T(8,128)} %bitcast.337, f32[4,128,16,8]{3,2,0,1:T(8,128)} %copy.209), kind=kLoop, calls=%fused_computation.149 | loop fusion | flops 2359296 | bytes 9437184 | tf_op jit(solution)/shard_map/concatenate | solution.py:23
  90.3 117.7 %conditional.3 = (f32[4,128,16,128]{3,2,1,0:T(8,128)}) conditional(s32[]{:T(128)} %convert_element_type.6, () %tuple.48, (f32[1,16,128]{2,1,0:T(8,128)S(1)}, f32[4,128,16,128]{3,2,0,1:T(8,128)}, f32[16,16]{1,0:T(8,128)S(1)}, f32[128,128]{1,0:T(8,128)S(1)}, s32[4,128]{1,0:T(4,128)S(1)}, /*index=5*/f32[4,128,16,144]{3,2,0,1:T(8,128)}, ...), branch_computations={%region_2.3_spmd, %region_3.5_spmd} | conditional | flops 2628803584 | bytes 248744064 | solution.py:131
  90.9 9.1 %copy.223 = f32[4,128,16,144]{1,2,0,3:T(8,128)} copy(f32[4,128,16,144]{3,2,0,1:T(8,128)} %get-tuple-element.253) | data formatting | bytes 9437184 | tf_op jit(solution)/shard_map
  100.0 5.1 %gather_fusion = f32[128,4,128,16]{2,3,1,0:T(8,128)} fusion(f32[4,128,16,144]{1,2,0,3:T(8,128)} %copy.223, s32[1024]{0:T(1024)S(1)} %pad_clamp_fusion.3), kind=kCustom, calls=%fused_computation.clone | custom fusion | bytes 8389120 | tf_op jit(solution)/shard_map/cond/branch_1_fun/jit(_take)/gather | solution.py:39
  105.1 5.1 %gather_fusion.1 = f32[128,4,128,16]{2,3,1,0:T(8,128)} fusion(f32[4,128,16,144]{1,2,0,3:T(8,128)} %copy.223, s32[1024]{0:T(1024)S(1)} %pad_clamp_fusion.2), kind=kCustom, calls=%fused_computation.2.clone | custom fusion | bytes 8389120 | tf_op jit(solution)/shard_map/cond/branch_1_fun/jit(_take)/gather | solution.py:39
  110.2 5.9 %select_bitcast_fusion.2 = (f32[4,128,16,128]{1,2,0,3:T(8,128)}, f32[4,128,16,128]{1,2,0,3:T(8,128)}) fusion(f32[128,4,128,16]{2,3,1,0:T(8,128)} %gather_fusion.1, pred[128]{0:T(512)(128)(4,1)S(1)} %get-tuple-element.301, f32[128,4,128,16]{2,3,1,0:T(8,128)} %gather_fusion, pred[128]{0:T(512)(128)(4,1)S(1)} %get-tuple-element.265), kind=kLoop, calls=%fused_computation.26 | loop fusion | flops 2097152 | bytes 16777472 | tf_op jit(solution)/shard_map/cond/branch_1_fun/jit(_take)/select_n | solution.py:39
  116.2 5.9 %copy.190 = f32[4,128,16,128]{3,2,1,0:T(8,128)} copy(f32[4,128,16,128]{1,2,0,3:T(8,128)} %get-tuple-element.307) | data formatting | bytes 8388608 | tf_op jit(solution)/shard_map/cond/branch_1_fun/jit(_take)/select_n | solution.py:39
  122.1 7.8 %fusion.14 = f32[4,128,128,16]{2,3,1,0:T(8,128)} fusion(f32[4,128,16,128]{3,2,1,0:T(8,128)} %copy.190, f32[4,16,16]{2,1,0:T(8,128)S(1)} %get-tuple-element.134), kind=kOutput, calls=%fused_computation.37 | convolution fusion | flops 201326592 | bytes 8396800 | tf_op jit(solution)/shard_map/cond/branch_1_fun/pq,flqe->flpe/dot_general | solution.py:40
  129.9 5.9 %copy.189 = f32[4,128,16,128]{3,2,1,0:T(8,128)} copy(f32[4,128,16,128]{1,2,0,3:T(8,128)} %get-tuple-element.308) | data formatting | bytes 8388608 | tf_op jit(solution)/shard_map/cond/branch_1_fun/jit(_take)/select_n | solution.py:39
  135.8 7.9 %fusion.16 = f32[4,128,128,16]{2,3,1,0:T(8,128)} fusion(f32[4,128,16,128]{3,2,1,0:T(8,128)} %copy.189, f32[4,16,16]{2,1,0:T(8,128)S(1)} %get-tuple-element.134), kind=kOutput, calls=%fused_computation.39 | convolution fusion | flops 201326592 | bytes 8396800 | tf_op jit(solution)/shard_map/cond/branch_1_fun/pq,flqe->flpe/dot_general | solution.py:40
  143.7 5.2 %gather_fusion.2 = f32[128,4,128,16]{2,3,1,0:T(8,128)} fusion(f32[4,128,16,144]{1,2,0,3:T(8,128)} %copy.223, s32[1024]{0:T(1024)S(1)} %pad_clamp_fusion.1), kind=kCustom, calls=%fused_computation.3.clone | custom fusion | bytes 8389120 | tf_op jit(solution)/shard_map/cond/branch_1_fun/jit(_take)/gather | solution.py:39
  148.8 5.1 %gather_fusion.3 = f32[128,4,128,16]{2,3,1,0:T(8,128)} fusion(f32[4,128,16,144]{1,2,0,3:T(8,128)} %copy.223, s32[1024]{0:T(1024)S(1)} %pad_clamp_fusion), kind=kCustom, calls=%fused_computation.4.clone | custom fusion | bytes 8389120 | tf_op jit(solution)/shard_map/cond/branch_1_fun/jit(_take)/gather | solution.py:39
  153.9 6.0 %select_bitcast_fusion = (f32[4,128,16,128]{1,2,0,3:T(8,128)}, f32[4,128,16,128]{1,2,0,3:T(8,128)}) fusion(f32[128,4,128,16]{2,3,1,0:T(8,128)} %gather_fusion.3, pred[128]{0:T(512)(128)(4,1)S(1)} %get-tuple-element.303, f32[128,4,128,16]{2,3,1,0:T(8,128)} %gather_fusion.2, pred[128]{0:T(512)(128)(4,1)S(1)} %get-tuple-element.299), kind=kLoop, calls=%fused_computation.24 | loop fusion | flops 2097152 | bytes 16777472 | tf_op jit(solution)/shard_map/cond/branch_1_fun/jit(_take)/select_n | solution.py:39
  159.9 6.0 %copy.192 = f32[4,128,16,128]{3,2,1,0:T(8,128)} copy(f32[4,128,16,128]{1,2,0,3:T(8,128)} %get-tuple-element.305) | data formatting | bytes 8388608 | tf_op jit(solution)/shard_map/cond/branch_1_fun/jit(_take)/select_n | solution.py:39
  166.0 7.9 %fusion.10 = f32[4,128,128,16]{2,3,1,0:T(8,128)} fusion(f32[4,128,16,128]{3,2,1,0:T(8,128)} %copy.192, f32[4,16,16]{2,1,0:T(8,128)S(1)} %get-tuple-element.134), kind=kOutput, calls=%fused_computation.33 | convolution fusion | flops 201326592 | bytes 8396800 | tf_op jit(solution)/shard_map/cond/branch_1_fun/pq,flqe->flpe/dot_general | solution.py:40
  173.9 5.9 %copy.191 = f32[4,128,16,128]{3,2,1,0:T(8,128)} copy(f32[4,128,16,128]{1,2,0,3:T(8,128)} %get-tuple-element.306) | data formatting | bytes 8388608 | tf_op jit(solution)/shard_map/cond/branch_1_fun/jit(_take)/select_n | solution.py:39
  179.8 8.0 %fusion.12 = f32[4,128,128,16]{2,3,1,0:T(8,128)} fusion(f32[4,128,16,128]{3,2,1,0:T(8,128)} %copy.191, f32[4,16,16]{2,1,0:T(8,128)S(1)} %get-tuple-element.134), kind=kOutput, calls=%fused_computation.35 | convolution fusion | flops 201326592 | bytes 8396800 | tf_op jit(solution)/shard_map/cond/branch_1_fun/pq,flqe->flpe/dot_general | solution.py:40
  187.9 7.1 %fusion.2 = f32[4,16,128,128]{2,3,1,0:T(8,128)} fusion(f32[4,128,16,128]{3,2,0,1:T(8,128)S(1)} %copy-done.3, f32[128,128]{1,0:T(8,128)S(1)} %get-tuple-element.131), kind=kOutput, calls=%fused_computation.22 | convolution fusion | flops 1610612736 | bytes 8454144 | tf_op jit(solution)/shard_map/cond/branch_1_fun/lm,fmpe->flpe/dot_general | solution.py:37
  195.0 11.3 %fusion.1 = f32[4,128,16,128]{3,2,1,0:T(8,128)} fusion(f32[4,128,128,16]{2,3,1,0:T(8,128)S(1)} %copy-done.7, f32[4,128,128,16]{2,3,1,0:T(8,128)} %fusion.12, f32[4,128,128,16]{2,3,1,0:T(8,128)S(1)} %copy-done.5, f32[4,128,128,16]{2,3,1,0:T(8,128)S(1)} %copy-done.6, f32[4,16,128,128]{2,3,1,0:T(8,128)} %fusion.2, f32[4,128,16,128]{3,2,0,1:T(8,128)S(1)} %copy-done.3, ...), kind=kOutput, calls=%fused_computation.17 | convolution fusion | flops 208666624 | bytes 29369344 | tf_op jit(solution)/shard_map/cond/branch_1_fun/pq,flqe->flpe/dot_general | solution.py:36
  206.3 1.4 fusion.9
  208.0 5.9 %copy.224 = f32[4,128,16,128]{1,2,0,3:T(8,128)} copy(f32[4,128,16,128]{3,2,1,0:T(8,128)} %get-tuple-element.329) | data formatting | bytes 8388608 | tf_op jit(solution)/shard_map/cond | solution.py:131
  215.1 2.2 collective-permute-start.2
  217.3 7.1 %collective-permute-start.3 = (f32[4,128,16,8]{1,2,0,3:T(8,128)S(1)}, f32[4,128,16,8]{1,2,0,3:T(8,128)S(1)}, u32[]{:S(2)}, u32[]{:S(2)}) collective-permute-start(f32[4,128,16,8]{1,2,0,3:T(8,128)S(1)} %get-tuple-element.320), channel_id=1, source_target_pairs={{1,0},{2,1},{3,2},{4,3},{5,4},{6,5},{7,6},{8,7},{9,8},{10,9},{11,1... | collective-permute-start | bytes 786440 | tf_op jit(solution)/shard_map/ppermute | solution.py:22
  224.4 2.3 pad_maximum_fusion.2
  226.7 1.6 collective-permute-done.3
  228.3 2.6 pad_maximum_fusion.1
  230.8 125.2 %conditional.4 = (f32[1,4,128,16,128]{4,3,2,1,0:T(8,128)}) conditional(s32[]{:T(128)} %convert_element_type.6, () %tuple.47, (f32[1,16,128]{2,1,0:T(8,128)S(1)}, f32[4,128,16,128]{3,2,1,0:T(8,128)}, f32[16,16]{1,0:T(8,128)S(1)}, f32[128,128]{1,0:T(8,128)S(1)}, s32[4,128]{1,0:T(4,128)S(1)}, /*index=5*/f32[4,128,16,144]{1,2,0,3:T(8,128)}, ...), branch_computations={%region_4.6_spmd, %region_5.7_spmd} | conditional | flops 2628803584 | bytes 235112544 | solution.py:131
  230.9 5.1 %gather_fusion.4 = f32[128,4,128,16]{2,3,1,0:T(8,128)} fusion(f32[4,128,16,144]{1,2,0,3:T(8,128)} %get-tuple-element.140, s32[1024]{0:T(1024)S(1)} %pad_clamp_fusion.7), kind=kCustom, calls=%fused_computation.5.clone | custom fusion | bytes 8389120 | tf_op jit(solution)/shard_map/cond/branch_1_fun/jit(_take)/gather | solution.py:39
  236.0 5.2 %gather_fusion.5 = f32[128,4,128,16]{2,3,1,0:T(8,128)} fusion(f32[4,128,16,144]{1,2,0,3:T(8,128)} %get-tuple-element.140, s32[1024]{0:T(1024)S(1)} %pad_clamp_fusion.6), kind=kCustom, calls=%fused_computation.6.clone | custom fusion | bytes 8389120 | tf_op jit(solution)/shard_map/cond/branch_1_fun/jit(_take)/gather | solution.py:39
  241.2 6.0 %select_bitcast_fusion.6 = (f32[4,128,16,128]{1,2,0,3:T(8,128)}, f32[4,128,16,128]{1,2,0,3:T(8,128)}) fusion(f32[128,4,128,16]{2,3,1,0:T(8,128)} %gather_fusion.5, pred[128]{0:T(512)(128)(4,1)S(1)} %get-tuple-element.311, f32[128,4,128,16]{2,3,1,0:T(8,128)} %gather_fusion.4, pred[128]{0:T(512)(128)(4,1)S(1)} %get-tuple-element.313), kind=kLoop, calls=%fused_computation.69 | loop fusion | flops 2097152 | bytes 16777472 | tf_op jit(solution)/shard_map/cond/branch_1_fun/jit(_take)/select_n | solution.py:39
  247.2 5.9 %copy.196 = f32[4,128,16,128]{3,2,1,0:T(8,128)} copy(f32[4,128,16,128]{1,2,0,3:T(8,128)} %get-tuple-element.317) | data formatting | bytes 8388608 | tf_op jit(solution)/shard_map/cond/branch_1_fun/jit(_take)/select_n | solution.py:39
  253.1 7.9 %fusion.33 = f32[4,128,128,16]{2,3,1,0:T(8,128)} fusion(f32[4,128,16,128]{3,2,1,0:T(8,128)} %copy.196, f32[4,16,16]{2,1,0:T(8,128)S(1)} %get-tuple-element.142), kind=kOutput, calls=%fused_computation.78 | convolution fusion | flops 201326592 | bytes 8396800 | tf_op jit(solution)/shard_map/cond/branch_1_fun/pq,flqe->flpe/dot_general | solution.py:40
  260.9 5.8 %copy.195 = f32[4,128,16,128]{3,2,1,0:T(8,128)} copy(f32[4,128,16,128]{1,2,0,3:T(8,128)} %get-tuple-element.318) | data formatting | bytes 8388608 | tf_op jit(solution)/shard_map/cond/branch_1_fun/jit(_take)/select_n | solution.py:39
  266.8 8.0 %fusion.35 = f32[4,128,128,16]{2,3,1,0:T(8,128)} fusion(f32[4,128,16,128]{3,2,1,0:T(8,128)} %copy.195, f32[4,16,16]{2,1,0:T(8,128)S(1)} %get-tuple-element.142), kind=kOutput, calls=%fused_computation.80 | convolution fusion | flops 201326592 | bytes 8396800 | tf_op jit(solution)/shard_map/cond/branch_1_fun/pq,flqe->flpe/dot_general | solution.py:40
  274.8 5.1 %gather_fusion.6 = f32[128,4,128,16]{2,3,1,0:T(8,128)} fusion(f32[4,128,16,144]{1,2,0,3:T(8,128)} %get-tuple-element.140, s32[1024]{0:T(1024)S(1)} %pad_clamp_fusion.5), kind=kCustom, calls=%fused_computation.7.clone | custom fusion | bytes 8389120 | tf_op jit(solution)/shard_map/cond/branch_1_fun/jit(_take)/gather | solution.py:39
  279.9 5.2 %gather_fusion.7 = f32[128,4,128,16]{2,3,1,0:T(8,128)} fusion(f32[4,128,16,144]{1,2,0,3:T(8,128)} %get-tuple-element.140, s32[1024]{0:T(1024)S(1)} %pad_clamp_fusion.4), kind=kCustom, calls=%fused_computation.8.clone | custom fusion | bytes 8389120 | tf_op jit(solution)/shard_map/cond/branch_1_fun/jit(_take)/gather | solution.py:39
  285.1 6.1 %select_bitcast_fusion.4 = (f32[4,128,16,128]{1,2,0,3:T(8,128)}, f32[4,128,16,128]{1,2,0,3:T(8,128)}) fusion(f32[128,4,128,16]{2,3,1,0:T(8,128)} %gather_fusion.7, pred[128]{0:T(512)(128)(4,1)S(1)} %get-tuple-element.273, f32[128,4,128,16]{2,3,1,0:T(8,128)} %gather_fusion.6, pred[128]{0:T(512)(128)(4,1)S(1)} %get-tuple-element.309), kind=kLoop, calls=%fused_computation.67 | loop fusion | flops 2097152 | bytes 16777472 | tf_op jit(solution)/shard_map/cond/branch_1_fun/jit(_take)/select_n | solution.py:39
  291.1 17.2 %copy.197 = f32[4,128,16,128]{3,2,1,0:T(8,128)} copy(f32[4,128,16,128]{1,2,0,3:T(8,128)} %get-tuple-element.316) | data formatting | bytes 8388608 | tf_op jit(solution)/shard_map/cond/branch_1_fun/jit(_take)/select_n | solution.py:39
  308.3 7.9 %fusion.31 = f32[4,128,128,16]{2,3,1,0:T(8,128)} fusion(f32[4,128,16,128]{3,2,1,0:T(8,128)} %copy.197, f32[4,16,16]{2,1,0:T(8,128)S(1)} %get-tuple-element.142), kind=kOutput, calls=%fused_computation.76 | convolution fusion | flops 201326592 | bytes 8396800 | tf_op jit(solution)/shard_map/cond/branch_1_fun/pq,flqe->flpe/dot_general | solution.py:40
  316.2 5.8 %copy.198 = f32[4,128,16,128]{3,2,1,0:T(8,128)} copy(f32[4,128,16,128]{1,2,0,3:T(8,128)} %get-tuple-element.315) | data formatting | bytes 8388608 | tf_op jit(solution)/shard_map/cond/branch_1_fun/jit(_take)/select_n | solution.py:39
  322.0 9.3 %fusion.25 = f32[4,16,128,128]{2,3,1,0:T(8,128)} fusion(f32[4,128,16,128]{3,2,1,0:T(8,128)} %get-tuple-element.136, f32[128,128]{1,0:T(8,128)S(1)} %get-tuple-element.139), kind=kOutput, calls=%fused_computation.65 | convolution fusion | flops 1610612736 | bytes 8454144 | tf_op jit(solution)/shard_map/cond/branch_1_fun/lm,fmpe->flpe/dot_general | solution.py:37
  331.3 8.0 %fusion.37 = f32[4,128,128,16]{2,3,1,0:T(8,128)} fusion(f32[4,128,16,128]{3,2,1,0:T(8,128)} %get-tuple-element.136, f32[16,16]{1,0:T(8,128)S(1)} %get-tuple-element.138), kind=kOutput, calls=%fused_computation.82 | convolution fusion | flops 201326592 | bytes 8389632 | tf_op jit(solution)/shard_map/cond/branch_1_fun/pq,flqe->flpe/dot_general | solution.py:36
  339.3 13.8 %fusion.24 = f32[4,128,16,128]{3,2,1,0:T(8,128)S(1)} fusion(f32[4,128,16,128]{3,2,1,0:T(8,128)} %get-tuple-element.136, f32[4,128,128,16]{2,3,1,0:T(8,128)S(1)} %copy-done.10, f32[4,128,128,16]{2,3,1,0:T(8,128)S(1)} %copy-done.8, f32[4,128,128,16]{2,3,1,0:T(8,128)S(1)} %copy-done.9, f32[4,128,128,16]{2,3,1,0:T(8,128)} %fusion.37, ...), kind=kOutput, calls=%fused_computation.60 | convolution fusion | flops 208666624 | bytes 33570816 | tf_op jit(solution)/shard_map/cond/branch_1_fun/pq,flqe->flpe/dot_general | solution.py:40
  353.1 2.0 copy.287
  356.1 1.2 conditional.5
  357.3 1.6 copy-done.1
  (91 shorter events, 14.2 us)
Async XLA Ops:
  0.6 66.2 %copy-start = (f32[1,32,128,128]{3,2,1,0:T(8,128)S(1)}, f32[1,32,128,128]{3,2,1,0:T(8,128)}, u32[]{:S(2)}) copy-start(f32[1,32,128,128]{3,2,1,0:T(8,128)} %param.47) | copy-start | bytes 6291460
  3.8 12.0 %all-to-all-start = ((s32[32,1,8]{2,1,0:T(1,128)}), s32[32,1,8]{2,1,0:T(1,128)S(1)}, u32[]{:S(2)}, u32[]{:S(2)}) async-start(s32[32,1,8]{2,1,0:T(1,128)} %bitcast.101), calls=%async_computation | async-start | bytes 32768 | tf_op jit(solution)/shard_map/all_to_all | solution.py:87
  18.2 43.2 %all-to-all-start.1 = ((f32[32,8,4,128]{3,1,2,0:T(8,128)}), f32[32,8,4,128]{3,1,2,0:T(8,128)S(1)}, u32[]{:S(2)}, u32[]{:S(2)}) async-start(f32[32,8,4,128]{3,1,2,0:T(8,128)} %fusion.75), calls=%async_computation.1 | async-start | bytes 1048576 | tf_op jit(solution)/shard_map/all_to_all | solution.py:96
  24.5 4.8 %copy-start.2 = (f32[1,4,128,16,128]{4,3,1,2,0:T(8,128)}, f32[1,4,128,16,128]{4,3,1,2,0:T(8,128)S(1)}, u32[]{:S(2)}) copy-start(f32[1,4,128,16,128]{4,3,1,2,0:T(8,128)S(1)} %copy.284) | copy-start | bytes 12582916
  29.3 22.3 %copy-start.22 = (s32[1,4,128]{2,1,0:T(4,128)S(1)}, s32[1,4,128]{2,1,0:T(4,128)}, u32[]{:S(2)}) copy-start(s32[1,4,128]{2,1,0:T(4,128)} %param.33) | copy-start | bytes 6148
  33.0 18.6 %collective-permute-start = (f32[4,128,16,8]{1,3,2,0:T(8,128)S(1)}, f32[4,128,16,8]{1,3,2,0:T(8,128)S(1)}, u32[]{:S(2)}, u32[]{:S(2)}) collective-permute-start(f32[4,128,16,8]{1,3,2,0:T(8,128)S(1)} %copy.207), channel_id=1, source_target_pairs={{0,1},{1,2},{2,3},{3,4},{4,5},{5,6},{6,7},{7,8},{8,9},{9,10},{10,1... | collective-permute-start | bytes 786440 | tf_op jit(solution)/shard_map/ppermute | solution.py:21
  38.8 17.2 %collective-permute-start.1 = (f32[4,128,16,8]{1,3,2,0:T(8,128)S(1)}, f32[4,128,16,8]{1,3,2,0:T(8,128)}, u32[]{:S(2)}, u32[]{:S(2)}) collective-permute-start(f32[4,128,16,8]{1,3,2,0:T(8,128)S(1)} %copy.208), channel_id=1, source_target_pairs={{1,0},{2,1},{3,2},{4,3},{5,4},{6,5},{7,6},{8,7},{9,8},{10,9},{11,1... | collective-permute-start | bytes 786440 | tf_op jit(solution)/shard_map/ppermute | solution.py:22
  47.7 176.7 %collective-permute-start.4 = (f32[4,80,128]{2,1,0:T(8,128)}, f32[4,80,128]{2,1,0:T(8,128)}, u32[]{:S(2)}, u32[]{:S(2)}) collective-permute-start(f32[4,80,128]{2,1,0:T(8,128)} %get-tuple-element.323), channel_id=1, source_target_pairs={{0,1},{1,2},{2,3},{3,4},{4,5},{5,6},{6,7},{8,9},{9,10},{10,11},{11... | collective-permute-start | bytes 491528 | tf_op jit(solution)/shard_map/ppermute | solution.py:21
  49.6 174.8 %collective-permute-start.5 = (f32[4,80,128]{2,1,0:T(8,128)}, f32[4,80,128]{2,1,0:T(8,128)}, u32[]{:S(2)}, u32[]{:S(2)}) collective-permute-start(f32[4,80,128]{2,1,0:T(8,128)} %get-tuple-element.324), channel_id=1, source_target_pairs={{1,0},{2,1},{3,2},{4,3},{5,4},{6,5},{7,6},{9,8},{10,9},{11,10},{12... | collective-permute-start | bytes 491528 | tf_op jit(solution)/shard_map/ppermute | solution.py:22
  56.0 14.1 %copy-start.16 = (f32[1,16,128]{2,1,0:T(8,128)S(1)}, f32[1,16,128]{2,1,0:T(8,128)}, u32[]{:S(2)}) copy-start(f32[1,16,128]{2,1,0:T(8,128)} %param.35) | copy-start | bytes 24580
  56.0 14.1 %copy-start.21 = (s32[1,32]{1,0:T(1,128)S(1)}, s32[1,32]{1,0:T(1,128)}, u32[]{:S(2)}) copy-start(s32[1,32]{1,0:T(1,128)} %param.46) | copy-start | bytes 388
  61.4 14.2 %all-to-all-start.2 = ((s32[32,8,1]{1,2,0:T(1,128)}), s32[32,8,1]{1,2,0:T(1,128)S(1)}, u32[]{:S(2)}, u32[]{:S(2)}) async-start(s32[32,8,1]{1,2,0:T(1,128)} %bitcast.113), calls=%async_computation.2 | async-start | bytes 32768 | tf_op jit(solution)/shard_map/all_to_all | solution.py:117
  75.6 280.5 %all-to-all-start.3 = ((f32[256,4,128]{2,1,0:T(4,128)}), f32[256,4,128]{2,1,0:T(4,128)S(1)}, u32[]{:S(2)}, u32[]{:S(2)}) async-start(f32[256,4,128]{2,1,0:T(4,128)} %copy.230), calls=%async_computation.3 | async-start | bytes 1048576 | tf_op jit(solution)/shard_map/all_to_all | solution.py:116
  81.4 8.9 %copy-start.12 = (f32[128,128]{1,0:T(8,128)S(1)}, f32[128,128]{1,0:T(8,128)}, u32[]{:S(2)}) copy-start(f32[128,128]{1,0:T(8,128)} %param.38) | copy-start | bytes 196612
  81.4 8.9 %copy-start.13 = (f32[4,16,16]{2,1,0:T(8,128)S(1)}, f32[4,16,16]{2,1,0:T(8,128)}, u32[]{:S(2)}) copy-start(f32[4,16,16]{2,1,0:T(8,128)} %param.37) | copy-start | bytes 12292
  81.4 8.9 %copy-start.15 = (f32[16,16]{1,0:T(8,128)S(1)}, f32[16,16]{1,0:T(8,128)}, u32[]{:S(2)}) copy-start(f32[16,16]{1,0:T(8,128)} %param.36) | copy-start | bytes 3076
  81.4 8.9 %copy-start.17 = (f32[1,16,128]{2,1,0:T(8,128)S(1)}, f32[1,16,128]{2,1,0:T(8,128)}, u32[]{:S(2)}) copy-start(f32[1,16,128]{2,1,0:T(8,128)} %param.34) | copy-start | bytes 24580
  179.8 8.0 %copy-start.3 = (f32[4,128,16,128]{3,2,0,1:T(8,128)S(1)}, f32[4,128,16,128]{3,2,0,1:T(8,128)}, u32[]{:S(2)}) copy-start(f32[4,128,16,128]{3,2,0,1:T(8,128)} %get-tuple-element.249) | copy-start | bytes 12582916 | tf_op jit(solution)/shard_map/cond
  179.8 15.2 %copy-start.7 = (f32[4,128,128,16]{2,3,1,0:T(8,128)S(1)}, f32[4,128,128,16]{2,3,1,0:T(8,128)}, u32[]{:S(2)}) copy-start(f32[4,128,128,16]{2,3,1,0:T(8,128)} %fusion.10) | copy-start | bytes 12582916 | tf_op jit(solution)/shard_map/cond
  187.8 7.1 %copy-start.5 = (f32[4,128,128,16]{2,3,1,0:T(8,128)S(1)}, f32[4,128,128,16]{2,3,1,0:T(8,128)}, u32[]{:S(2)}) copy-start(f32[4,128,128,16]{2,3,1,0:T(8,128)} %fusion.14) | copy-start | bytes 12582916 | tf_op jit(solution)/shard_map/cond
  187.8 7.1 %copy-start.6 = (f32[4,128,128,16]{2,3,1,0:T(8,128)S(1)}, f32[4,128,128,16]{2,3,1,0:T(8,128)}, u32[]{:S(2)}) copy-start(f32[4,128,128,16]{2,3,1,0:T(8,128)} %fusion.16) | copy-start | bytes 12582916 | tf_op jit(solution)/shard_map/cond
  208.0 16.4 %copy-start.11 = (f32[1,4,80,1024]{3,2,1,0:T(8,128)S(1)}, f32[1,4,80,1024]{3,2,1,0:T(8,128)}, u32[]{:S(2)}) copy-start(f32[1,4,80,1024]{3,2,1,0:T(8,128)} %param.39) | copy-start | bytes 3932164
  213.9 14.4 %copy-start.4 = (f32[4,128,16,128]{1,2,0,3:T(8,128)S(1)}, f32[4,128,16,128]{1,2,0,3:T(8,128)}, u32[]{:S(2)}) copy-start(f32[4,128,16,128]{1,2,0,3:T(8,128)} %copy.224) | copy-start | bytes 12582916
  215.1 11.6 %collective-permute-start.2 = (f32[4,128,16,8]{1,2,0,3:T(8,128)S(1)}, f32[4,128,16,8]{1,2,0,3:T(8,128)S(1)}, u32[]{:S(2)}, u32[]{:S(2)}) collective-permute-start(f32[4,128,16,8]{1,2,0,3:T(8,128)S(1)} %get-tuple-element.319), channel_id=1, source_target_pairs={{0,1},{1,2},{2,3},{3,4},{4,5},{5,6},{6,7},{7,8},{8,9},{9,10},{10,1... | collective-permute-start | bytes 786440 | tf_op jit(solution)/shard_map/ppermute | solution.py:21
  217.3 11.0 %collective-permute-start.3 = (f32[4,128,16,8]{1,2,0,3:T(8,128)S(1)}, f32[4,128,16,8]{1,2,0,3:T(8,128)S(1)}, u32[]{:S(2)}, u32[]{:S(2)}) collective-permute-start(f32[4,128,16,8]{1,2,0,3:T(8,128)S(1)} %get-tuple-element.320), channel_id=1, source_target_pairs={{1,0},{2,1},{3,2},{4,3},{5,4},{6,5},{7,6},{8,7},{9,8},{10,9},{11,1... | collective-permute-start | bytes 786440 | tf_op jit(solution)/shard_map/ppermute | solution.py:22
  230.8 125.2 %copy-start.14 = (f32[80,80]{1,0:T(8,128)S(1)}, f32[80,80]{1,0:T(8,128)}, u32[]{:S(2)}) copy-start(f32[80,80]{1,0:T(8,128)} %param.42) | copy-start | bytes 76804
  230.8 125.2 %copy-start.18 = (f32[1,6,1024]{2,0,1:T(1,128)S(1)}, f32[1,6,1024]{2,0,1:T(1,128)}, u32[]{:S(2)}) copy-start(f32[1,6,1024]{2,0,1:T(1,128)} %param.41) | copy-start | bytes 73732
  230.8 125.2 %copy-start.19 = (s32[1,6,1024]{2,0,1:T(1,128)S(1)}, s32[1,6,1024]{2,0,1:T(1,128)}, u32[]{:S(2)}) copy-start(s32[1,6,1024]{2,0,1:T(1,128)} %param.40) | copy-start | bytes 73732
  230.8 125.2 %copy-start.20 = (s32[1,1024]{1,0:T(1,128)S(1)}, s32[1,1024]{1,0:T(1,128)}, u32[]{:S(2)}) copy-start(s32[1,1024]{1,0:T(1,128)} %param.43) | copy-start | bytes 12292
  322.0 17.3 %copy-start.10 = (f32[4,128,128,16]{2,3,1,0:T(8,128)S(1)}, f32[4,128,128,16]{2,3,1,0:T(8,128)}, u32[]{:S(2)}) copy-start(f32[4,128,128,16]{2,3,1,0:T(8,128)} %fusion.31) | copy-start | bytes 12582916 | tf_op jit(solution)/shard_map/cond
  331.3 8.0 %copy-start.8 = (f32[4,128,128,16]{2,3,1,0:T(8,128)S(1)}, f32[4,128,128,16]{2,3,1,0:T(8,128)}, u32[]{:S(2)}) copy-start(f32[4,128,128,16]{2,3,1,0:T(8,128)} %fusion.33) | copy-start | bytes 12582916 | tf_op jit(solution)/shard_map/cond
  331.3 8.0 %copy-start.9 = (f32[4,128,128,16]{2,3,1,0:T(8,128)S(1)}, f32[4,128,128,16]{2,3,1,0:T(8,128)}, u32[]{:S(2)}) copy-start(f32[4,128,128,16]{2,3,1,0:T(8,128)} %fusion.35) | copy-start | bytes 12582916 | tf_op jit(solution)/shard_map/cond
  357.3 1.6 copy-start.1
where the time goes:
time: 363 us; the launch traced here: 359 us
  local copies, waits for them, and re-layouts  152 us (42%)
  matrix products  113 us (31%)
  other arithmetic  43.1 us (12%)
  starting transfers between devices  42.4 us (12%)
  waiting for transfers between devices  6.54 us (2%)
    dot_general x8, matrix products, dynamics(): jnp.einsum('pq,flqe->flpe', coupling[side], beside, precision=highest)  69.2 us
    select_n x8, local copies, waits for them, and re-layouts, dynamics(): beside = jnp.take(extended, index[side], axis=3)  58.4 us
    gather x8, local copies, waits for them, and re-layouts, dynamics(): beside = jnp.take(extended, index[side], axis=3)  41.1 us
    select_n x4, other arithmetic, dynamics(): beside = jnp.take(extended, index[side], axis=3)  24 us
    dot_general x2, matrix products, dynamics(): tend = jnp.einsum('pq,flqe->flpe', stiffness, current, precision=highest)  19.3 us
    dot_general x2, matrix products, dynamics(): jnp.einsum('lm,fmpe->flpe', atm_vertical, current, precision=highest)  16.4 us
    ppermute x3, starting transfers between devices, extended_2(): after = lax.ppermute(initial, axis, down)  15.5 us
    concatenate x3, other arithmetic, extended_2(): shard = jnp.concatenate([before, shard, after], axis=dim)  13.7 us
  transfers between devices with their start and end apart: 10, of which 2 were waited for; matrix products, arithmetic and copies ran while one was open for 83% of the time, Pallas kernels for 0%

commit v1 on v0

v1 whole, which is shorter than its diff:
```python
import functools

import jax
import jax.numpy as jnp
from jax import lax
from jax.experimental import pallas as pl
from jax.experimental.pallas import tpu as pltpu
from jax.sharding import PartitionSpec as P

RIM = 8
BLK = 128
HALO_O = 128
LANES = 128
GROUP = 8

F32 = jnp.float32
BF16 = jnp.bfloat16
VMEM_LIMIT = 56 * 1024 * 1024
ANY = pl.BlockSpec(memory_space=pl.ANY)
SMEM = pl.BlockSpec(memory_space=pltpu.SMEM)
VMEM = pl.BlockSpec(memory_space=pltpu.VMEM)


def params():
    return pltpu.CompilerParams(vmem_limit_bytes=VMEM_LIMIT)


def cost(flops, moved):
    return pl.CostEstimate(flops=flops, bytes_accessed=moved, transcendentals=0)


def split(x):
    hi = x.astype(BF16)
    return hi, (x - hi.astype(F32)).astype(BF16)


def dot(a, b):
    return jnp.dot(a, b, preferred_element_type=F32)


def dot_t(a, b):
    return lax.dot_general(a, b, (((1,), (1,)), ((), ())), preferred_element_type=F32)


def turned(rows):
    n = rows.shape[0]
    if n < LANES:
        rows = jnp.concatenate([rows, jnp.zeros((LANES - n, LANES), rows.dtype)], axis=0)
    return rows.T


def turn_kernel(flag, x, o, xt, up, down, xv, tv, in_sem, out_sem, halo_sem):
    fields, points = xv.shape[0], 16
    rows = tv.shape[1]
    olev, cells = o.shape[1], o.shape[2]

    @pl.when(flag[0] == 0)
    def _():
        loads = [pltpu.make_async_copy(x.at[f], xv.at[f], in_sem.at[f]) for f in range(fields)]
        for load in loads:
            load.start()
        for f in range(fields):
            loads[f].wait()
            for q in range(points):
                t = xv[f, pl.ds(q, LANES, stride=points), :].T
                for g in range(LANES // GROUP):
                    tv[f, pl.ds(g * GROUP * points + q * GROUP, GROUP), :] = t[g * GROUP : (g + 1) * GROUP]
            pltpu.make_async_copy(tv.at[f, pl.ds(rows - LANES, LANES)], up.at[f], halo_sem.at[0, f]).start()
            pltpu.make_async_copy(tv.at[f, pl.ds(0, LANES)], down.at[f], halo_sem.at[1, f]).start()
            pltpu.make_async_copy(tv.at[f], xt.at[f], out_sem.at[f]).start()
        for f in range(fields):
            pltpu.make_async_copy(tv.at[f, pl.ds(rows - LANES, LANES)], up.at[f], halo_sem.at[0, f]).wait()
            pltpu.make_async_copy(tv.at[f, pl.ds(0, LANES)], down.at[f], halo_sem.at[1, f]).wait()
            pltpu.make_async_copy(tv.at[f], xt.at[f], out_sem.at[f]).wait()

    @pl.when(flag[0] != 0)
    def _():
        copies = []
        for f in range(fields):
            copies.append(
                pltpu.make_async_copy(
                    o.at[f, :, pl.ds(cells - HALO_O, HALO_O)], up.at[f, pl.ds(0, olev)], halo_sem.at[0, f]
                )
            )
            copies.append(
                pltpu.make_async_copy(o.at[f, :, pl.ds(0, HALO_O)], down.at[f, pl.ds(0, olev)], halo_sem.at[1, f])
            )
        for copy in copies:
            copy.start()
        for copy in copies:
            copy.wait()


def turn(flag, state, ocean):
    fields, levels, points, elems = state.shape
    rows = points * elems
    return pl.pallas_call(
        turn_kernel,
        out_shape=(
            jax.ShapeDtypeStruct((fields, rows, levels), F32),
            jax.ShapeDtypeStruct((fields, LANES, LANES), F32),
            jax.ShapeDtypeStruct((fields, LANES, LANES), F32),
        ),
        in_specs=[SMEM, ANY, ANY],
        out_specs=(ANY, ANY, ANY),
        scratch_shapes=[
            pltpu.VMEM((fields, levels * points, elems), F32),
            pltpu.VMEM((fields, rows, levels), F32),
            pltpu.SemaphoreType.DMA((fields,)),
            pltpu.SemaphoreType.DMA((fields,)),
            pltpu.SemaphoreType.DMA((2, fields)),
        ],
        compiler_params=params(),
        cost_estimate=cost(0, 9 << 20),
        name="turn_state",
    )(flag, state.reshape(fields, levels * points, elems), ocean)


def table_kernel(flag, base, nbr, ops, hi, lo, nt, cx):
    block = pl.program_id(0)
    points = ops.shape[1]
    sides = nbr.shape[0]

    @pl.when(flag[0] == 0)
    def _():
        @pl.when(block == 0)
        def _():
            nt[...] = turned((nbr[...] - base[0]).astype(F32))
            spread = lax.broadcasted_iota(jnp.int32, (points, LANES), 1) // GROUP
            spread = (spread == lax.broadcasted_iota(jnp.int32, (points, LANES), 0)).astype(F32)
            cx[...] = lax.dot_general(
                ops[...],
                spread,
                (((1,), (0,)), ((), ())),
                precision=lax.Precision.HIGHEST,
                preferred_element_type=F32,
            )

        lane = lax.broadcasted_iota(jnp.int32, (GROUP, LANES), 1) % GROUP
        lane_f = lane.astype(F32)
        same = lane == lax.broadcasted_iota(jnp.int32, (GROUP, LANES), 0)
        for g in range(2):
            first = pl.multiple_of(block * 2 * GROUP + g * GROUP, GROUP)
            own = nt[pl.ds(first, GROUP), :]
            for h in range(4):
                cols = pl.ds(h * LANES, LANES)
                if h - g not in (0, 1, 2):
                    zero = jnp.zeros((LANES, LANES), BF16)
                    hi[0, pl.ds(g * LANES, LANES), cols] = zero
                    lo[0, pl.ds(g * LANES, LANES), cols] = zero
                    continue
                start = (block * 2 * GROUP + (h - 1) * GROUP).astype(F32)
                masks = [
                    jnp.broadcast_to(own[:, s : s + 1], (GROUP, LANES)) - start == lane_f for s in range(sides)
                ]
                for p in range(0, points, 2):
                    pair = []
                    for pp in (p, p + 1):
                        total = jnp.zeros((GROUP, LANES), F32)
                        for s in range(sides):
                            row = jnp.broadcast_to(cx[pl.ds(s * points + pp, 1), :], (GROUP, LANES))
                            total = total + jnp.where(masks[s], row, 0.0)
                        if h == g + 1:
                            row = jnp.broadcast_to(cx[pl.ds(sides * points + pp, 1), :], (GROUP, LANES))
                            total = total + jnp.where(same, row, 0.0)
                        pair.append(total)
                    top, rest = split(jnp.concatenate(pair, axis=0))
                    at = pl.ds(g * LANES + p * GROUP, 2 * GROUP)
                    hi[0, at, cols] = top
                    lo[0, at, cols] = rest


def tables(flag, base, nbr, ops, points):
    blocks = nbr.shape[1] // (2 * GROUP)
    shape = jax.ShapeDtypeStruct((blocks, 2 * LANES, 4 * LANES), BF16)
    out = pl.BlockSpec((1, 2 * LANES, 4 * LANES), lambda b: (b, 0, 0))
    return pl.pallas_call(
        table_kernel,
        grid=(blocks,),
        out_shape=(shape, shape),
        in_specs=[SMEM, SMEM, VMEM, VMEM],
        out_specs=(out, out),
        scratch_shapes=[pltpu.VMEM((LANES, LANES), F32), pltpu.VMEM((ops.shape[0], LANES), F32)],
        compiler_params=params(),
        cost_estimate=cost(0, 4 << 20),
        name="neighbour_tables",
    )(flag, base, nbr, ops)


def put_split(xhl, at, f, fields, x):
    hi, lo = split(x)
    xhl[at, pl.ds(f * LANES, LANES)] = hi
    xhl[at, pl.ds((fields + f) * LANES, LANES)] = lo


def advance(b, xv, xhl, thi, tlo, wa, mb, store):
    fields = xv.shape[0]
    width = fields * LANES
    first = pl.multiple_of(b * 2 * LANES, 2 * LANES)
    window = pl.ds(first, 4 * LANES)
    both = dot(thi[b], xhl[window, :])
    rest = dot(tlo[b], xhl[window, pl.ds(0, width)])
    rows = pl.ds(first, 2 * LANES)
    inner = pl.ds(pl.multiple_of(first + LANES, LANES), 2 * LANES)
    m = mb[rows, :]
    for f in range(fields):
        lo_at = slice((fields + f) * LANES, (fields + f + 1) * LANES)
        hi_at = slice(f * LANES, (f + 1) * LANES)
        pair = jnp.concatenate([xhl[inner, hi_at], xhl[inner, lo_at]], axis=1)
        v = dot(pair, wa[...])
        tend = both[:, hi_at] + both[:, lo_at] + rest[:, hi_at] + v[:, :LANES] + v[:, LANES:]
        store(f, rows, xv[f, rows, :] + m * tend)


def prepare(metric, vertical, wa, mb):
    points = metric.shape[0]
    mt = turned(metric[...])
    for g in range(LANES // GROUP):
        for q in range(points):
            mb[pl.ds((g * points + q) * GROUP, GROUP), :] = jnp.broadcast_to(
                mt[g * GROUP : (g + 1) * GROUP, q : q + 1], (GROUP, LANES)
            )
    hi, lo = split(vertical[...].T)
    wa[pl.ds(0, LANES), pl.ds(0, LANES)] = hi
    wa[pl.ds(LANES, LANES), pl.ds(0, LANES)] = hi
    wa[pl.ds(0, LANES), pl.ds(LANES, LANES)] = lo
    wa[pl.ds(LANES, LANES), pl.ds(LANES, LANES)] = jnp.zeros((LANES, LANES), BF16)


def table_copies(thi, tlo, hi_v, lo_v, sem):
    blocks = thi.shape[0]
    out = []
    for b in range(blocks):
        out.append(
            (
                pltpu.make_async_copy(thi.at[b], hi_v.at[b], sem.at[0, b]),
                pltpu.make_async_copy(tlo.at[b], lo_v.at[b], sem.at[1, b]),
            )
        )
    return out


def first_kernel(
    flag, xt, left, right, thi, tlo, metric, vertical, u, edges, xv, xhl, hi_v, lo_v, wa, mb, x_sem, t_sem, u_sem, e_sem
):
    fields, rows = xv.shape[0], xv.shape[1]
    blocks = thi.shape[0]

    @pl.when(flag[0] == 0)
    def _():
        loads = [pltpu.make_async_copy(xt.at[f], xv.at[f], x_sem.at[f]) for f in range(fields)]
        for load in loads:
            load.start()
        table = table_copies(thi, tlo, hi_v, lo_v, t_sem)
        for a, b in table:
            a.start()
            b.start()
        prepare(metric, vertical, wa, mb)
        for f in range(fields):
            put_split(xhl, pl.ds(0, LANES), f, fields, left[f])
            put_split(xhl, pl.ds(rows + LANES, LANES), f, fields, right[f])
        for f in range(fields):
            loads[f].wait()
            for c in range(rows // LANES):
                put_split(xhl, pl.ds((c + 1) * LANES, LANES), f, fields, xv[f, pl.ds(c * LANES, LANES), :])
        for a, b in table:
            a.wait()
            b.wait()

        def store(f, at, value):
            xv[f, at, :] = value

        @pl.loop(0, blocks)
        def _(b):
            advance(b, xv, xhl, hi_v, lo_v, wa, mb, store)

        copies = []
        for f in range(fields):
            copies.append(pltpu.make_async_copy(xv.at[f], u.at[f], u_sem.at[f]))
            copies.append(pltpu.make_async_copy(xv.at[f, pl.ds(0, LANES)], edges.at[0, f], e_sem.at[0, f]))
            copies.append(pltpu.make_async_copy(xv.at[f, pl.ds(rows - LANES, LANES)], edges.at[1, f], e_sem.at[1, f]))
        for copy in copies:
            copy.start()
        for copy in copies:
            copy.wait()


def first_step(flag, xt, left, right, thi, tlo, metric, vertical):
    fields, rows, levels = xt.shape
    blocks = thi.shape[0]
    return pl.pallas_call(
        first_kernel,
        out_shape=(
            jax.ShapeDtypeStruct((fields, rows, levels), F32),
            jax.ShapeDtypeStruct((2, fields, LANES, LANES), F32),
        ),
        in_specs=[SMEM, ANY, VMEM, VMEM, ANY, ANY, VMEM, VMEM],
        out_specs=(ANY, ANY),
        scratch_shapes=[
            pltpu.VMEM((fields, rows, levels), F32),
            pltpu.VMEM((rows + 2 * LANES, 2 * fields * LANES), BF16),
            pltpu.VMEM(thi.shape, BF16),
            pltpu.VMEM(thi.shape, BF16),
            pltpu.VMEM((2 * LANES, 2 * LANES), BF16),
            pltpu.VMEM((rows, LANES), F32),
            pltpu.SemaphoreType.DMA((fields,)),
            pltpu.SemaphoreType.DMA((2, blocks)),
            pltpu.SemaphoreType.DMA((fields,)),
            pltpu.SemaphoreType.DMA((2, fields)),
        ],
        compiler_params=params(),
        cost_estimate=cost(10_000_000_000, 12 << 20),
        name="first_step",
    )(flag, xt, left, right, thi, tlo, metric, vertical)


def flux_kernel(
    flag, owner, block, source, tops, weights, coef, surface_level, edges, flux, sent, down, up, wv, wcat, surf, fl, w_sem
):
    pairs = weights.shape[0]
    points = coef.shape[0]
    fields = surface_level.shape[0]
    ocean_blocks = sent.shape[0] // tops.shape[0]

    @pl.when(flag[0] == 0)
    def _():
        parts = w_sem.shape[0]
        each = pairs // parts
        loads = [
            pltpu.make_async_copy(weights.at[pl.ds(i * each, each)], wv.at[pl.ds(i * each, each)], w_sem.at[i])
            for i in range(parts)
        ]
        for load in loads:
            load.start()
        surf[...] = jnp.zeros_like(surf)
        sent[...] = jnp.zeros_like(sent)

        def doubled(rows):
            hi, lo = split(rows)
            hi, lo = hi.astype(F32), lo.astype(F32)
            eight = jnp.concatenate([hi, lo], axis=0).astype(BF16)
            return jnp.concatenate([eight, eight], axis=1)

        for i in range(parts):
            loads[i].wait()

            @pl.loop(i * each, (i + 1) * each)
            def _(r):
                hi, lo = split(wv[r])
                wcat[r, :, pl.ds(0, BLK)] = hi
                wcat[r, :, pl.ds(BLK, BLK)] = lo

        for r in range(pairs):
            at = pl.multiple_of(block[r] * BLK, BLK)
            rows = doubled(tops[owner[r], :, pl.ds(at, BLK)])
            out = dot_t(rows, wcat[r])
            surf[source[r]] += out[:fields] + out[fields:]

        for p in range(points):
            value = coef[pl.ds(p, 1), :] * (surface_level[:, p, :] - surf[p])
            fl[p] = value
            flux[:, p, :] = value

        for r in range(pairs):
            rows = doubled(fl[source[r]])
            both = jnp.concatenate([wcat[r, :, pl.ds(0, BLK)], wcat[r, :, pl.ds(BLK, BLK)]], axis=0)
            out = dot(rows, both)
            sent[owner[r] * ocean_blocks + block[r]] += out[:fields] + out[fields:]

        lane = lax.broadcasted_iota(jnp.int32, (GROUP, LANES), 1)
        for f in range(fields):
            ft = turned(flux[f])
            for side, out_ref, g in ((0, down, 0), (1, up, LANES // GROUP - 1)):
                for q in range(points):
                    at = pl.ds(q * GROUP, GROUP)
                    column = jnp.broadcast_to(ft[g * GROUP : (g + 1) * GROUP, q : q + 1], (GROUP, LANES))
                    out_ref[f, at, :] = edges[side, f, at, :] - jnp.where(lane == LANES - 1, 0.5 * column, 0.0)


def fluxes(flag, owner, block, source, tops, weights, coef, surface_level, edges, ocean_blocks):
    fields, points, elems = surface_level.shape
    pairs = weights.shape[0]
    owners = tops.shape[0]
    halo = jax.ShapeDtypeStruct((fields, LANES, LANES), F32)
    return pl.pallas_call(
        flux_kernel,
        out_shape=(
            jax.ShapeDtypeStruct((fields, points, elems), F32),
            jax.ShapeDtypeStruct((owners * ocean_blocks, fields, BLK), F32),
            halo,
            halo,
        ),
        in_specs=[SMEM, SMEM, SMEM, SMEM, VMEM, ANY, VMEM, VMEM, VMEM],
        out_specs=(VMEM, VMEM, VMEM, VMEM),
        scratch_shapes=[
            pltpu.VMEM(weights.shape, F32),
            pltpu.VMEM((pairs, BLK, 2 * BLK), BF16),
            pltpu.VMEM((points, fields, BLK), F32),
            pltpu.VMEM((points, fields, BLK), F32),
            pltpu.SemaphoreType.DMA((4,)),
        ],
        compiler_params=params(),
        cost_estimate=cost(1_000_000_000, 4 << 20),
        name="fluxes",
    )(flag, owner, block, source, tops, weights, coef, surface_level, edges)


def second_kernel(
    flag, u, left, right, thi, tlo, metric, vertical, flux, out, xv, xhl, hi_v, lo_v, wa, mb, ov, x_sem, t_sem, o_sem
):
    fields, rows = xv.shape[0], xv.shape[1]
    blocks = thi.shape[0]
    points = metric.shape[0]
    levels = xv.shape[2]

    @pl.when(flag[0] == 0)
    def _():
        loads = [pltpu.make_async_copy(u.at[f], xv.at[f], x_sem.at[f]) for f in range(fields)]
        for load in loads:
            load.start()
        table = table_copies(thi, tlo, hi_v, lo_v, t_sem)
        for a, b in table:
            a.start()
            b.start()
        prepare(metric, vertical, wa, mb)
        for f in range(fields):
            put_split(xhl, pl.ds(0, LANES), f, fields, left[f])
            put_split(xhl, pl.ds(rows + LANES, LANES), f, fields, right[f])
        lane = lax.broadcasted_iota(jnp.int32, (GROUP, LANES), 1)
        for f in range(fields):
            ft = turned(-0.5 * flux[f])
            loads[f].wait()
            for g in range(LANES // GROUP):
                pieces = []
                for q in range(points):
                    column = jnp.broadcast_to(ft[g * GROUP : (g + 1) * GROUP, q : q + 1], (GROUP, LANES))
                    pieces.append(jnp.where(lane == LANES - 1, column, 0.0))
                at = pl.ds(g * LANES, LANES)
                x = xv[f, at, :] + jnp.concatenate(pieces, axis=0)
                xv[f, at, :] = x
                put_split(xhl, pl.ds((g + 1) * LANES, LANES), f, fields, x)
        for a, b in table:
            a.wait()
            b.wait()

        def store(f, at, value):
            xv[f, at, :] = value

        @pl.loop(0, blocks)
        def _(b):
            advance(b, xv, xhl, hi_v, lo_v, wa, mb, store)

        copies = [pltpu.make_async_copy(ov.at[f], out.at[f], o_sem.at[f]) for f in range(fields)]
        for f in range(fields):
            for p in range(points):
                cols = [xv[f, pl.ds(g * LANES + p * GROUP, GROUP), :] for g in range(LANES // GROUP)]
                ov[f, pl.ds(p, LANES, stride=points), :] = jnp.concatenate(cols, axis=0).T
            last = pl.ds((levels - 1) * points, points)
            ov[f, last, :] = ov[f, last, :] - 0.5 * flux[f]
            copies[f].start()
        for copy in copies:
            copy.wait()

    @pl.when(flag[0] != 0)
    def _():
        ov[0] = jnp.zeros_like(ov[0])
        copies = [pltpu.make_async_copy(ov.at[0], out.at[f], o_sem.at[f]) for f in range(fields)]
        for copy in copies:
            copy.start()
        for copy in copies:
            copy.wait()


def second_step(flag, u, left, right, thi, tlo, metric, vertical, flux):
    fields, rows, levels = u.shape
    blocks = thi.shape[0]
    points = metric.shape[0]
    return pl.pallas_call(
        second_kernel,
        out_shape=jax.ShapeDtypeStruct((fields, levels * points, LANES), F32),
        in_specs=[SMEM, ANY, VMEM, VMEM, ANY, ANY, VMEM, VMEM, VMEM],
        out_specs=ANY,
        scratch_shapes=[
            pltpu.VMEM((fields, rows, levels), F32),
            pltpu.VMEM((rows + 2 * LANES, 2 * fields * LANES), BF16),
            pltpu.VMEM(thi.shape, BF16),
            pltpu.VMEM(thi.shape, BF16),
            pltpu.VMEM((2 * LANES, 2 * LANES), BF16),
            pltpu.VMEM((rows, LANES), F32),
            pltpu.VMEM((fields, levels * points, LANES), F32),
            pltpu.SemaphoreType.DMA((fields,)),
            pltpu.SemaphoreType.DMA((2, blocks)),
            pltpu.SemaphoreType.DMA((fields,)),
        ],
        compiler_params=params(),
        cost_estimate=cost(10_000_000_000, 12 << 20),
        name="second_step",
    )(flag, u, left, right, thi, tlo, metric, vertical, flux)


def ocean_kernel(flag, base, o, left, right, nbr, diff, vertical, mask, out, ov, ext, dhi, dlo, res, o_sem, out_sem):
    fields, olev, cells = ov.shape
    sides = nbr.shape[0]
    blocks = cells // LANES

    @pl.when(flag[0] != 0)
    def _():
        load = pltpu.make_async_copy(o, ov, o_sem)
        load.start()
        load.wait()
        for f in range(fields):
            rows = pl.ds(f * olev, olev)
            for at, value in ((0, left[f, :olev, :]), (HALO_O + cells, right[f, :olev, :])):
                hi, lo = split(value)
                ext[0, rows, pl.ds(at, HALO_O)] = hi
                ext[1, rows, pl.ds(at, HALO_O)] = lo
            hi, lo = split(ov[f])
            ext[0, rows, pl.ds(HALO_O, cells)] = hi
            ext[1, rows, pl.ds(HALO_O, cells)] = lo
        vhi, vlo = split(vertical[...])

        @pl.loop(0, blocks)
        def _(b):
            first = pl.multiple_of(b * LANES, LANES)
            here = pl.ds(first, LANES)
            start = base[0] + first - HALO_O
            place = lax.broadcasted_iota(jnp.int32, (3 * LANES, LANES), 0)
            table = jnp.zeros((3 * LANES, LANES), F32)
            held = jnp.zeros((1, LANES), F32)
            for k in range(sides):
                d = diff[pl.ds(k, 1), here]
                held = held + d
                table = table + jnp.where(place == nbr[pl.ds(k, 1), here] - start, d, 0.0)
            hi, lo = split(table)
            window = pl.ds(first, 3 * LANES)
            lap = dot(ext[0, :, window], hi) + dot(ext[1, :, window], hi) + dot(ext[0, :, window], lo)
            inner = pl.ds(pl.multiple_of(first + HALO_O, LANES), LANES)
            sea = mask[:, here] == 1
            for f in range(fields):
                rows = pl.ds(f * olev, olev)
                xhi, xlo = ext[0, rows, inner], ext[1, rows, inner]
                v = dot(vhi, xhi) + dot(vhi, xlo) + dot(vlo, xhi)
                own = ov[f, :, here]
                fresh = own + (lap[f * olev : (f + 1) * olev] - held * own) + v
                res[f, :, here] = jnp.where(sea, fresh, own)

    @pl.when(flag[0] == 0)
    def _():
        res[...] = jnp.zeros_like(res)

    copy = pltpu.make_async_copy(res, out, out_sem)
    copy.start()
    copy.wait()


def ocean_step(flag, base, ocean, left, right, nbr, diff, vertical, mask):
    fields, olev, cells = ocean.shape
    return pl.pallas_call(
        ocean_kernel,
        out_shape=jax.ShapeDtypeStruct(ocean.shape, F32),
        in_specs=[SMEM, SMEM, ANY, VMEM, VMEM, VMEM, VMEM, VMEM, VMEM],
        out_specs=ANY,
        scratch_shapes=[
            pltpu.VMEM(ocean.shape, F32),
            pltpu.VMEM((2, fields * olev, cells + 2 * HALO_O), BF16),
            pltpu.VMEM((8, LANES), BF16),
            pltpu.VMEM((8, LANES), BF16),
            pltpu.VMEM(ocean.shape, F32),
            pltpu.SemaphoreType.DMA,
            pltpu.SemaphoreType.DMA,
        ],
        compiler_params=params(),
        cost_estimate=cost(2_000_000_000, 3 << 20),
        name="ocean_step",
    )(flag, base, ocean, left, right, nbr, diff, vertical, mask)


def finish_kernel(flag, fresh, arrived, mask, out, rows_v, in_sem, out_sem):
    del fresh
    fields, cells = rows_v.shape[0], rows_v.shape[2]
    parts = arrived.shape[0]

    @pl.when(flag[0] != 0)
    def _():
        loads = [
            pltpu.make_async_copy(out.at[f, pl.ds(0, 8)], rows_v.at[f], in_sem.at[f]) for f in range(fields)
        ]
        stores = [
            pltpu.make_async_copy(rows_v.at[f], out.at[f, pl.ds(0, 8)], out_sem.at[f]) for f in range(fields)
        ]
        for load in loads:
            load.start()
        for load in loads:
            load.wait()
        for b in range(cells // BLK):
            here = pl.ds(b * BLK, BLK)
            total = arrived[0, b]
            for i in range(1, parts):
                total = total + arrived[i, b]
            total = jnp.where(mask[:, here] == 1, 0.5 * total, 0.0)
            for f in range(fields):
                rows_v[f, pl.ds(0, 1), here] = rows_v[f, pl.ds(0, 1), here] + total[f : f + 1]
        for store in stores:
            store.start()
        for store in stores:
            store.wait()


def finish(flag, fresh, arrived, mask):
    fields, olev, cells = fresh.shape
    return pl.pallas_call(
        finish_kernel,
        out_shape=jax.ShapeDtypeStruct(fresh.shape, F32),
        in_specs=[SMEM, ANY, VMEM, VMEM],
        out_specs=ANY,
        input_output_aliases={1: 0},
        scratch_shapes=[
            pltpu.VMEM((fields, 8, cells), F32),
            pltpu.SemaphoreType.DMA((fields,)),
            pltpu.SemaphoreType.DMA((fields,)),
        ],
        compiler_params=params(),
        cost_estimate=cost(0, 1 << 18),
        name="finish_ocean",
    )(flag, fresh, arrived, mask)


def local(
    atm_state,
    elem_nbr,
    elem_metric,
    bulk_coef,
    stiffness,
    coupling,
    atm_vertical,
    ocean_state,
    cell_nbr,
    cell_diff,
    ocean_vertical,
    sea_mask,
    pair_owner,
    pair_block,
    pair_src,
    remap_weight,
):
    n_comp = lax.axis_size("comp")
    n_dom = lax.axis_size("dom")
    comp_index = lax.axis_index("comp")
    dom_index = lax.axis_index("dom")
    live = n_comp - 1
    state = atm_state[0]
    ocean = ocean_state[0]
    fields, levels, points, elems = state.shape
    cells = ocean.shape[2]
    ocean_blocks = cells // BLK
    flag = (comp_index == live).astype(jnp.int32).reshape(1)
    joined = (comp_index * n_dom + dom_index) * elems
    elem_base = joined.astype(jnp.int32).reshape(1)
    cell_base = (dom_index * cells).astype(jnp.int32).reshape(1)

    both = ("comp", "dom")
    atm_up = [(i, i + 1) for i in range(live * n_dom - 1)]
    sea_up = [(live * n_dom + i, live * n_dom + i + 1) for i in range(n_dom - 1)]
    going_up = atm_up + sea_up
    going_down = [(j, i) for i, j in going_up]

    def from_ocean(c):
        return [(live * n_dom + d, c * n_dom + d) for d in range(n_dom)]

    def to_ocean(c):
        return [(c * n_dom + d, live * n_dom + d) for d in range(n_dom)]

    top = ocean[:, 0, :]
    got = sum(lax.ppermute(top, both, from_ocean(c)) for c in range(live))
    tops = lax.all_to_all(
        jnp.broadcast_to(got[None], (n_dom,) + got.shape), "dom", split_axis=0, concat_axis=0, tiled=True
    )

    xt, send_up, send_down = turn(flag, state, ocean)
    left = lax.ppermute(send_up, both, going_up)
    right = lax.ppermute(send_down, both, going_down)

    ops = jnp.concatenate([coupling.reshape(-1, points), stiffness], axis=0)
    thi, tlo = tables(flag, elem_base, elem_nbr[0], ops, points)
    u, edges = first_step(flag, xt, left, right, thi, tlo, elem_metric[0], atm_vertical)
    flux, sent, edge_down, edge_up = fluxes(
        flag,
        pair_owner[0, :, 0],
        pair_block[0],
        pair_src[0],
        tops,
        remap_weight[0],
        bulk_coef[0],
        state[:, levels - 1],
        edges,
        ocean_blocks,
    )
    left2 = lax.ppermute(edge_up, both, atm_up)
    right2 = lax.ppermute(edge_down, both, [(j, i) for i, j in atm_up])

    ocean_new = ocean_step(
        flag, cell_base, ocean, left, right, cell_nbr[0], cell_diff[0], ocean_vertical, sea_mask
    )

    by_owner = lax.all_to_all(
        sent.reshape(n_dom, ocean_blocks, fields, BLK), "dom", split_axis=0, concat_axis=0, tiled=True
    )
    mine = jnp.sum(by_owner, axis=0)
    arrived = jnp.stack([lax.ppermute(mine, both, to_ocean(c)) for c in range(live)])

    atm_next = second_step(flag, u, left2, right2, thi, tlo, elem_metric[0], atm_vertical, flux)
    ocean_next = finish(flag, ocean_new, arrived, sea_mask)
    return (atm_next.reshape(state.shape)[None], ocean_next[None])


def solution(mesh):
    in_specs = (
        P("comp", None, None, None, "dom"),
        P("comp", None, "dom"),
        P("comp", None, "dom"),
        P("comp", None, "dom"),
        P(),
        P(),
        P(),
        P("comp", None, None, "dom"),
        P("comp", None, "dom"),
        P("comp", None, "dom"),
        P(),
        P("comp", "dom"),
        P("comp", "dom", None),
        P("comp", "dom"),
        P("comp", "dom"),
        P("comp", "dom", None, None),
    )
    out_specs = (P("comp", None, None, None, "dom"), P("comp", None, None, "dom"))
    return jax.shard_map(local, mesh=mesh, in_specs=in_specs, out_specs=out_specs, check_vma=False)
```

time: 363 us -> 85.8 us (0.24)
  local copies, waits for them, and re-layouts: 152 us -> 6.38 us
  matrix products: 113 us -> 0 us
  Pallas kernels: 0 us -> 44.4 us
  other arithmetic: 43.1 us -> 1.29 us
  starting transfers between devices: 42.4 us -> 31.9 us
  waiting for transfers between devices: 6.54 us -> 0.03 us
    dot_general x18 -> x0, matrix products: 113 us -> none  [the longest x8 69.2 us: dynamics(): jnp.einsum('pq,flqe->flpe', coupling[side], beside, precision=highest)]
    select_n x8 -> x0, local copies, waits for them, and re-layouts: 58.4 us -> none  [dynamics(): beside = jnp.take(extended, index[side], axis=3)]
    pallas_call x0 -> x7, Pallas kernels: none -> 44.4 us  [the longest x1 14 us: second_step(): pl.pallas_call(second_kernel, out_shape=jax.ShapeDtypeStruct((fields, lev...]
    gather x9 -> x0, local copies, waits for them, and re-layouts: 42.1 us -> none  [the longest x8 41.1 us: dynamics(): beside = jnp.take(extended, index[side], axis=3)]
    select_n x5 -> x0, other arithmetic: 24.9 us -> none  [the longest x4 24 us: dynamics(): beside = jnp.take(extended, index[side], axis=3)]
    slice x6 -> x1, local copies, waits for them, and re-layouts: 16.1 us -> 0.92 us  [local(): top = ocean[:, 0, :]]
    concatenate x3 -> x1, other arithmetic: 13.7 us -> 0.62 us  [local(): ops = jnp.concatenate([coupling.reshape(-1, points), stiffness], axis=0)]
    all_to_all x4 -> x2, starting transfers between devices: 20.7 us -> 8.4 us  [the longest x1 5.03 us: local(): lax.all_to_all(sent.reshape(n_dom, ocean_blocks, fields, BLK), 'dom', spl...]
  transfers between devices with their start and end apart: 10 -> 12, of which waited for: 2 -> 0; matrix products, arithmetic and copies ran while one was open for 83% -> 5% of each run, Pallas kernels for 0% -> 30%
where the time goes in v1:
time: 85.8 us; the launch traced here: 85 us
  Pallas kernels  44.4 us (52%)
  starting transfers between devices  31.9 us (37%)
  local copies, waits for them, and re-layouts  6.38 us (7%)
  other arithmetic  1.29 us (2%)
  between operations  0.96 us (1%)
    pallas_call x1, Pallas kernels, second_step(): pl.pallas_call(second_kernel, out_shape=jax.ShapeDtypeStruct((fields, lev...  14 us
    pallas_call x1, Pallas kernels, first_step(): pl.pallas_call(first_kernel, out_shape=(jax.ShapeDtypeStruct((fields, row...  12.8 us
    ppermute x1, starting transfers between devices, local(): right = lax.ppermute(send_down, both, going_down)  7.24 us
    ppermute x1, starting transfers between devices, local(): right2 = lax.ppermute(edge_down, both, [(j, i) for i, j in atm_up])  6.75 us
    pallas_call x1, Pallas kernels, tables(): pl.pallas_call(table_kernel, grid=(blocks,), out_shape=(shape, shape), in...  5.43 us
    all_to_all x1, starting transfers between devices, local(): lax.all_to_all(sent.reshape(n_dom, ocean_blocks, fields, BLK), 'dom', spl...  5.03 us
    pallas_call x1, Pallas kernels, fluxes(): pl.pallas_call(flux_kernel, out_shape=(jax.ShapeDtypeStruct((fields, poin...  4.8 us
    pallas_call x1, Pallas kernels, turn(): pl.pallas_call(turn_kernel, out_shape=(jax.ShapeDtypeStruct((fields, rows...  4.28 us
  transfers between devices with their start and end apart: 12, of which 0 were waited for; matrix products, arithmetic and copies ran while one was open for 5% of the time, Pallas kernels for 30%

profile of v1, /device:TPU:4, one launch (start us, length us, event | category | flops | bytes accessed | tf_op | source)
XLA Modules:
  0.0 85.0 jit_solution(15670271477232738334)
XLA Ops:
  0.6 0.9 %slice.8 = f32[4,1,1024]{2,1,0:T(1,128)S(1)} slice(f32[4,80,1024]{2,1,0:T(8,128)} %bitcast.35), slice={[0:4], [0:1], [0:1024]} | slice | bytes 32768 | tf_op jit(solution)/shard_map/slice | solution.py:673
  1.6 1.3 %collective-permute-start.4 = (f32[4,1024]{1,0:T(4,128)S(1)}, f32[4,1024]{1,0:T(4,128)S(1)}, u32[]{:S(2)}, u32[]{:S(2)}) collective-permute-start(f32[4,1024]{1,0:T(4,128)S(1)} %bitcast.43), channel_id=1, source_target_pairs={{24,16},{25,17},{26,18},{27,19},{28,20},{29,21},{30,22},{31,23}} | collective-permute-start | bytes 49160 | tf_op jit(solution)/shard_map/ppermute | solution.py:674
  2.9 0.7 collective-permute-start.2
  3.5 0.7 collective-permute-start.3
  4.2 0.0 copy-start
  4.2 4.3 %turn_state.1 = (f32[4,2048,128]{2,1,0:T(8,128)}, f32[4,128,128]{2,1,0:T(8,128)}, f32[4,128,128]{2,1,0:T(8,128)}) custom-call(s32[1]{0:T(128)} %bitcast.flag, f32[4,2048,128]{2,1,0:T(8,128)} %bitcast.33, f32[4,80,1024]{2,1,0:T(8,128)} %bitcast.36), custom_call_target="tpu_custom_call" | custom-call | bytes 9437184 | tf_op jit(solution)/shard_map/turn_state/pallas_call | solution.py:97
  8.5 1.9 %collective-permute-start = (f32[4,128,128]{2,1,0:T(8,128)}, f32[4,128,128]{2,1,0:T(8,128)S(1)}, u32[]{:S(2)}, u32[]{:S(2)}) collective-permute-start(f32[4,128,128]{2,1,0:T(8,128)} %get-tuple-element.14), channel_id=1, source_target_pairs={{0,1},{1,2},{2,3},{3,4},{4,5},{5,6},{6,7},{7,8},{8,9},{9,10},{10,1... | collective-permute-start | bytes 786440 | tf_op jit(solution)/shard_map/ppermute | solution.py:680
  10.4 0.0 copy-start.2
  10.5 0.0 copy-start.5
  10.5 7.2 %collective-permute-start.1 = (f32[4,128,128]{2,1,0:T(8,128)}, f32[4,128,128]{2,1,0:T(8,128)S(1)}, u32[]{:S(2)}, u32[]{:S(2)}) collective-permute-start(f32[4,128,128]{2,1,0:T(8,128)} %get-tuple-element.15), channel_id=1, source_target_pairs={{1,0},{2,1},{3,2},{4,3},{5,4},{6,5},{7,6},{8,7},{9,8},{10,9},{11,1... | collective-permute-start | bytes 786440 | tf_op jit(solution)/shard_map/ppermute | solution.py:681
  17.7 0.0 copy-done
  17.7 0.6 copy.32
  18.4 0.6 slice_bitcast_fusion.surface_level
  19.0 0.0 copy-done.2
  19.0 0.0 copy-done.5
  19.0 0.6 pad_maximum_fusion.1.ops
  19.6 5.4 %neighbour_tables.1 = (bf16[8,256,512]{2,1,0:T(8,128)(2,1)}, bf16[8,256,512]{2,1,0:T(8,128)(2,1)}) custom-call(s32[1]{0:T(128)} %bitcast.flag, s32[1]{0:T(128)} %bitcast.3.base, s32[4,128]{1,0:T(4,128)} %bitcast.49, f32[80,16]{1,0:T(8,128)} %pad_maximum_fusion.1.ops), custom_call_target="tpu_custom_call" | custom-call | bytes 4194304 | tf_op jit(solution)/shard_map/neighbour_tables/pallas_call | solution.py:177
  25.0 0.0 collective-permute-done.4
  25.0 0.0 collective-permute-done.2
  25.0 0.0 collective-permute-done.3
  25.1 0.7 broadcast_in_dim.4
  25.7 3.4 %all-to-all-start = ((f32[8,4,1024]{2,1,0:T(4,128)}), f32[8,4,1024]{2,1,0:T(4,128)S(1)}, u32[]{:S(2)}, u32[]{:S(2)}) async-start(f32[8,4,1024]{2,1,0:T(4,128)} %broadcast_in_dim.4), calls=%async_computation | async-start | bytes 262144 | tf_op jit(solution)/shard_map/all_to_all | solution.py:675
  29.1 0.0 collective-permute-done.left
  29.1 0.0 copy-start.6
  29.1 0.0 collective-permute-done.1.right
  29.1 0.0 copy-start.7
  29.2 0.7 copy-done.6
  29.8 0.1 copy-done.7
  30.0 0.0 copy-start.3
  30.0 0.0 copy-start.4
  30.0 12.8 %first_step.1 = (f32[4,2048,128]{2,1,0:T(8,128)}, f32[2,4,128,128]{3,2,1,0:T(8,128)}) custom-call(s32[1]{0:T(128)} %bitcast.flag, f32[4,2048,128]{2,1,0:T(8,128)} %get-tuple-element.13.xt, f32[4,128,128]{2,1,0:T(8,128)} %copy-done.6, f32[4,128,128]{2,1,0:T(8,128)} %copy-done.7, bf16[8,256,512]{2,1,0:T(8,128)(2,1)} %get-tuple-element.16.thi, ...), custom_call_target="tpu_custom_call" | custom-call | flops 10000000000 | bytes 12582912 | tf_op jit(solution)/shard_map/first_step/pallas_call | solution.py:291
  42.8 0.0 all-to-all-done.tops
  42.8 0.0 copy-start.1
  42.8 0.7 copy-done.1
  43.5 4.8 %fluxes.1 = (f32[4,16,128]{2,1,0:T(8,128)}, f32[64,4,128]{2,1,0:T(4,128)}, f32[4,128,128]{2,1,0:T(8,128)}, f32[4,128,128]{2,1,0:T(8,128)}) custom-call(s32[1]{0:T(128)} %bitcast.flag, s32[32]{0:T(128)} %bitcast.54, s32[32]{0:T(128)} %bitcast.55, s32[32]{0:T(128)} %bitcast.56, f32[8,4,1024]{2,1,0:T(4,128)} %copy-done.1, f32[32,128,128]{2,1,0:T(8,128)} %bitcast.50, ...), custom_call_target="tpu_custom_call" | custom-call | flops 1000000000 | bytes 4194304 | tf_op jit(solution)/shard_map/fluxes/pallas_call | solution.py:385
  48.3 5.0 %all-to-all-start.1 = ((f32[8,8,4,128]{3,2,1,0:T(4,128)}), f32[8,8,4,128]{3,2,1,0:T(4,128)S(1)}, u32[]{:S(2)}, u32[]{:S(2)}) async-start(f32[8,8,4,128]{3,2,1,0:T(4,128)} %bitcast.39), calls=%async_computation.1 | async-start | bytes 262144 | tf_op jit(solution)/shard_map/all_to_all | solution.py:705
  53.3 0.0 copy-done.3
  53.3 0.6 copy.34
  53.9 0.0 copy-done.4
  53.9 0.6 copy.33
  54.5 2.4 %collective-permute-start.5 = (f32[4,128,128]{2,1,0:T(8,128)}, f32[4,128,128]{2,1,0:T(8,128)S(1)}, u32[]{:S(2)}, u32[]{:S(2)}) collective-permute-start(f32[4,128,128]{2,1,0:T(8,128)} %get-tuple-element.20), channel_id=1, source_target_pairs={{0,1},{1,2},{2,3},{3,4},{4,5},{5,6},{6,7},{7,8},{8,9},{9,10},{10,1... | collective-permute-start | bytes 786440 | tf_op jit(solution)/shard_map/ppermute | solution.py:698
  57.0 6.7 %collective-permute-start.6 = (f32[4,128,128]{2,1,0:T(8,128)}, f32[4,128,128]{2,1,0:T(8,128)S(1)}, u32[]{:S(2)}, u32[]{:S(2)}) collective-permute-start(f32[4,128,128]{2,1,0:T(8,128)} %get-tuple-element.21), channel_id=1, source_target_pairs={{1,0},{2,1},{3,2},{4,3},{5,4},{6,5},{7,6},{8,7},{9,8},{10,9},{11,1... | collective-permute-start | bytes 786440 | tf_op jit(solution)/shard_map/ppermute | solution.py:699
  63.7 0.0 all-to-all-done.1
  63.8 1.3 %collective-permute-start.9 = (f32[8,4,128]{2,1,0:T(4,128)S(1)}, f32[8,4,128]{2,1,0:T(4,128)S(1)}, u32[]{:S(2)}, u32[]{:S(2)}) collective-permute-start(f32[8,4,128]{2,1,0:T(4,128)S(1)} %reduce_sum.9), channel_id=1, source_target_pairs={{16,24},{17,25},{18,26},{19,27},{20,28},{21,29},{22,30},{23,31}} | collective-permute-start | bytes 49160 | tf_op jit(solution)/shard_map/ppermute | solution.py:709
  65.0 0.7 collective-permute-start.8
  65.7 0.7 collective-permute-start.7
  66.4 2.2 %ocean_step.1.fresh = f32[4,80,1024]{2,1,0:T(8,128)} custom-call(s32[1]{0:T(128)} %bitcast.flag, s32[1]{0:T(128)} %bitcast.15.base, f32[4,80,1024]{2,1,0:T(8,128)} %bitcast.37, f32[4,128,128]{2,1,0:T(8,128)} %copy-done.6, f32[4,128,128]{2,1,0:T(8,128)} %copy-done.7, s32[6,1024]{1,0:T(8,128)} %bitcast.40, f32[6,1024]{1,0:T(8,128)} %bitcast.41, ...), custom_call_target="tpu_custom_call" | custom-call | flops 2000000000 | bytes 3145728 | tf_op jit(solution)/shard_map/ocean_step/pallas_call | solution.py:558
  68.6 0.0 collective-permute-done.9
  68.6 0.0 collective-permute-done.8
  68.6 0.0 collective-permute-done.7
  68.7 0.6 pad_maximum_fusion.arrived
  69.3 0.9 %finish_ocean.1 = f32[4,80,1024]{2,1,0:T(8,128)} custom-call(s32[1]{0:T(128)} %bitcast.flag, f32[4,80,1024]{2,1,0:T(8,128)} %ocean_step.1.fresh, f32[3,8,4,128]{3,2,1,0:T(4,128)} %pad_maximum_fusion.arrived, s32[1,1024]{1,0:T(1,128)} %mask.3), custom_call_target="tpu_custom_call", output_to_operand_aliasing={{}: (1, {})} | custom-call | bytes 262144 | tf_op jit(solution)/shard_map/finish_ocean/pallas_call | solution.py:611
  70.2 0.0 collective-permute-done.5.left
  70.2 0.0 copy-start.8
  70.2 0.0 collective-permute-done.6.right
  70.2 0.0 copy-start.9
  70.2 0.7 copy-done.8
  70.9 0.1 copy-done.9
  71.0 14.0 %second_step.1 = f32[4,2048,128]{2,1,0:T(8,128)} custom-call(s32[1]{0:T(128)} %bitcast.flag, f32[4,2048,128]{2,1,0:T(8,128)} %get-tuple-element.18.u, f32[4,128,128]{2,1,0:T(8,128)} %copy-done.8, f32[4,128,128]{2,1,0:T(8,128)} %copy-done.9, bf16[8,256,512]{2,1,0:T(8,128)(2,1)} %get-tuple-element.16.thi, bf16[8,256,512]{2,1,0:T(8,128)(2,1)} %get-tuple-element.17.tlo, ...), custom_call_target="tpu_custom_call" | custom-call | flops 10000000000 | bytes 12582912 | tf_op jit(solution)/shard_map/second_step/pallas_call | solution.py:478
  (3 shorter events, 0.0 us)
Async XLA Ops:
  1.6 23.5 %collective-permute-start.4 = (f32[4,1024]{1,0:T(4,128)S(1)}, f32[4,1024]{1,0:T(4,128)S(1)}, u32[]{:S(2)}, u32[]{:S(2)}) collective-permute-start(f32[4,1024]{1,0:T(4,128)S(1)} %bitcast.43), channel_id=1, source_target_pairs={{24,16},{25,17},{26,18},{27,19},{28,20},{29,21},{30,22},{31,23}} | collective-permute-start | bytes 49160 | tf_op jit(solution)/shard_map/ppermute | solution.py:674
  2.9 22.2 %collective-permute-start.2 = (f32[4,1024]{1,0:T(4,128)S(1)}, f32[4,1024]{1,0:T(4,128)S(1)}, u32[]{:S(2)}, u32[]{:S(2)}) collective-permute-start(f32[4,1024]{1,0:T(4,128)S(1)} %bitcast.44), channel_id=1, source_target_pairs={{24,0},{25,1},{26,2},{27,3},{28,4},{29,5},{30,6},{31,7}} | collective-permute-start | bytes 49160 | tf_op jit(solution)/shard_map/ppermute | solution.py:674
  3.5 21.5 %collective-permute-start.3 = (f32[4,1024]{1,0:T(4,128)S(1)}, f32[4,1024]{1,0:T(4,128)S(1)}, u32[]{:S(2)}, u32[]{:S(2)}) collective-permute-start(f32[4,1024]{1,0:T(4,128)S(1)} %bitcast.45), channel_id=1, source_target_pairs={{24,8},{25,9},{26,10},{27,11},{28,12},{29,13},{30,14},{31,15}} | collective-permute-start | bytes 49160 | tf_op jit(solution)/shard_map/ppermute | solution.py:674
  4.2 13.5 %copy-start = (f32[1,4,128,16,128]{4,3,2,1,0:T(8,128)S(1)}, f32[1,4,128,16,128]{4,3,2,1,0:T(8,128)}, u32[]{:S(2)}) copy-start(f32[1,4,128,16,128]{4,3,2,1,0:T(8,128)} %param.16) | copy-start | bytes 12582916
  8.5 20.6 %collective-permute-start = (f32[4,128,128]{2,1,0:T(8,128)}, f32[4,128,128]{2,1,0:T(8,128)S(1)}, u32[]{:S(2)}, u32[]{:S(2)}) collective-permute-start(f32[4,128,128]{2,1,0:T(8,128)} %get-tuple-element.14), channel_id=1, source_target_pairs={{0,1},{1,2},{2,3},{3,4},{4,5},{5,6},{6,7},{7,8},{8,9},{9,10},{10,1... | collective-permute-start | bytes 786440 | tf_op jit(solution)/shard_map/ppermute | solution.py:680
  10.4 8.5 %copy-start.2 = (f32[4,16,16]{2,1,0:T(8,128)S(1)}, f32[4,16,16]{2,1,0:T(8,128)}, u32[]{:S(2)}) copy-start(f32[4,16,16]{2,1,0:T(8,128)} %param.21) | copy-start | bytes 12292
  10.5 8.5 %copy-start.5 = (f32[16,16]{1,0:T(8,128)S(1)}, f32[16,16]{1,0:T(8,128)}, u32[]{:S(2)}) copy-start(f32[16,16]{1,0:T(8,128)} %param.20) | copy-start | bytes 3076
  10.5 18.7 %collective-permute-start.1 = (f32[4,128,128]{2,1,0:T(8,128)}, f32[4,128,128]{2,1,0:T(8,128)S(1)}, u32[]{:S(2)}, u32[]{:S(2)}) collective-permute-start(f32[4,128,128]{2,1,0:T(8,128)} %get-tuple-element.15), channel_id=1, source_target_pairs={{1,0},{2,1},{3,2},{4,3},{5,4},{6,5},{7,6},{8,7},{9,8},{10,9},{11,1... | collective-permute-start | bytes 786440 | tf_op jit(solution)/shard_map/ppermute | solution.py:681
  25.7 17.1 %all-to-all-start = ((f32[8,4,1024]{2,1,0:T(4,128)}), f32[8,4,1024]{2,1,0:T(4,128)S(1)}, u32[]{:S(2)}, u32[]{:S(2)}) async-start(f32[8,4,1024]{2,1,0:T(4,128)} %broadcast_in_dim.4), calls=%async_computation | async-start | bytes 262144 | tf_op jit(solution)/shard_map/all_to_all | solution.py:675
  29.1 0.7 copy-start.6
  29.1 0.8 copy-start.7
  30.0 23.4 %copy-start.3 = (s32[1,6,1024]{2,0,1:T(1,128)S(1)}, s32[1,6,1024]{2,0,1:T(1,128)}, u32[]{:S(2)}) copy-start(s32[1,6,1024]{2,0,1:T(1,128)} %param.24) | copy-start | bytes 73732
  30.0 24.0 %copy-start.4 = (f32[1,6,1024]{2,0,1:T(1,128)S(1)}, f32[1,6,1024]{2,0,1:T(1,128)}, u32[]{:S(2)}) copy-start(f32[1,6,1024]{2,0,1:T(1,128)} %param.25) | copy-start | bytes 73732
  42.8 0.7 copy-start.1
  48.3 15.4 %all-to-all-start.1 = ((f32[8,8,4,128]{3,2,1,0:T(4,128)}), f32[8,8,4,128]{3,2,1,0:T(4,128)S(1)}, u32[]{:S(2)}, u32[]{:S(2)}) async-start(f32[8,8,4,128]{3,2,1,0:T(4,128)} %bitcast.39), calls=%async_computation.1 | async-start | bytes 262144 | tf_op jit(solution)/shard_map/all_to_all | solution.py:705
  54.5 15.6 %collective-permute-start.5 = (f32[4,128,128]{2,1,0:T(8,128)}, f32[4,128,128]{2,1,0:T(8,128)S(1)}, u32[]{:S(2)}, u32[]{:S(2)}) collective-permute-start(f32[4,128,128]{2,1,0:T(8,128)} %get-tuple-element.20), channel_id=1, source_target_pairs={{0,1},{1,2},{2,3},{3,4},{4,5},{5,6},{6,7},{7,8},{8,9},{9,10},{10,1... | collective-permute-start | bytes 786440 | tf_op jit(solution)/shard_map/ppermute | solution.py:698
  57.0 13.2 %collective-permute-start.6 = (f32[4,128,128]{2,1,0:T(8,128)}, f32[4,128,128]{2,1,0:T(8,128)S(1)}, u32[]{:S(2)}, u32[]{:S(2)}) collective-permute-start(f32[4,128,128]{2,1,0:T(8,128)} %get-tuple-element.21), channel_id=1, source_target_pairs={{1,0},{2,1},{3,2},{4,3},{5,4},{6,5},{7,6},{8,7},{9,8},{10,9},{11,1... | collective-permute-start | bytes 786440 | tf_op jit(solution)/shard_map/ppermute | solution.py:699
  63.8 4.9 %collective-permute-start.9 = (f32[8,4,128]{2,1,0:T(4,128)S(1)}, f32[8,4,128]{2,1,0:T(4,128)S(1)}, u32[]{:S(2)}, u32[]{:S(2)}) collective-permute-start(f32[8,4,128]{2,1,0:T(4,128)S(1)} %reduce_sum.9), channel_id=1, source_target_pairs={{16,24},{17,25},{18,26},{19,27},{20,28},{21,29},{22,30},{23,31}} | collective-permute-start | bytes 49160 | tf_op jit(solution)/shard_map/ppermute | solution.py:709
  65.0 3.6 %collective-permute-start.8 = (f32[8,4,128]{2,1,0:T(4,128)S(1)}, f32[8,4,128]{2,1,0:T(4,128)S(1)}, u32[]{:S(2)}, u32[]{:S(2)}) collective-permute-start(f32[8,4,128]{2,1,0:T(4,128)S(1)} %reduce_sum.9), channel_id=1, source_target_pairs={{8,24},{9,25},{10,26},{11,27},{12,28},{13,29},{14,30},{15,31}} | collective-permute-start | bytes 49160 | tf_op jit(solution)/shard_map/ppermute | solution.py:709
  65.7 2.9 %collective-permute-start.7 = (f32[8,4,128]{2,1,0:T(4,128)S(1)}, f32[8,4,128]{2,1,0:T(4,128)S(1)}, u32[]{:S(2)}, u32[]{:S(2)}) collective-permute-start(f32[8,4,128]{2,1,0:T(4,128)S(1)} %reduce_sum.9), channel_id=1, source_target_pairs={{0,24},{1,25},{2,26},{3,27},{4,28},{5,29},{6,30},{7,31}} | collective-permute-start | bytes 49160 | tf_op jit(solution)/shard_map/ppermute | solution.py:709
  70.2 0.7 copy-start.8
  70.2 0.8 copy-start.9

commit v2 on v0

v2 whole, which is shorter than its diff:
```python
import functools

import jax
import jax.numpy as jnp
from jax import lax
from jax.experimental import pallas as pl
from jax.experimental.pallas import tpu as pltpu
from jax.sharding import PartitionSpec as P

RIM = 8
BLK = 128
HALO_O = 128
LANES = 128
GROUP = 8

F32 = jnp.float32
BF16 = jnp.bfloat16
ANY = pl.BlockSpec(memory_space=pl.ANY)
HBM = pl.BlockSpec(memory_space=pltpu.HBM)
SMEM = pl.BlockSpec(memory_space=pltpu.SMEM)
VMEM = pl.BlockSpec(memory_space=pltpu.VMEM)


def params(mib):
    return pltpu.CompilerParams(vmem_limit_bytes=mib << 20)


def cost(flops, moved):
    return pl.CostEstimate(flops=flops, bytes_accessed=moved, transcendentals=0)


def split(x):
    hi = x.astype(BF16)
    return hi, (x - hi.astype(F32)).astype(BF16)


def dot(a, b):
    return jnp.dot(a, b, preferred_element_type=F32)


def dot_t(a, b):
    return lax.dot_general(a, b, (((1,), (1,)), ((), ())), preferred_element_type=F32)


def turned(rows):
    n = rows.shape[0]
    if n < LANES:
        rows = jnp.concatenate([rows, jnp.zeros((LANES - n, LANES), rows.dtype)], axis=0)
    return rows.T


OCEAN, DOM, ELEM, CELL = range(4)


def copies(pairs, sem):
    return [pltpu.make_async_copy(a, b, sem.at[i]) for i, (a, b) in enumerate(pairs)]


def start(many):
    for one in many:
        one.start()


def wait(many):
    for one in many:
        one.wait()


def hand_out(dom, low_high, to_core, to_chip):
    core = dom[0] % 2
    to_core[...] = low_high[1 - core]
    to_chip[...] = low_high[core]


def take_in(dom, from_core, from_chip, f):
    first = dom[0] % 2 == 0
    a, b = from_core[f], from_chip[f]
    return jnp.where(first, b, a), jnp.where(first, a, b)


def turn_kernel(ocean, dom, x, o, xt, to_core, to_chip, surface, xv, tv, hv, in_sem, out_sem, o_sem):
    fields, points = xv.shape[0], 16
    olev, cells = o.shape[1], o.shape[2]
    groups = LANES // GROUP

    @pl.when(ocean[0] == 0)
    def _():
        loads = copies([(x.at[f], xv.at[f]) for f in range(fields)], in_sem)
        start(loads)
        outs = []
        levels = xv.shape[1] // points
        for f in range(fields):
            loads[f].wait()
            surface[f] = xv[f, pl.ds((levels - 1) * points, points), :]
            hi_at, lo_at = pl.ds(f * LANES, LANES), pl.ds((fields + f) * LANES, LANES)
            for q in range(0, points, 2):
                one = xv[f, pl.ds(q, LANES, stride=points), :].T
                two = xv[f, pl.ds(q + 1, LANES, stride=points), :].T
                for g in range(groups):
                    part = slice(g * GROUP, (g + 1) * GROUP)
                    rows = jnp.concatenate([one[part], two[part]], axis=0)
                    if g == 0:
                        hv[0, f, pl.ds(q * GROUP, 2 * GROUP), :] = rows
                    if g == groups - 1:
                        hv[1, f, pl.ds(q * GROUP, 2 * GROUP), :] = rows
                    hi, lo = split(rows)
                    at = pl.ds((g * points + q) * GROUP, 2 * GROUP)
                    tv[at, hi_at] = hi
                    tv[at, lo_at] = lo
            outs += copies([(tv.at[:, at], xt.at[:, at]) for at in (hi_at, lo_at)], out_sem.at[f])
            start(outs[-2:])
        hand_out(dom, hv, to_core, to_chip)
        wait(outs)

    @pl.when(ocean[0] != 0)
    def _():
        pairs = []
        for f in range(fields):
            pairs.append((o.at[f, :, pl.ds(0, HALO_O)], hv.at[0, f, pl.ds(0, olev)]))
            pairs.append((o.at[f, :, pl.ds(cells - HALO_O, HALO_O)], hv.at[1, f, pl.ds(0, olev)]))
        loads = copies(pairs, o_sem)
        start(loads)
        wait(loads)
        hand_out(dom, hv, to_core, to_chip)


def turn(ocean_flag, dom, state, ocean):
    fields, levels, points, elems = state.shape
    rows = points * elems
    halo = jax.ShapeDtypeStruct((fields, LANES, LANES), F32)
    return pl.pallas_call(
        turn_kernel,
        out_shape=(
            jax.ShapeDtypeStruct((rows, 2 * fields * LANES), BF16),
            halo,
            halo,
            jax.ShapeDtypeStruct((fields, points, elems), F32),
        ),
        in_specs=[SMEM, SMEM, ANY, ANY],
        out_specs=(ANY, VMEM, VMEM, VMEM),
        scratch_shapes=[
            pltpu.VMEM((fields, levels * points, elems), F32),
            pltpu.VMEM((rows, 2 * fields * LANES), BF16),
            pltpu.VMEM((2, fields, LANES, LANES), F32),
            pltpu.SemaphoreType.DMA((fields,)),
            pltpu.SemaphoreType.DMA((fields, 2)),
            pltpu.SemaphoreType.DMA((2 * fields,)),
        ],
        compiler_params=params(60),
        cost_estimate=cost(2_000_000_000, 9 << 20),
        name="turn_state",
    )(ocean_flag, dom, state.reshape(fields, levels * points, elems), ocean)


def table_kernel(ocean, base, nbr, coupling, stiffness, out, cx, nt, table, sem):
    blocks = table.shape[0]
    points = stiffness.shape[0]
    sides = nbr.shape[0]

    @pl.when(ocean[0] == 0)
    def _():
        nt[...] = turned((nbr[...] - base[0]).astype(F32))
        spread = lax.broadcasted_iota(jnp.int32, (points, LANES), 1) // GROUP
        spread = (spread == lax.broadcasted_iota(jnp.int32, (points, LANES), 0)).astype(F32)
        for ops, first in ((coupling, 0), (stiffness, sides * points)):
            cx[pl.ds(first, ops.shape[0]), :] = jnp.dot(
                ops[...], spread, precision=lax.Precision.HIGHEST, preferred_element_type=F32
            )
        lane = lax.broadcasted_iota(jnp.int32, (GROUP, LANES), 1) % GROUP
        lane_f = lane.astype(F32)
        same = lane == lax.broadcasted_iota(jnp.int32, (GROUP, LANES), 0)
        zero = jnp.zeros((LANES, LANES), BF16)

        @pl.loop(0, blocks)
        def _(block):
            for g in range(2):
                first = pl.multiple_of(block * 2 * GROUP + g * GROUP, GROUP)
                own = nt[pl.ds(first, GROUP), :]
                cols = [jnp.broadcast_to(own[:, s : s + 1], (GROUP, LANES)) for s in range(sides)]
                masks = {}
                for h in range(4):
                    if h - g not in (0, 1, 2):
                        at = pl.ds(h * LANES, LANES)
                        table[block, pl.ds(g * LANES, LANES), at] = zero
                        table[block, pl.ds((2 + g) * LANES, LANES), at] = zero
                        continue
                    begin = (block * 2 * GROUP + (h - 1) * GROUP).astype(F32)
                    masks[h] = [col - begin == lane_f for col in cols]
                for p in range(0, points, 2):
                    rows = [
                        [
                            jnp.broadcast_to(cx[pl.ds(s * points + pp, 1), :], (GROUP, LANES))
                            for s in range(sides + 1)
                        ]
                        for pp in (p, p + 1)
                    ]
                    for h in masks:
                        pair = []
                        for row in rows:
                            total = jnp.where(masks[h][0], row[0], 0.0)
                            for s in range(1, sides):
                                total = total + jnp.where(masks[h][s], row[s], 0.0)
                            if h == g + 1:
                                total = total + jnp.where(same, row[sides], 0.0)
                            pair.append(total)
                        top, rest = split(jnp.concatenate(pair, axis=0))
                        at = pl.ds(h * LANES, LANES)
                        table[block, pl.ds(g * LANES + p * GROUP, 2 * GROUP), at] = top
                        table[block, pl.ds((2 + g) * LANES + p * GROUP, 2 * GROUP), at] = rest
            pltpu.make_async_copy(table.at[block], out.at[block], sem.at[block]).start()

        wait(copies([(table.at[b], out.at[b]) for b in range(blocks)], sem))


def tables(ocean_flag, base, nbr, coupling, stiffness):
    points = stiffness.shape[0]
    sides = nbr.shape[0]
    blocks = nbr.shape[1] // (2 * GROUP)
    return pl.pallas_call(
        table_kernel,
        out_shape=jax.ShapeDtypeStruct((blocks, 4 * LANES, 4 * LANES), BF16),
        in_specs=[SMEM, SMEM, VMEM, VMEM, VMEM],
        out_specs=ANY,
        scratch_shapes=[
            pltpu.VMEM(((sides + 1) * points, LANES), F32),
            pltpu.VMEM((LANES, LANES), F32),
            pltpu.VMEM((blocks, 4 * LANES, 4 * LANES), BF16),
            pltpu.SemaphoreType.DMA((blocks,)),
        ],
        compiler_params=params(58),
        cost_estimate=cost(4_000_000_000, 4 << 20),
        name="neighbour_tables",
    )(ocean_flag, base, nbr, coupling.reshape(sides * points, points), stiffness)


def put_split(xhl, at, f, fields, x):
    hi, lo = split(x)
    xhl[at, pl.ds(f * LANES, LANES)] = hi
    xhl[at, pl.ds((fields + f) * LANES, LANES)] = lo


def columns(turned_rows, first, points):
    pieces = []
    for g in range(2):
        own = turned_rows[pl.ds(pl.multiple_of(first + g * GROUP, GROUP), GROUP), :]
        pieces += [jnp.broadcast_to(own[:, q : q + 1], (GROUP, LANES)) for q in range(points)]
    return jnp.concatenate(pieces, axis=0)


def advance(window, table, wa, mt, element, points, store):
    fields = window.shape[1] // (2 * LANES)
    width = fields * LANES
    rows = 2 * LANES
    heads = dot(table[...], window[:, pl.ds(0, width)])
    rest = dot(table[pl.ds(0, rows), :], window[:, pl.ds(width, width)])
    inner = pl.ds(LANES, rows)
    hi = [window[inner, f * LANES : (f + 1) * LANES] for f in range(fields)]
    lo = [window[inner, (fields + f) * LANES : (fields + f + 1) * LANES] for f in range(fields)]
    v = dot(jnp.concatenate([jnp.concatenate([a, b], axis=1) for a, b in zip(hi, lo)], axis=0), wa[...])
    m = columns(mt, element, points)
    for f in range(fields):
        at = slice(f * LANES, (f + 1) * LANES)
        own = slice(f * rows, (f + 1) * rows)
        tend = heads[:rows, at] + heads[rows:, at] + rest[:, at] + v[own, :LANES] + v[own, LANES:]
        store(f, hi[f].astype(F32) + lo[f].astype(F32) + m * tend)


def prepare(metric, vertical, wa, mt):
    mt[...] = turned(metric[...])
    hi, lo = split(vertical[...].T)
    wa[pl.ds(0, LANES), pl.ds(0, LANES)] = hi
    wa[pl.ds(LANES, LANES), pl.ds(0, LANES)] = hi
    wa[pl.ds(0, LANES), pl.ds(LANES, LANES)] = lo
    wa[pl.ds(LANES, LANES), pl.ds(LANES, LANES)] = jnp.zeros((LANES, LANES), BF16)


def put_flux(ft, flux):
    for f in range(flux.shape[0]):
        ft[f] = turned(-0.5 * flux[f])


def edge_windows(dom, xhl, x, from_core, from_chip):
    fields = from_core.shape[0]
    rows = x.shape[0]
    side = 3 * LANES
    xhl[pl.ds(LANES, side), :] = x[pl.ds(0, side), :]
    xhl[pl.ds(4 * LANES, side), :] = x[pl.ds(rows - side, side), :]
    for f in range(fields):
        left, right = take_in(dom, from_core, from_chip, f)
        put_split(xhl, pl.ds(0, LANES), f, fields, left)
        put_split(xhl, pl.ds(7 * LANES, LANES), f, fields, right)


def edge_kernel(ocean, dom, xt, from_core, from_chip, table, metric, vertical, flux, u, to_core, to_chip, xhl, hv, wa, mt, ft):
    fields, points = flux.shape[0], flux.shape[1]
    blocks = table.shape[0]

    @pl.when(ocean[0] == 0)
    def _():
        prepare(metric, vertical, wa, mt)
        put_flux(ft, flux)
        edge_windows(dom, xhl, xt, from_core, from_chip)
        last_lane = lax.broadcasted_iota(jnp.int32, (2 * LANES, LANES), 1) == LANES - 1
        for i in range(2):
            b = i * (blocks - 1)
            element = b * 2 * GROUP

            def store(f, value):
                value = value + jnp.where(last_lane, columns(ft.at[f], element, points), 0.0)
                put_split(u, pl.ds(i * 2 * LANES, 2 * LANES), f, fields, value)
                hv[i, f] = value[:LANES] if i == 0 else value[LANES:]

            advance(xhl.at[pl.ds(i * 4 * LANES, 4 * LANES)], table.at[b], wa, mt, element, points, store)
        hand_out(dom, hv, to_core, to_chip)


def edge_step(ocean_flag, dom, xt, from_core, from_chip, table, metric, vertical, flux):
    width = xt.shape[1]
    fields = flux.shape[0]
    halo = jax.ShapeDtypeStruct((fields, LANES, LANES), F32)
    return pl.pallas_call(
        edge_kernel,
        out_shape=(jax.ShapeDtypeStruct((4 * LANES, width), BF16), halo, halo),
        in_specs=[SMEM, SMEM] + [VMEM] * 7,
        out_specs=(VMEM, VMEM, VMEM),
        scratch_shapes=[
            pltpu.VMEM((8 * LANES, width), BF16),
            pltpu.VMEM((2, fields, LANES, LANES), F32),
            pltpu.VMEM((2 * LANES, 2 * LANES), BF16),
            pltpu.VMEM((LANES, LANES), F32),
            pltpu.VMEM((fields, LANES, LANES), F32),
        ],
        compiler_params=params(12),
        cost_estimate=cost(4_000_000_000, 3 << 20),
        name="edge_step",
    )(ocean_flag, dom, xt, from_core, from_chip, table, metric, vertical, flux)


def inner_kernel(
    ocean, dom, base, xt, ue, table, metric, vertical, flux, o, from_core, from_chip, nbr, diff, sea, overt,
    u, fresh, zeroed,
    wa, mt, ft, ov, ext, res, zv, o_sem, z_sem, r_sem,
):
    fields, points = flux.shape[0], flux.shape[1]
    rows = xt.shape[0]
    blocks = table.shape[0]
    edge = 2 * LANES

    @pl.when(ocean[0] == 0)
    def _():
        res[0] = jnp.zeros_like(res[0])
        zeros = copies([(res.at[0], fresh.at[f]) for f in range(fields)], z_sem)
        start(zeros)
        prepare(metric, vertical, wa, mt)
        put_flux(ft, flux)
        u[pl.ds(0, edge), :] = ue[pl.ds(0, edge), :]
        u[pl.ds(rows - edge, edge), :] = ue[pl.ds(edge, edge), :]
        last_lane = lax.broadcasted_iota(jnp.int32, (edge, LANES), 1) == LANES - 1

        @pl.loop(1, blocks - 1)
        def _(b):
            first = pl.multiple_of(b * edge, edge)
            element = b * 2 * GROUP

            def store(f, value):
                value = value + jnp.where(last_lane, columns(ft.at[f], element, points), 0.0)
                put_split(u, pl.ds(first, edge), f, fields, value)

            window = xt.at[pl.ds(pl.multiple_of(first - LANES, LANES), 4 * LANES)]
            advance(window, table.at[b], wa, mt, element, points, store)

        wait(zeros)

    @pl.when(ocean[0] != 0)
    def _():
        load = pltpu.make_async_copy(o, ov, o_sem.at[0])
        load.start()
        zv[...] = jnp.zeros_like(zv)
        zeros = copies([(zv, zeroed.at[f]) for f in range(fields)], z_sem)
        start(zeros)
        ocean_part(dom, base, load, from_core, from_chip, nbr, diff, sea, overt, fresh, ov, ext, res, r_sem)
        wait(zeros)


def ocean_part(dom, base, load, from_core, from_chip, nbr, diff, sea, overt, fresh, ov, ext, res, r_sem):
    fields, olev, cells = ov.shape
    sides = nbr.shape[0]
    for f in range(fields):
        rows = pl.ds(f * olev, olev)
        left, right = take_in(dom, from_core, from_chip, f)
        for at, value in ((0, left[:olev]), (HALO_O + cells, right[:olev])):
            hi, lo = split(value)
            ext[0, rows, pl.ds(at, HALO_O)] = hi
            ext[1, rows, pl.ds(at, HALO_O)] = lo
    load.wait()
    for f in range(fields):
        rows = pl.ds(f * olev, olev)
        hi, lo = split(ov[f])
        ext[0, rows, pl.ds(HALO_O, cells)] = hi
        ext[1, rows, pl.ds(HALO_O, cells)] = lo
    vhi, vlo = split(overt[...])

    @pl.loop(0, cells // LANES)
    def _(b):
        first = pl.multiple_of(b * LANES, LANES)
        here = pl.ds(first, LANES)
        begin = base[0] + first - HALO_O
        place = lax.broadcasted_iota(jnp.int32, (3 * LANES, LANES), 0)
        table = jnp.zeros((3 * LANES, LANES), F32)
        held = jnp.zeros((1, LANES), F32)
        for k in range(sides):
            d = diff[k, :, here]
            held = held + d
            table = table + jnp.where(place == nbr[k, :, here] - begin, d, 0.0)
        hi, lo = split(table)
        window = pl.ds(first, 3 * LANES)
        lap = dot(ext[0, :, window], hi) + dot(ext[1, :, window], hi) + dot(ext[0, :, window], lo)
        inner = pl.ds(pl.multiple_of(first + HALO_O, LANES), LANES)
        wet = sea[:, here] == 1
        for f in range(fields):
            rows = pl.ds(f * olev, olev)
            xhi, xlo = ext[0, rows, inner], ext[1, rows, inner]
            v = dot(vhi, xhi) + dot(vhi, xlo) + dot(vlo, xhi)
            own = ov[f, :, here]
            new = own + (lap[f * olev : (f + 1) * olev] - held * own) + v
            res[f, :, here] = jnp.where(wet, new, own)

    out = pltpu.make_async_copy(res, fresh, r_sem.at[0])
    out.start()
    out.wait()


def inner_step(
    ocean_flag, dom, base, xt, ue, table, metric, vertical, flux, ocean, from_core, from_chip, nbr, diff, sea, overt
):
    rows, width = xt.shape
    fields, points = flux.shape[0], flux.shape[1]
    olev, cells = ocean.shape[1], ocean.shape[2]
    return pl.pallas_call(
        inner_kernel,
        out_shape=(
            jax.ShapeDtypeStruct((rows, width), BF16),
            jax.ShapeDtypeStruct(ocean.shape, F32),
            jax.ShapeDtypeStruct((fields, rows, LANES), F32),
        ),
        in_specs=[SMEM, SMEM, SMEM] + [VMEM] * 6 + [HBM] + [VMEM] * 6,
        out_specs=(VMEM, HBM, HBM),
        scratch_shapes=[
            pltpu.VMEM((2 * LANES, 2 * LANES), BF16),
            pltpu.VMEM((LANES, LANES), F32),
            pltpu.VMEM((fields, LANES, LANES), F32),
            pltpu.VMEM(ocean.shape, F32),
            pltpu.VMEM((2, fields * olev, cells + 2 * HALO_O), BF16),
            pltpu.VMEM(ocean.shape, F32),
            pltpu.VMEM((rows, LANES), F32),
            pltpu.SemaphoreType.DMA((1,)),
            pltpu.SemaphoreType.DMA((fields,)),
            pltpu.SemaphoreType.DMA((1,)),
        ],
        compiler_params=params(20),
        cost_estimate=cost(10_000_000_000, 10 << 20),
        name="inner_step",
    )(ocean_flag, dom, base, xt, ue, table, metric, vertical, flux, ocean, from_core, from_chip, nbr, diff, sea, overt)


def flux_kernel(ocean, dom, owner, block, source, *refs):
    n_tops = len(refs) - 9
    tops = refs[:n_tops]
    weights, coef, sv, flux, sent, tv, wcat, surf, fl = refs[n_tops:]
    pairs = weights.shape[0]
    points, fields = coef.shape[0], flux.shape[0]
    ocean_blocks = sent.shape[0] // n_tops
    chips = n_tops // 2

    @pl.when(ocean[0] == 0)
    def _():
        surf[...] = jnp.zeros_like(surf)
        sent[...] = jnp.zeros_like(sent)
        chip, core = dom[0] // 2, dom[0] % 2

        def doubled(rows):
            hi, lo = split(rows)
            eight = jnp.concatenate([hi.astype(F32), lo.astype(F32)], axis=0).astype(BF16)
            return jnp.concatenate([eight, eight], axis=1)

        @pl.loop(0, pairs, unroll=4)
        def _(r):
            hi, lo = split(weights[r])
            wcat[r, :, pl.ds(0, BLK)] = hi
            wcat[r, :, pl.ds(BLK, BLK)] = lo

        for i in range(n_tops):
            tv[i] = tops[i][...]
        for r in range(pairs):
            at = pl.multiple_of(block[r] * BLK, BLK)
            which = owner[r]
            slot = ((which // 2) ^ chip) + jnp.where(which % 2 == core, 0, chips)
            rows = doubled(tv[slot, :, pl.ds(at, BLK)])
            out = dot_t(rows, wcat[r])
            surf[source[r]] += out[:fields] + out[fields:]

        for p in range(points):
            value = coef[pl.ds(p, 1), :] * (sv[:, p, :] - surf[p])
            fl[p] = value
            flux[:, p, :] = value

        for r in range(pairs):
            rows = doubled(fl[source[r]])
            both = jnp.concatenate([wcat[r, :, pl.ds(0, BLK)], wcat[r, :, pl.ds(BLK, BLK)]], axis=0)
            out = dot(rows, both)
            sent[owner[r] * ocean_blocks + block[r]] += out[:fields] + out[fields:]


def fluxes(ocean_flag, dom, owner, block, source, tops, weights, coef, surface, ocean_blocks):
    fields, points, elems = surface.shape
    pairs = weights.shape[0]
    n = len(tops)
    return pl.pallas_call(
        flux_kernel,
        out_shape=(
            jax.ShapeDtypeStruct((fields, points, elems), F32),
            jax.ShapeDtypeStruct((n * ocean_blocks, fields, BLK), F32),
        ),
        in_specs=[SMEM] * 5 + [VMEM] * (n + 3),
        out_specs=(VMEM, VMEM),
        scratch_shapes=[
            pltpu.VMEM((n,) + tops[0].shape, F32),
            pltpu.VMEM((pairs, BLK, 2 * BLK), BF16),
            pltpu.VMEM((points, fields, BLK), F32),
            pltpu.VMEM((points, fields, BLK), F32),
        ],
        compiler_params=params(8),
        cost_estimate=cost(4_000_000_000, 4 << 20),
        name="fluxes",
    )(ocean_flag, dom, owner, block, source, *tops, weights, coef, surface)


def second_kernel(ocean, dom, u, from_core, from_chip, table, metric, vertical, flux, held, out, xhl, wa, mt, xv, ov, o_sem):
    del held
    fields, points = flux.shape[0], flux.shape[1]
    rows, levels = xv.shape[1], xv.shape[2]
    blocks = table.shape[0]
    edge = 2 * LANES

    @pl.when(ocean[0] == 0)
    def _():
        prepare(metric, vertical, wa, mt)
        edge_windows(dom, xhl, u, from_core, from_chip)

        def step(b, window):
            def store(f, value):
                xv[f, pl.ds(b * edge if isinstance(b, int) else pl.multiple_of(b * edge, edge), edge), :] = value

            advance(window, table.at[b], wa, mt, b * 2 * GROUP, points, store)

        @pl.loop(1, blocks - 1)
        def _(b):
            step(b, u.at[pl.ds(pl.multiple_of(b * edge - LANES, LANES), 4 * LANES)])

        step(0, xhl.at[pl.ds(0, 4 * LANES)])
        step(blocks - 1, xhl.at[pl.ds(4 * LANES, 4 * LANES)])
        outs = copies([(ov.at[f], out.at[f]) for f in range(fields)], o_sem)
        for f in range(fields):
            for p in range(points):
                cols = [xv[f, pl.ds(g * LANES + p * GROUP, GROUP), :] for g in range(LANES // GROUP)]
                ov[f, pl.ds(p, LANES, stride=points), :] = jnp.concatenate(cols, axis=0).T
            last = pl.ds((levels - 1) * points, points)
            ov[f, last, :] = ov[f, last, :] - 0.5 * flux[f]
            outs[f].start()
        wait(outs)


def second_step(ocean_flag, dom, u, from_core, from_chip, table, metric, vertical, flux, zeroed, levels):
    fields, points = flux.shape[0], flux.shape[1]
    rows, width = u.shape
    return pl.pallas_call(
        second_kernel,
        out_shape=jax.ShapeDtypeStruct((fields, levels * points, LANES), F32),
        in_specs=[SMEM, SMEM] + [VMEM] * 7 + [HBM],
        out_specs=HBM,
        input_output_aliases={9: 0},
        scratch_shapes=[
            pltpu.VMEM((8 * LANES, width), BF16),
            pltpu.VMEM((2 * LANES, 2 * LANES), BF16),
            pltpu.VMEM((LANES, LANES), F32),
            pltpu.VMEM((fields, rows, levels), F32),
            pltpu.VMEM((fields, levels * points, LANES), F32),
            pltpu.SemaphoreType.DMA((fields,)),
        ],
        compiler_params=params(20),
        cost_estimate=cost(10_000_000_000, 12 << 20),
        name="second_step",
    )(ocean_flag, dom, u, from_core, from_chip, table, metric, vertical, flux, zeroed)


def gather_kernel(ocean, dom, a, b, c, same, other):
    chips = same.shape[0]
    per = same.shape[1]

    @pl.when(ocean[0] != 0)
    def _():
        chip, core = dom[0] // 2, dom[0] % 2
        for out, side in ((same, 0), (other, 1)):
            for s in range(chips):
                at = pl.ds(((chip ^ s) * 2 + (core ^ side)) * per, per)
                out[s] = a[at] + b[at] + c[at]


def gather_sent(ocean_flag, dom, parts, chips):
    total, fields, blk = parts[0].shape
    per = total // (2 * chips)
    shape = jax.ShapeDtypeStruct((chips, per, fields, blk), F32)
    return pl.pallas_call(
        gather_kernel,
        out_shape=(shape, shape),
        in_specs=[SMEM, SMEM, VMEM, VMEM, VMEM],
        out_specs=(VMEM, VMEM),
        compiler_params=params(4),
        cost_estimate=cost(0, 1 << 19),
        name="gather_sent",
    )(ocean_flag, dom, *parts)


def pair_kernel(ocean, same, other, *outs):
    @pl.when(ocean[0] != 0)
    def _():
        for s, out in enumerate(outs):
            out[...] = same[s] + other[s]


def pair_sums(ocean_flag, same, other):
    chips = same.shape[0]
    return pl.pallas_call(
        pair_kernel,
        out_shape=(jax.ShapeDtypeStruct(same.shape[1:], F32),) * chips,
        in_specs=[SMEM, VMEM, VMEM],
        out_specs=(VMEM,) * chips,
        compiler_params=params(4),
        cost_estimate=cost(0, 1 << 18),
        name="pair_sums",
    )(ocean_flag, same, other)


def finish_kernel(ocean, fresh, sea, *refs):
    del fresh
    n = len(refs) - 4
    parts, (out, rows_v, in_sem, out_sem) = refs[:n], refs[n:]
    fields, cells = rows_v.shape[0], rows_v.shape[2]

    @pl.when(ocean[0] != 0)
    def _():
        loads = copies([(out.at[f, pl.ds(0, 8)], rows_v.at[f]) for f in range(fields)], in_sem)
        start(loads)
        wait(loads)
        for b in range(cells // BLK):
            here = pl.ds(b * BLK, BLK)
            total = parts[0][b]
            for part in parts[1:]:
                total = total + part[b]
            total = jnp.where(sea[:, here] == 1, 0.5 * total, 0.0)
            for f in range(fields):
                rows_v[f, pl.ds(0, 1), here] = rows_v[f, pl.ds(0, 1), here] + total[f : f + 1]
        stores = copies([(rows_v.at[f], out.at[f, pl.ds(0, 8)]) for f in range(fields)], out_sem)
        start(stores)
        wait(stores)


def finish(ocean_flag, fresh, parts, sea):
    fields, olev, cells = fresh.shape
    return pl.pallas_call(
        finish_kernel,
        out_shape=jax.ShapeDtypeStruct(fresh.shape, F32),
        in_specs=[SMEM, HBM] + [VMEM] * (1 + len(parts)),
        out_specs=HBM,
        input_output_aliases={1: 0},
        scratch_shapes=[
            pltpu.VMEM((fields, 8, cells), F32),
            pltpu.SemaphoreType.DMA((fields,)),
            pltpu.SemaphoreType.DMA((fields,)),
        ],
        compiler_params=params(4),
        cost_estimate=cost(0, 1 << 18),
        name="finish_ocean",
    )(ocean_flag, fresh, sea, *parts)


def local(
    atm_state,
    elem_nbr,
    elem_metric,
    bulk_coef,
    stiffness,
    coupling,
    atm_vertical,
    ocean_state,
    cell_nbr,
    cell_diff,
    ocean_vertical,
    sea_mask,
    pair_owner,
    pair_block,
    pair_src,
    remap_weight,
):
    n_comp = lax.axis_size("comp")
    n_dom = lax.axis_size("dom")
    comp_index = lax.axis_index("comp")
    dom_index = lax.axis_index("dom")
    live = n_comp - 1
    chips = n_dom // 2
    state = atm_state[0]
    ocean = ocean_state[0]
    fields, levels, points, elems = state.shape
    cells = ocean.shape[2]
    ocean_blocks = cells // BLK
    one = lambda value: value.astype(jnp.int32).reshape(1)
    flag = one(comp_index == live)
    dom = one(dom_index)
    elem_base = one((comp_index * n_dom + dom_index) * elems)
    cell_base = one(dom_index * cells)

    both = ("comp", "dom")
    swapped = [(d, d ^ 1) for d in range(n_dom)]
    between = [(i, i + 1) for i in range(1, live * n_dom - 1, 2)]
    atm_chips = between + [(j, i) for i, j in between]
    between = [(live * n_dom + i, live * n_dom + i + 1) for i in range(1, n_dom - 1, 2)]
    all_chips = atm_chips + between + [(j, i) for i, j in between]

    def from_ocean(c):
        return [(live * n_dom + d, c * n_dom + d) for d in range(n_dom)]

    def to_ocean(c):
        return [(j, i) for i, j in from_ocean(c)]

    def shifted(by):
        return [(d, d ^ (2 * by)) for d in range(n_dom)]

    def among_ocean(pairs):
        return [(live * n_dom + a, live * n_dom + b) for a, b in pairs]

    top = ocean[:, 0, :]
    brought = [lax.ppermute(top, both, from_ocean(c)) for c in range(live)]
    xt, to_core, to_chip, surface = turn(flag, dom, state, ocean)
    brought, to_core, to_chip = lax.optimization_barrier((brought, to_core, to_chip))
    from_core = lax.ppermute(to_core, "dom", swapped)
    from_chip = lax.ppermute(to_chip, both, all_chips)
    got = sum(brought)
    near = [got] + [lax.ppermute(got, "dom", shifted(s)) for s in range(1, chips)]
    nbr, got = lax.optimization_barrier((elem_nbr[0], got))
    table = tables(flag, elem_base, nbr, coupling, stiffness)
    near, table = lax.optimization_barrier((near, table))
    tops = near + [lax.ppermute(part, "dom", swapped) for part in near]

    flux, sent = fluxes(
        flag,
        dom,
        pair_owner[0, :, 0],
        pair_block[0],
        pair_src[0],
        tops,
        remap_weight[0],
        bulk_coef[0],
        surface,
        ocean_blocks,
    )
    parts = [lax.ppermute(sent, both, to_ocean(c)) for c in range(live)]
    metric = elem_metric[0]
    ue, to_core, to_chip = edge_step(flag, dom, xt, from_core, from_chip, table, metric, atm_vertical, flux)
    from_core2 = lax.ppermute(to_core, "dom", swapped)
    from_chip2 = lax.ppermute(to_chip, both, atm_chips)

    u, fresh, zeroed = inner_step(
        flag,
        dom,
        cell_base,
        xt,
        ue,
        table,
        metric,
        atm_vertical,
        flux,
        ocean,
        from_core,
        from_chip,
        cell_nbr[0][:, None],
        cell_diff[0][:, None],
        sea_mask,
        ocean_vertical,
    )

    parts, u = lax.optimization_barrier((parts, u))
    same, other = gather_sent(flag, dom, parts, chips)
    arrived = lax.ppermute(other, both, among_ocean(swapped))
    pieces = pair_sums(flag, same, arrived)
    mine = [pieces[0]] + [
        lax.ppermute(pieces[s], both, among_ocean(shifted(s))) for s in range(1, chips)
    ]

    atm_next = second_step(flag, dom, u, from_core2, from_chip2, table, metric, atm_vertical, flux, zeroed, levels)
    ocean_next = finish(flag, fresh, mine, sea_mask)
    return (atm_next.reshape(state.shape)[None], ocean_next[None])


def solution(mesh):
    in_specs = (
        P("comp", None, None, None, "dom"),
        P("comp", None, "dom"),
        P("comp", None, "dom"),
        P("comp", None, "dom"),
        P(),
        P(),
        P(),
        P("comp", None, None, "dom"),
        P("comp", None, "dom"),
        P("comp", None, "dom"),
        P(),
        P("comp", "dom"),
        P("comp", "dom", None),
        P("comp", "dom"),
        P("comp", "dom"),
        P("comp", "dom", None, None),
    )
    out_specs = (P("comp", None, None, None, "dom"), P("comp", None, None, "dom"))
    return jax.shard_map(local, mesh=mesh, in_specs=in_specs, out_specs=out_specs, check_vma=False)
```

time: 363 us -> 55.3 us (0.15)
  local copies, waits for them, and re-layouts: 152 us -> 1.02 us
  matrix products: 113 us -> 0 us
  other arithmetic: 43.1 us -> 0.01 us
  Pallas kernels: 0 us -> 26 us
  starting transfers between devices: 42.4 us -> 22.7 us
    dot_general x18 -> x0, matrix products: 113 us -> none  [the longest x8 69.2 us: dynamics(): jnp.einsum('pq,flqe->flpe', coupling[side], beside, precision=highest)]
    select_n x8 -> x0, local copies, waits for them, and re-layouts: 58.4 us -> none  [dynamics(): beside = jnp.take(extended, index[side], axis=3)]
    gather x9 -> x0, local copies, waits for them, and re-layouts: 42.1 us -> none  [the longest x8 41.1 us: dynamics(): beside = jnp.take(extended, index[side], axis=3)]
    pallas_call x0 -> x9, Pallas kernels: none -> 26 us  [the longest x1 8.53 us: second_step(): pl.pallas_call(second_kernel, out_shape=jax.ShapeDtypeStruct((fields, lev...]
    select_n x5 -> x0, other arithmetic: 24.9 us -> none  [the longest x4 24 us: dynamics(): beside = jnp.take(extended, index[side], axis=3)]
    all_to_all x4 -> x0, starting transfers between devices: 20.7 us -> none  [the longest x1 6.1 us: local(): lax.all_to_all(request_ids.reshape(n_comp * n_dom, capacity), ('comp', 'd...]
    slice x6 -> x1, local copies, waits for them, and re-layouts: 16.1 us -> 0.92 us  [local(): top = ocean[:, 0, :]]
    concatenate x3 -> x0, other arithmetic: 13.7 us -> none  [extended_2(): shard = jnp.concatenate([before, shard, after], axis=dim)]
  transfers between devices with their start and end apart: 10 -> 21, of which waited for: 2 -> 3; matrix products, arithmetic and copies ran while one was open for 83% -> 0% of each run, Pallas kernels for 0% -> 32%
where the time goes in v2:
time: 55.3 us; the launch traced here: 54.8 us
  Pallas kernels  26 us (47%)
  starting transfers between devices  22.7 us (41%)
  waiting for transfers between devices  3.97 us (7%)
  between operations  1.19 us (2%)
  local copies, waits for them, and re-layouts  1.02 us (2%)
    pallas_call x1, Pallas kernels, second_step(): pl.pallas_call(second_kernel, out_shape=jax.ShapeDtypeStruct((fields, lev...  8.53 us
    pallas_call x1, Pallas kernels, turn(): pl.pallas_call(turn_kernel, out_shape=(jax.ShapeDtypeStruct((rows, 2 * fi...  4.98 us
    pallas_call x1, Pallas kernels, inner_step(): pl.pallas_call(inner_kernel, out_shape=(jax.ShapeDtypeStruct((rows, width...  4.81 us
    ppermute x3, starting transfers between devices, local(): lax.ppermute(got, 'dom', shifted(s))  4.72 us
    ppermute x1, starting transfers between devices, local(): from_chip = lax.ppermute(to_chip, both, all_chips)  4.57 us
    ppermute x1, starting transfers between devices, local(): from_chip2 = lax.ppermute(to_chip, both, atm_chips)  4.25 us
    pallas_call x1, Pallas kernels, tables(): pl.pallas_call(table_kernel, out_shape=jax.ShapeDtypeStruct((blocks, 4 *...  3.88 us
    ppermute x3, starting transfers between devices, local(): parts = [lax.ppermute(sent, both, to_ocean(c)) for c in range(live)]  2.77 us
  transfers between devices with their start and end apart: 21, of which 3 were waited for; matrix products, arithmetic and copies ran while one was open for 0% of the time, Pallas kernels for 32%

profile of v2, /device:TPU:4, one launch (start us, length us, event | category | flops | bytes accessed | tf_op | source)
XLA Modules:
  0.0 54.8 jit_solution(14583943059168835797)
XLA Ops:
  0.6 0.9 %slice.4 = f32[4,1,1024]{2,1,0:T(1,128)S(1)} slice(f32[4,80,1024]{2,1,0:T(8,128)} %bitcast.21), slice={[0:4], [0:1], [0:1024]} | slice | bytes 32768 | tf_op jit(solution)/shard_map/slice | solution.py:741
  1.6 0.7 %collective-permute-start = (f32[4,1024]{1,0:T(4,128)S(1)}, f32[4,1024]{1,0:T(4,128)S(1)}, u32[]{:S(2)}, u32[]{:S(2)}) collective-permute-start(f32[4,1024]{1,0:T(4,128)S(1)} %bitcast.35), channel_id=1, source_target_pairs={{24,0},{25,1},{26,2},{27,3},{28,4},{29,5},{30,6},{31,7}} | collective-permute-start | bytes 49160 | tf_op jit(solution)/shard_map/ppermute | solution.py:742
  2.2 0.7 %collective-permute-start.1 = (f32[4,1024]{1,0:T(4,128)S(1)}, f32[4,1024]{1,0:T(4,128)S(1)}, u32[]{:S(2)}, u32[]{:S(2)}) collective-permute-start(f32[4,1024]{1,0:T(4,128)S(1)} %bitcast.36), channel_id=1, source_target_pairs={{24,8},{25,9},{26,10},{27,11},{28,12},{29,13},{30,14},{31,15}} | collective-permute-start | bytes 49160 | tf_op jit(solution)/shard_map/ppermute | solution.py:742
  2.9 1.3 %collective-permute-start.2 = (f32[4,1024]{1,0:T(4,128)S(1)}, f32[4,1024]{1,0:T(4,128)S(1)}, u32[]{:S(2)}, u32[]{:S(2)}) collective-permute-start(f32[4,1024]{1,0:T(4,128)S(1)} %bitcast.37), channel_id=1, source_target_pairs={{24,16},{25,17},{26,18},{27,19},{28,20},{29,21},{30,22},{31,23}} | collective-permute-start | bytes 49160 | tf_op jit(solution)/shard_map/ppermute | solution.py:742
  4.2 5.0 %turn_state.1 = (bf16[2048,1024]{1,0:T(8,128)(2,1)}, f32[4,128,128]{2,1,0:T(8,128)}, f32[4,128,128]{2,1,0:T(8,128)}, f32[4,16,128]{2,1,0:T(8,128)}) custom-call(s32[1]{0:T(128)} %bitcast.ocean, s32[1]{0:T(128)} %bitcast.1.dom, f32[4,2048,128]{2,1,0:T(8,128)} %bitcast.38, f32[4,80,1024]{2,1,0:T(8,128)} %bitcast.22), custom_call_target="tpu_custom_call" | custom-call | flops 2000000000 | bytes 9437184 | tf_op jit(solution)/shard_map/turn_state/pallas_call | solution.py:131
  9.2 0.0 collective-permute-done
  9.2 0.0 collective-permute-done.1
  9.2 0.0 collective-permute-done.2
  9.3 2.1 %collective-permute-start.3 = (f32[4,1024]{1,0:T(4,128)S(1)}, f32[4,1024]{1,0:T(4,128)S(1)}, u32[]{:S(2)}, u32[]{:S(2)}) collective-permute-start(f32[4,1024]{1,0:T(4,128)S(1)} %add_add_fusion.refs_0_), channel_id=1, source_target_pairs={{0,2},{1,3},{2,0},{3,1},{4,6},{5,7},{6,4},{7,5},{8,10},{9,11},{10,... | collective-permute-start | bytes 49160 | tf_op jit(solution)/shard_map/ppermute | solution.py:748
  11.4 2.6 %collective-permute-start.4 = (f32[4,1024]{1,0:T(4,128)S(1)}, f32[4,1024]{1,0:T(4,128)S(1)}, u32[]{:S(2)}, u32[]{:S(2)}) collective-permute-start(f32[4,1024]{1,0:T(4,128)S(1)} %add_add_fusion.refs_0_), channel_id=1, source_target_pairs={{0,4},{1,5},{2,6},{3,7},{4,0},{5,1},{6,2},{7,3},{8,12},{9,13},{10,... | collective-permute-start | bytes 49160 | tf_op jit(solution)/shard_map/ppermute | solution.py:748
  14.0 0.0 collective-permute-start.5
  14.0 0.0 copy-start.7
  14.0 0.0 copy-start.9
  14.0 0.0 copy-start.10
  14.0 0.0 copy-start.11
  14.1 3.9 %neighbour_tables.1.table = bf16[8,512,512]{2,1,0:T(8,128)(2,1)} custom-call(s32[1]{0:T(128)} %bitcast.ocean, s32[1]{0:T(128)} %bitcast.7.base, s32[4,128]{1,0:T(4,128)} %bitcast.40, f32[64,16]{1,0:T(8,128)} %bitcast.39, f32[16,16]{1,0:T(8,128)} %stiffness.1), custom_call_target="tpu_custom_call" | custom-call | flops 4000000000 | bytes 4194304 | tf_op jit(solution)/shard_map/neighbour_tables/pallas_call | solution.py:219
  17.9 0.0 collective-permute-done.3.refs_1_
  18.0 0.0 collective-permute-done.4.refs_2_
  18.0 1.6 %collective-permute-done.5.refs_3_ = f32[4,1024]{1,0:T(4,128)S(1)} collective-permute-done((f32[4,1024]{1,0:T(4,128)S(1)}, f32[4,1024]{1,0:T(4,128)S(1)}, u32[]{:S(2)}, u32[]{:S(2)}) %collective-permute-start.5) | collective-permute-done | bytes 16416 | tf_op jit(solution)/shard_map/ppermute | solution.py:748
  19.5 0.0 collective-permute-start.6
  19.5 0.5 collective-permute-start.7
  20.0 0.0 collective-permute-start.8
  20.0 0.5 collective-permute-start.9
  20.5 0.0 collective-permute-start.13
  20.5 0.2 collective-permute-done.6.refs_4_
  20.7 0.0 copy-done.15
  20.7 4.6 %collective-permute-start.14 = (f32[4,128,128]{2,1,0:T(8,128)S(1)}, f32[4,128,128]{2,1,0:T(8,128)S(1)}, u32[]{:S(2)}, u32[]{:S(2)}) collective-permute-start(f32[4,128,128]{2,1,0:T(8,128)S(1)} %copy-done.15), channel_id=1, source_target_pairs={{1,2},{3,4},{5,6},{7,8},{9,10},{11,12},{13,14},{15,16},{17,18},{19... | collective-permute-start | bytes 786440 | tf_op jit(solution)/shard_map/ppermute | solution.py:746
  25.3 0.0 collective-permute-done.7.refs_5_
  25.3 0.0 collective-permute-done.8.refs_6_
  25.3 0.0 collective-permute-done.9.refs_7_
  25.4 0.0 copy-start.3
  25.4 0.0 copy-start.8
  25.4 0.0 copy-start.12
  25.4 2.0 %fluxes.1 = (f32[4,16,128]{2,1,0:T(8,128)S(1)}, f32[64,4,128]{2,1,0:T(4,128)S(1)}) custom-call(s32[1]{0:T(128)} %bitcast.ocean, s32[1]{0:T(128)} %bitcast.1.dom, s32[32]{0:T(128)S(1)} %bitcast.31, s32[32]{0:T(128)S(1)} %bitcast.32, s32[32]{0:T(128)S(1)} %bitcast.33, f32[4,1024]{1,0:T(4,128)S(1)} %add_add_fusion.refs_0_, ...), custom_call_target="tpu_custom_call" | custom-call | flops 4000000000 | bytes 4194304 | tf_op jit(solution)/shard_map/fluxes/pallas_call | solution.py:518
  27.5 0.8 %collective-permute-start.10 = (f32[64,4,128]{2,1,0:T(4,128)S(1)}, f32[64,4,128]{2,1,0:T(4,128)S(1)}, u32[]{:S(2)}, u32[]{:S(2)}) collective-permute-start(f32[64,4,128]{2,1,0:T(4,128)S(1)} %get-tuple-element.46), channel_id=1, source_target_pairs={{0,24},{1,25},{2,26},{3,27},{4,28},{5,29},{6,30},{7,31}} | collective-permute-start | bytes 393224 | tf_op jit(solution)/shard_map/ppermute | solution.py:766
  28.3 0.7 %collective-permute-start.11 = (f32[64,4,128]{2,1,0:T(4,128)S(1)}, f32[64,4,128]{2,1,0:T(4,128)S(1)}, u32[]{:S(2)}, u32[]{:S(2)}) collective-permute-start(f32[64,4,128]{2,1,0:T(4,128)S(1)} %get-tuple-element.46), channel_id=1, source_target_pairs={{8,24},{9,25},{10,26},{11,27},{12,28},{13,29},{14,30},{15,31}} | collective-permute-start | bytes 393224 | tf_op jit(solution)/shard_map/ppermute | solution.py:766
  28.9 1.3 %collective-permute-start.12 = (f32[64,4,128]{2,1,0:T(4,128)S(1)}, f32[64,4,128]{2,1,0:T(4,128)S(1)}, u32[]{:S(2)}, u32[]{:S(2)}) collective-permute-start(f32[64,4,128]{2,1,0:T(4,128)S(1)} %get-tuple-element.46), channel_id=1, source_target_pairs={{16,24},{17,25},{18,26},{19,27},{20,28},{21,29},{22,30},{23,31}} | collective-permute-start | bytes 393224 | tf_op jit(solution)/shard_map/ppermute | solution.py:766
  30.2 0.0 collective-permute-done.13.from_core
  30.3 2.2 %collective-permute-done.14.from_chip = f32[4,128,128]{2,1,0:T(8,128)S(1)} collective-permute-done((f32[4,128,128]{2,1,0:T(8,128)S(1)}, f32[4,128,128]{2,1,0:T(8,128)S(1)}, u32[]{:S(2)}, u32[]{:S(2)}) %collective-permute-start.14) | collective-permute-done | bytes 262176 | tf_op jit(solution)/shard_map/ppermute | solution.py:746
  32.5 0.0 copy-done.13
  32.5 0.0 copy-start
  32.5 0.0 copy-start.1
  32.5 0.0 copy-start.4
  32.5 0.0 copy-start.5
  32.5 0.0 copy-start.6
  32.5 1.6 %edge_step.1 = (bf16[512,1024]{1,0:T(8,128)(2,1)S(1)}, f32[4,128,128]{2,1,0:T(8,128)S(1)}, f32[4,128,128]{2,1,0:T(8,128)S(1)}) custom-call(s32[1]{0:T(128)} %bitcast.ocean, s32[1]{0:T(128)} %bitcast.1.dom, bf16[2048,1024]{1,0:T(8,128)(2,1)S(1)} %copy-done.12, f32[4,128,128]{2,1,0:T(8,128)S(1)} %collective-permute-done.13.from_core, ...), custom_call_target="tpu_custom_call" | custom-call | flops 4000000000 | bytes 3145728 | tf_op jit(solution)/shard_map/edge_step/pallas_call | solution.py:321
  34.2 0.1 collective-permute-start.15
  34.3 4.2 %collective-permute-start.16 = (f32[4,128,128]{2,1,0:T(8,128)S(1)}, f32[4,128,128]{2,1,0:T(8,128)S(1)}, u32[]{:S(2)}, u32[]{:S(2)}) collective-permute-start(f32[4,128,128]{2,1,0:T(8,128)S(1)} %get-tuple-element.56), channel_id=1, source_target_pairs={{1,2},{3,4},{5,6},{7,8},{9,10},{11,12},{13,14},{15,16},{17,18},{19... | collective-permute-start | bytes 786440 | tf_op jit(solution)/shard_map/ppermute | solution.py:770
  38.6 4.8 %inner_step.1 = (bf16[2048,1024]{1,0:T(8,128)(2,1)S(1)}, f32[4,80,1024]{2,1,0:T(8,128)}, f32[4,2048,128]{2,1,0:T(8,128)}) custom-call(s32[1]{0:T(128)} %bitcast.ocean, s32[1]{0:T(128)} %bitcast.1.dom, s32[1]{0:T(128)} %bitcast.12.base, bf16[2048,1024]{1,0:T(8,128)(2,1)S(1)} %copy-done.12, bf16[512,1024]{1,0:T(8,128)(2,1)S(1)} %get-tuple-element.52.ue, ...), custom_call_target="tpu_custom_call" | custom-call | flops 10000000000 | bytes 10485760 | tf_op jit(solution)/shard_map/inner_step/pallas_call | solution.py:439
  43.4 0.0 collective-permute-done.10.a
  43.4 0.0 collective-permute-done.11.b
  43.4 0.0 collective-permute-done.12.c
  43.4 0.7 %collective-permute-start.17 = (f32[4,8,4,128]{3,2,1,0:T(4,128)S(1)}, f32[4,8,4,128]{3,2,1,0:T(4,128)S(1)}, u32[]{:S(2)}, u32[]{:S(2)}) collective-permute-start(f32[4,8,4,128]{3,2,1,0:T(4,128)S(1)} %get-tuple-element.63), channel_id=1, source_target_pairs={{24,25},{25,24},{26,27},{27,26},{28,29},{29,28},{30,31},{31,30}} | collective-permute-start | bytes 196616 | tf_op jit(solution)/shard_map/ppermute | solution.py:793
  44.1 0.0 collective-permute-done.17.other
  44.1 0.7 %collective-permute-start.18 = (f32[8,4,128]{2,1,0:T(4,128)S(1)}, f32[8,4,128]{2,1,0:T(4,128)S(1)}, u32[]{:S(2)}, u32[]{:S(2)}) collective-permute-start(f32[8,4,128]{2,1,0:T(4,128)S(1)} %get-tuple-element.65), channel_id=1, source_target_pairs={{24,26},{25,27},{26,24},{27,25},{28,30},{29,31},{30,28},{31,29}} | collective-permute-start | bytes 49160 | tf_op jit(solution)/shard_map/ppermute | solution.py:796
  44.8 0.7 %collective-permute-start.19 = (f32[8,4,128]{2,1,0:T(4,128)S(1)}, f32[8,4,128]{2,1,0:T(4,128)S(1)}, u32[]{:S(2)}, u32[]{:S(2)}) collective-permute-start(f32[8,4,128]{2,1,0:T(4,128)S(1)} %get-tuple-element.66), channel_id=1, source_target_pairs={{24,28},{25,29},{26,30},{27,31},{28,24},{29,25},{30,26},{31,27}} | collective-permute-start | bytes 49160 | tf_op jit(solution)/shard_map/ppermute | solution.py:796
  45.5 0.7 %collective-permute-start.20 = (f32[8,4,128]{2,1,0:T(4,128)S(1)}, f32[8,4,128]{2,1,0:T(4,128)S(1)}, u32[]{:S(2)}, u32[]{:S(2)}) collective-permute-start(f32[8,4,128]{2,1,0:T(4,128)S(1)} %get-tuple-element.67), channel_id=1, source_target_pairs={{24,30},{25,31},{26,28},{27,29},{28,26},{29,27},{30,24},{31,25}} | collective-permute-start | bytes 49160 | tf_op jit(solution)/shard_map/ppermute | solution.py:796
  46.1 0.0 collective-permute-done.18.refs_1_
  46.1 0.0 collective-permute-done.19.refs_2_
  46.2 0.0 collective-permute-done.20.refs_3_
  46.2 0.1 finish_ocean.1
  46.3 0.0 collective-permute-done.15.from_core
  46.3 0.0 collective-permute-done.16.from_chip
  46.3 8.5 %second_step.1 = f32[4,2048,128]{2,1,0:T(8,128)} custom-call(s32[1]{0:T(128)} %bitcast.ocean, s32[1]{0:T(128)} %bitcast.1.dom, bf16[2048,1024]{1,0:T(8,128)(2,1)S(1)} %get-tuple-element.54.u, f32[4,128,128]{2,1,0:T(8,128)S(1)} %collective-permute-done.15.from_core, ...), custom_call_target="tpu_custom_call", output_to_operand_aliasing={{}: (9, {})} | custom-call | flops 10000000000 | bytes 12582912 | tf_op jit(solution)/shard_map/second_step/pallas_call | solution.py:576
  (24 shorter events, 0.1 us)
Async XLA Ops:
  1.6 7.6 %collective-permute-start = (f32[4,1024]{1,0:T(4,128)S(1)}, f32[4,1024]{1,0:T(4,128)S(1)}, u32[]{:S(2)}, u32[]{:S(2)}) collective-permute-start(f32[4,1024]{1,0:T(4,128)S(1)} %bitcast.35), channel_id=1, source_target_pairs={{24,0},{25,1},{26,2},{27,3},{28,4},{29,5},{30,6},{31,7}} | collective-permute-start | bytes 49160 | tf_op jit(solution)/shard_map/ppermute | solution.py:742
  2.2 7.0 %collective-permute-start.1 = (f32[4,1024]{1,0:T(4,128)S(1)}, f32[4,1024]{1,0:T(4,128)S(1)}, u32[]{:S(2)}, u32[]{:S(2)}) collective-permute-start(f32[4,1024]{1,0:T(4,128)S(1)} %bitcast.36), channel_id=1, source_target_pairs={{24,8},{25,9},{26,10},{27,11},{28,12},{29,13},{30,14},{31,15}} | collective-permute-start | bytes 49160 | tf_op jit(solution)/shard_map/ppermute | solution.py:742
  2.9 6.3 %collective-permute-start.2 = (f32[4,1024]{1,0:T(4,128)S(1)}, f32[4,1024]{1,0:T(4,128)S(1)}, u32[]{:S(2)}, u32[]{:S(2)}) collective-permute-start(f32[4,1024]{1,0:T(4,128)S(1)} %bitcast.37), channel_id=1, source_target_pairs={{24,16},{25,17},{26,18},{27,19},{28,20},{29,21},{30,22},{31,23}} | collective-permute-start | bytes 49160 | tf_op jit(solution)/shard_map/ppermute | solution.py:742
  9.3 8.7 %collective-permute-start.3 = (f32[4,1024]{1,0:T(4,128)S(1)}, f32[4,1024]{1,0:T(4,128)S(1)}, u32[]{:S(2)}, u32[]{:S(2)}) collective-permute-start(f32[4,1024]{1,0:T(4,128)S(1)} %add_add_fusion.refs_0_), channel_id=1, source_target_pairs={{0,2},{1,3},{2,0},{3,1},{4,6},{5,7},{6,4},{7,5},{8,10},{9,11},{10,... | collective-permute-start | bytes 49160 | tf_op jit(solution)/shard_map/ppermute | solution.py:748
  11.4 6.6 %collective-permute-start.4 = (f32[4,1024]{1,0:T(4,128)S(1)}, f32[4,1024]{1,0:T(4,128)S(1)}, u32[]{:S(2)}, u32[]{:S(2)}) collective-permute-start(f32[4,1024]{1,0:T(4,128)S(1)} %add_add_fusion.refs_0_), channel_id=1, source_target_pairs={{0,4},{1,5},{2,6},{3,7},{4,0},{5,1},{6,2},{7,3},{8,12},{9,13},{10,... | collective-permute-start | bytes 49160 | tf_op jit(solution)/shard_map/ppermute | solution.py:748
  14.0 5.5 %collective-permute-start.5 = (f32[4,1024]{1,0:T(4,128)S(1)}, f32[4,1024]{1,0:T(4,128)S(1)}, u32[]{:S(2)}, u32[]{:S(2)}) collective-permute-start(f32[4,1024]{1,0:T(4,128)S(1)} %add_add_fusion.refs_0_), channel_id=1, source_target_pairs={{0,6},{1,7},{2,4},{3,5},{4,2},{5,3},{6,0},{7,1},{8,14},{9,15},{10,... | collective-permute-start | bytes 49160 | tf_op jit(solution)/shard_map/ppermute | solution.py:748
  14.0 6.6 %copy-start.16 = (f32[4,128,128]{2,1,0:T(8,128)S(1)}, f32[4,128,128]{2,1,0:T(8,128)}, u32[]{:S(2)}) copy-start(f32[4,128,128]{2,1,0:T(8,128)} %get-tuple-element.48) | copy-start | bytes 786436
  14.0 6.7 %copy-start.15 = (f32[4,128,128]{2,1,0:T(8,128)S(1)}, f32[4,128,128]{2,1,0:T(8,128)}, u32[]{:S(2)}) copy-start(f32[4,128,128]{2,1,0:T(8,128)} %get-tuple-element.49) | copy-start | bytes 786436
  14.0 11.3 %copy-start.2 = (f32[1,32,128,128]{3,2,1,0:T(8,128)S(1)}, f32[1,32,128,128]{3,2,1,0:T(8,128)}, u32[]{:S(2)}) copy-start(f32[1,32,128,128]{3,2,1,0:T(8,128)} %param.31) | copy-start | bytes 6291460
  14.0 11.3 %copy-start.7 = (f32[1,16,128]{2,1,0:T(8,128)S(1)}, f32[1,16,128]{2,1,0:T(8,128)}, u32[]{:S(2)}) copy-start(f32[1,16,128]{2,1,0:T(8,128)} %param.19) | copy-start | bytes 24580
  14.0 11.3 %copy-start.9 = (s32[1,32,1]{1,2,0:T(1,128)S(1)}, s32[1,32,1]{1,2,0:T(1,128)}, u32[]{:S(2)}) copy-start(s32[1,32,1]{1,2,0:T(1,128)} %param.28) | copy-start | bytes 388
  14.0 11.3 %copy-start.10 = (s32[1,32]{1,0:T(1,128)S(1)}, s32[1,32]{1,0:T(1,128)}, u32[]{:S(2)}) copy-start(s32[1,32]{1,0:T(1,128)} %param.29) | copy-start | bytes 388
  14.0 11.3 %copy-start.11 = (s32[1,32]{1,0:T(1,128)S(1)}, s32[1,32]{1,0:T(1,128)}, u32[]{:S(2)}) copy-start(s32[1,32]{1,0:T(1,128)} %param.30) | copy-start | bytes 388
  14.0 11.3 %copy-start.14 = (f32[4,16,128]{2,1,0:T(8,128)S(1)}, f32[4,16,128]{2,1,0:T(8,128)}, u32[]{:S(2)}) copy-start(f32[4,16,128]{2,1,0:T(8,128)} %get-tuple-element.45.refs_10_) | copy-start | bytes 98308
  19.5 1.2 %collective-permute-start.6 = (f32[4,1024]{1,0:T(4,128)S(1)}, f32[4,1024]{1,0:T(4,128)S(1)}, u32[]{:S(2)}, u32[]{:S(2)}) collective-permute-start(f32[4,1024]{1,0:T(4,128)S(1)} %add_add_fusion.refs_0_), channel_id=1, source_target_pairs={{0,1},{1,0},{2,3},{3,2},{4,5},{5,4},{6,7},{7,6},{8,9},{9,8},{10,11... | collective-permute-start | bytes 49160 | tf_op jit(solution)/shard_map/ppermute | solution.py:752
  19.5 5.8 %collective-permute-start.7 = (f32[4,1024]{1,0:T(4,128)S(1)}, f32[4,1024]{1,0:T(4,128)S(1)}, u32[]{:S(2)}, u32[]{:S(2)}) collective-permute-start(f32[4,1024]{1,0:T(4,128)S(1)} %collective-permute-done.3.refs_1_), channel_id=1, source_target_pairs={{0,1},{1,0},{2,3},{3,2},{4,5},{5,4},{6,7},{7,6},{8,9},{9,8},{10,11... | collective-permute-start | bytes 49160 | tf_op jit(solution)/shard_map/ppermute | solution.py:752
  20.0 5.3 %collective-permute-start.8 = (f32[4,1024]{1,0:T(4,128)S(1)}, f32[4,1024]{1,0:T(4,128)S(1)}, u32[]{:S(2)}, u32[]{:S(2)}) collective-permute-start(f32[4,1024]{1,0:T(4,128)S(1)} %collective-permute-done.4.refs_2_), channel_id=1, source_target_pairs={{0,1},{1,0},{2,3},{3,2},{4,5},{5,4},{6,7},{7,6},{8,9},{9,8},{10,11... | collective-permute-start | bytes 49160 | tf_op jit(solution)/shard_map/ppermute | solution.py:752
  20.0 5.3 %collective-permute-start.9 = (f32[4,1024]{1,0:T(4,128)S(1)}, f32[4,1024]{1,0:T(4,128)S(1)}, u32[]{:S(2)}, u32[]{:S(2)}) collective-permute-start(f32[4,1024]{1,0:T(4,128)S(1)} %collective-permute-done.5.refs_3_), channel_id=1, source_target_pairs={{0,1},{1,0},{2,3},{3,2},{4,5},{5,4},{6,7},{7,6},{8,9},{9,8},{10,11... | collective-permute-start | bytes 49160 | tf_op jit(solution)/shard_map/ppermute | solution.py:752
  20.5 9.7 %collective-permute-start.13 = (f32[4,128,128]{2,1,0:T(8,128)S(1)}, f32[4,128,128]{2,1,0:T(8,128)S(1)}, u32[]{:S(2)}, u32[]{:S(2)}) collective-permute-start(f32[4,128,128]{2,1,0:T(8,128)S(1)} %copy-done.16), channel_id=1, source_target_pairs={{0,1},{1,0},{2,3},{3,2},{4,5},{5,4},{6,7},{7,6},{8,9},{9,8},{10,11... | collective-permute-start | bytes 786440 | tf_op jit(solution)/shard_map/ppermute | solution.py:745
  20.7 11.8 %collective-permute-start.14 = (f32[4,128,128]{2,1,0:T(8,128)S(1)}, f32[4,128,128]{2,1,0:T(8,128)S(1)}, u32[]{:S(2)}, u32[]{:S(2)}) collective-permute-start(f32[4,128,128]{2,1,0:T(8,128)S(1)} %copy-done.15), channel_id=1, source_target_pairs={{1,2},{3,4},{5,6},{7,8},{9,10},{11,12},{13,14},{15,16},{17,18},{19... | collective-permute-start | bytes 786440 | tf_op jit(solution)/shard_map/ppermute | solution.py:746
  25.4 7.1 %copy-start.3 = (f32[128,128]{1,0:T(8,128)S(1)}, f32[128,128]{1,0:T(8,128)}, u32[]{:S(2)}) copy-start(f32[128,128]{1,0:T(8,128)} %vertical.5) | copy-start | bytes 196612
  25.4 7.1 %copy-start.8 = (f32[1,16,128]{2,1,0:T(8,128)S(1)}, f32[1,16,128]{2,1,0:T(8,128)}, u32[]{:S(2)}) copy-start(f32[1,16,128]{2,1,0:T(8,128)} %param.18) | copy-start | bytes 24580
  25.4 7.1 %copy-start.12 = (bf16[2048,1024]{1,0:T(8,128)(2,1)S(1)}, bf16[2048,1024]{1,0:T(8,128)(2,1)}, u32[]{:S(2)}) copy-start(bf16[2048,1024]{1,0:T(8,128)(2,1)} %get-tuple-element.47.xt) | copy-start | bytes 12582916
  25.4 7.1 %copy-start.13 = (bf16[8,512,512]{2,1,0:T(8,128)(2,1)S(1)}, bf16[8,512,512]{2,1,0:T(8,128)(2,1)}, u32[]{:S(2)}) copy-start(bf16[8,512,512]{2,1,0:T(8,128)(2,1)} %neighbour_tables.1.table) | copy-start | bytes 12582916
  27.5 15.9 %collective-permute-start.10 = (f32[64,4,128]{2,1,0:T(4,128)S(1)}, f32[64,4,128]{2,1,0:T(4,128)S(1)}, u32[]{:S(2)}, u32[]{:S(2)}) collective-permute-start(f32[64,4,128]{2,1,0:T(4,128)S(1)} %get-tuple-element.46), channel_id=1, source_target_pairs={{0,24},{1,25},{2,26},{3,27},{4,28},{5,29},{6,30},{7,31}} | collective-permute-start | bytes 393224 | tf_op jit(solution)/shard_map/ppermute | solution.py:766
  28.3 15.1 %collective-permute-start.11 = (f32[64,4,128]{2,1,0:T(4,128)S(1)}, f32[64,4,128]{2,1,0:T(4,128)S(1)}, u32[]{:S(2)}, u32[]{:S(2)}) collective-permute-start(f32[64,4,128]{2,1,0:T(4,128)S(1)} %get-tuple-element.46), channel_id=1, source_target_pairs={{8,24},{9,25},{10,26},{11,27},{12,28},{13,29},{14,30},{15,31}} | collective-permute-start | bytes 393224 | tf_op jit(solution)/shard_map/ppermute | solution.py:766
  28.9 14.5 %collective-permute-start.12 = (f32[64,4,128]{2,1,0:T(4,128)S(1)}, f32[64,4,128]{2,1,0:T(4,128)S(1)}, u32[]{:S(2)}, u32[]{:S(2)}) collective-permute-start(f32[64,4,128]{2,1,0:T(4,128)S(1)} %get-tuple-element.46), channel_id=1, source_target_pairs={{16,24},{17,25},{18,26},{19,27},{20,28},{21,29},{22,30},{23,31}} | collective-permute-start | bytes 393224 | tf_op jit(solution)/shard_map/ppermute | solution.py:766
  32.5 6.0 %copy-start = (s32[1,1024]{1,0:T(1,128)S(1)}, s32[1,1024]{1,0:T(1,128)}, u32[]{:S(2)}) copy-start(s32[1,1024]{1,0:T(1,128)} %sea.3) | copy-start | bytes 12292
  32.5 6.0 %copy-start.1 = (f32[1,4,80,1024]{3,2,1,0:T(8,128)S(1)}, f32[1,4,80,1024]{3,2,1,0:T(8,128)}, u32[]{:S(2)}) copy-start(f32[1,4,80,1024]{3,2,1,0:T(8,128)} %param.23) | copy-start | bytes 3932164
  32.5 6.0 %copy-start.4 = (f32[80,80]{1,0:T(8,128)S(1)}, f32[80,80]{1,0:T(8,128)}, u32[]{:S(2)}) copy-start(f32[80,80]{1,0:T(8,128)} %overt.1) | copy-start | bytes 76804
  32.5 6.0 %copy-start.5 = (s32[1,6,1024]{2,0,1:T(1,128)S(1)}, s32[1,6,1024]{2,0,1:T(1,128)}, u32[]{:S(2)}) copy-start(s32[1,6,1024]{2,0,1:T(1,128)} %param.24) | copy-start | bytes 73732
  32.5 6.0 %copy-start.6 = (f32[1,6,1024]{2,0,1:T(1,128)S(1)}, f32[1,6,1024]{2,0,1:T(1,128)}, u32[]{:S(2)}) copy-start(f32[1,6,1024]{2,0,1:T(1,128)} %param.25) | copy-start | bytes 73732
  34.2 12.1 %collective-permute-start.15 = (f32[4,128,128]{2,1,0:T(8,128)S(1)}, f32[4,128,128]{2,1,0:T(8,128)S(1)}, u32[]{:S(2)}, u32[]{:S(2)}) collective-permute-start(f32[4,128,128]{2,1,0:T(8,128)S(1)} %get-tuple-element.55), channel_id=1, source_target_pairs={{0,1},{1,0},{2,3},{3,2},{4,5},{5,4},{6,7},{7,6},{8,9},{9,8},{10,11... | collective-permute-start | bytes 786440 | tf_op jit(solution)/shard_map/ppermute | solution.py:769
  34.3 12.0 %collective-permute-start.16 = (f32[4,128,128]{2,1,0:T(8,128)S(1)}, f32[4,128,128]{2,1,0:T(8,128)S(1)}, u32[]{:S(2)}, u32[]{:S(2)}) collective-permute-start(f32[4,128,128]{2,1,0:T(8,128)S(1)} %get-tuple-element.56), channel_id=1, source_target_pairs={{1,2},{3,4},{5,6},{7,8},{9,10},{11,12},{13,14},{15,16},{17,18},{19... | collective-permute-start | bytes 786440 | tf_op jit(solution)/shard_map/ppermute | solution.py:770
  43.4 0.7 %collective-permute-start.17 = (f32[4,8,4,128]{3,2,1,0:T(4,128)S(1)}, f32[4,8,4,128]{3,2,1,0:T(4,128)S(1)}, u32[]{:S(2)}, u32[]{:S(2)}) collective-permute-start(f32[4,8,4,128]{3,2,1,0:T(4,128)S(1)} %get-tuple-element.63), channel_id=1, source_target_pairs={{24,25},{25,24},{26,27},{27,26},{28,29},{29,28},{30,31},{31,30}} | collective-permute-start | bytes 196616 | tf_op jit(solution)/shard_map/ppermute | solution.py:793
  44.1 2.0 %collective-permute-start.18 = (f32[8,4,128]{2,1,0:T(4,128)S(1)}, f32[8,4,128]{2,1,0:T(4,128)S(1)}, u32[]{:S(2)}, u32[]{:S(2)}) collective-permute-start(f32[8,4,128]{2,1,0:T(4,128)S(1)} %get-tuple-element.65), channel_id=1, source_target_pairs={{24,26},{25,27},{26,24},{27,25},{28,30},{29,31},{30,28},{31,29}} | collective-permute-start | bytes 49160 | tf_op jit(solution)/shard_map/ppermute | solution.py:796
  44.8 1.4 %collective-permute-start.19 = (f32[8,4,128]{2,1,0:T(4,128)S(1)}, f32[8,4,128]{2,1,0:T(4,128)S(1)}, u32[]{:S(2)}, u32[]{:S(2)}) collective-permute-start(f32[8,4,128]{2,1,0:T(4,128)S(1)} %get-tuple-element.66), channel_id=1, source_target_pairs={{24,28},{25,29},{26,30},{27,31},{28,24},{29,25},{30,26},{31,27}} | collective-permute-start | bytes 49160 | tf_op jit(solution)/shard_map/ppermute | solution.py:796
  45.5 0.7 %collective-permute-start.20 = (f32[8,4,128]{2,1,0:T(4,128)S(1)}, f32[8,4,128]{2,1,0:T(4,128)S(1)}, u32[]{:S(2)}, u32[]{:S(2)}) collective-permute-start(f32[8,4,128]{2,1,0:T(4,128)S(1)} %get-tuple-element.67), channel_id=1, source_target_pairs={{24,30},{25,31},{26,28},{27,29},{28,26},{29,27},{30,24},{31,25}} | collective-permute-start | bytes 49160 | tf_op jit(solution)/shard_map/ppermute | solution.py:796

commit v3 on v2

v3 whole, which is shorter than its diff:
```python
import functools

import jax
import jax.numpy as jnp
from jax import lax
from jax.experimental import pallas as pl
from jax.experimental.pallas import tpu as pltpu
from jax.sharding import PartitionSpec as P

RIM = 8
BLK = 128
HALO_O = 128
LANES = 128
GROUP = 8
TURN = 60

F32 = jnp.float32
BF16 = jnp.bfloat16
ANY = pl.BlockSpec(memory_space=pl.ANY)
HBM = pl.BlockSpec(memory_space=pltpu.HBM)
SMEM = pl.BlockSpec(memory_space=pltpu.SMEM)
VMEM = pl.BlockSpec(memory_space=pltpu.VMEM)


def params(mib):
    return pltpu.CompilerParams(vmem_limit_bytes=mib << 20)


def cost(flops, moved):
    return pl.CostEstimate(flops=flops, bytes_accessed=moved, transcendentals=0)


def split(x):
    hi = x.astype(BF16)
    return hi, (x - hi.astype(F32)).astype(BF16)


def dot(a, b):
    return jnp.dot(a, b, preferred_element_type=F32)


def dot_t(a, b):
    return lax.dot_general(a, b, (((1,), (1,)), ((), ())), preferred_element_type=F32)


def turned(rows):
    n = rows.shape[0]
    if n < LANES:
        rows = jnp.concatenate([rows, jnp.zeros((LANES - n, LANES), rows.dtype)], axis=0)
    return rows.T


OCEAN, DOM, ELEM, CELL = range(4)


def copies(pairs, sem):
    return [pltpu.make_async_copy(a, b, sem.at[i]) for i, (a, b) in enumerate(pairs)]


def start(many):
    for one in many:
        one.start()


def wait(many):
    for one in many:
        one.wait()


def hand_out(dom, low_high, to_core, to_chip):
    core = dom[0] % 2
    to_core[...] = low_high[1 - core]
    to_chip[...] = low_high[core]


def take_in(dom, from_core, from_chip, f):
    first = dom[0] % 2 == 0
    a, b = from_core[f], from_chip[f]
    return jnp.where(first, b, a), jnp.where(first, a, b)


def turn_kernel(ocean, dom, x, o, xt, to_core, to_chip, surface, zeroed, xv, tv, hv, in_sem, out_sem, o_sem, z_sem):
    fields, points = xv.shape[0], 16
    olev, cells = o.shape[1], o.shape[2]
    groups = LANES // GROUP

    @pl.when(ocean[0] == 0)
    def _():
        loads = copies([(x.at[f], xv.at[f]) for f in range(fields)], in_sem)
        start(loads)
        outs = []
        levels = xv.shape[1] // points
        for f in range(fields):
            loads[f].wait()
            surface[f] = xv[f, pl.ds((levels - 1) * points, points), :]
            hi_at, lo_at = pl.ds(f * LANES, LANES), pl.ds((fields + f) * LANES, LANES)
            for q in range(0, points, 2):
                one = xv[f, pl.ds(q, LANES, stride=points), :].T
                two = xv[f, pl.ds(q + 1, LANES, stride=points), :].T
                for g in range(groups):
                    part = slice(g * GROUP, (g + 1) * GROUP)
                    rows = jnp.concatenate([one[part], two[part]], axis=0)
                    if g == 0:
                        hv[0, f, pl.ds(q * GROUP, 2 * GROUP), :] = rows
                    if g == groups - 1:
                        hv[1, f, pl.ds(q * GROUP, 2 * GROUP), :] = rows
                    hi, lo = split(rows)
                    at = pl.ds((g * points + q) * GROUP, 2 * GROUP)
                    tv[at, hi_at] = hi
                    tv[at, lo_at] = lo
            outs += copies([(tv.at[:, at], xt.at[:, at]) for at in (hi_at, lo_at)], out_sem.at[f])
            start(outs[-2:])
        hand_out(dom, hv, to_core, to_chip)
        wait(outs)

    @pl.when(ocean[0] != 0)
    def _():
        xv[0] = jnp.zeros_like(xv[0])
        zeros = copies([(xv.at[0], zeroed.at[f]) for f in range(fields)], z_sem)
        pairs = []
        for f in range(fields):
            pairs.append((o.at[f, :, pl.ds(0, HALO_O)], hv.at[0, f, pl.ds(0, olev)]))
            pairs.append((o.at[f, :, pl.ds(cells - HALO_O, HALO_O)], hv.at[1, f, pl.ds(0, olev)]))
        loads = copies(pairs, o_sem)
        start(loads)
        start(zeros)
        wait(loads)
        hand_out(dom, hv, to_core, to_chip)
        wait(zeros)


def turn(ocean_flag, dom, state, ocean):
    fields, levels, points, elems = state.shape
    rows = points * elems
    halo = jax.ShapeDtypeStruct((fields, LANES, LANES), F32)
    return pl.pallas_call(
        turn_kernel,
        out_shape=(
            jax.ShapeDtypeStruct((rows, 2 * fields * LANES), BF16),
            halo,
            halo,
            jax.ShapeDtypeStruct((fields, points, elems), F32),
            jax.ShapeDtypeStruct((fields, levels * points, elems), F32),
        ),
        in_specs=[SMEM, SMEM, ANY, ANY],
        out_specs=(ANY, VMEM, VMEM, VMEM, HBM),
        scratch_shapes=[
            pltpu.VMEM((fields, levels * points, elems), F32),
            pltpu.VMEM((rows, 2 * fields * LANES), BF16),
            pltpu.VMEM((2, fields, LANES, LANES), F32),
            pltpu.SemaphoreType.DMA((fields,)),
            pltpu.SemaphoreType.DMA((fields, 2)),
            pltpu.SemaphoreType.DMA((2 * fields,)),
            pltpu.SemaphoreType.DMA((fields,)),
        ],
        compiler_params=params(TURN),
        cost_estimate=cost(2000000000, 9 << 20),
        name="turn_state",
    )(ocean_flag, dom, state.reshape(fields, levels * points, elems), ocean)


def prepare_table(base, nbr, coupling, stiffness, cx, nt):
    points = stiffness.shape[0]
    nt[...] = turned((nbr[...] - base[0]).astype(F32))
    spread = lax.broadcasted_iota(jnp.int32, (points, LANES), 1) // GROUP
    spread = (spread == lax.broadcasted_iota(jnp.int32, (points, LANES), 0)).astype(F32)
    for ops, first in ((coupling, 0), (stiffness, coupling.shape[0])):
        cx[pl.ds(first, ops.shape[0]), :] = jnp.dot(
            ops[...], spread, precision=lax.Precision.HIGHEST, preferred_element_type=F32
        )


def build_table(block, table, slot, cx, nt, sides, points):
    lane = lax.broadcasted_iota(jnp.int32, (GROUP, LANES), 1) % GROUP
    lane_f = lane.astype(F32)
    same = lane == lax.broadcasted_iota(jnp.int32, (GROUP, LANES), 0)
    zero = jnp.zeros((LANES, LANES), BF16)
    for g in range(2):
        first = pl.multiple_of(block * 2 * GROUP + g * GROUP, GROUP)
        own = nt[pl.ds(first, GROUP), :]
        cols = [jnp.broadcast_to(own[:, s : s + 1], (GROUP, LANES)) for s in range(sides)]
        masks = {}
        for h in range(4):
            if h - g not in (0, 1, 2):
                at = pl.ds(h * LANES, LANES)
                table[slot, pl.ds(g * LANES, LANES), at] = zero
                table[slot, pl.ds((2 + g) * LANES, LANES), at] = zero
                continue
            begin = jnp.asarray(block * 2 * GROUP + (h - 1) * GROUP, jnp.int32).astype(F32)
            masks[h] = [col - begin == lane_f for col in cols]
        for p in range(0, points, 2):
            rows = [
                [jnp.broadcast_to(cx[pl.ds(s * points + pp, 1), :], (GROUP, LANES)) for s in range(sides + 1)]
                for pp in (p, p + 1)
            ]
            for h in masks:
                pair = []
                for row in rows:
                    total = jnp.where(masks[h][0], row[0], 0.0)
                    for s in range(1, sides):
                        total = total + jnp.where(masks[h][s], row[s], 0.0)
                    if h == g + 1:
                        total = total + jnp.where(same, row[sides], 0.0)
                    pair.append(total)
                top, rest = split(jnp.concatenate(pair, axis=0))
                at = pl.ds(h * LANES, LANES)
                table[slot, pl.ds(g * LANES + p * GROUP, 2 * GROUP), at] = top
                table[slot, pl.ds((2 + g) * LANES + p * GROUP, 2 * GROUP), at] = rest


def put_split(xhl, at, f, fields, x):
    hi, lo = split(x)
    xhl[at, pl.ds(f * LANES, LANES)] = hi
    xhl[at, pl.ds((fields + f) * LANES, LANES)] = lo


def columns(turned_rows, first, points):
    pieces = []
    for g in range(2):
        own = turned_rows[pl.ds(pl.multiple_of(first + g * GROUP, GROUP), GROUP), :]
        pieces += [jnp.broadcast_to(own[:, q : q + 1], (GROUP, LANES)) for q in range(points)]
    return jnp.concatenate(pieces, axis=0)


def advance(window, table, wa, mt, element, points, store, chosen):
    fields = window.shape[1] // (2 * LANES)
    rows = 2 * LANES
    n = len(chosen)
    heads = dot(table[...], window[:, pl.ds(chosen[0] * LANES, n * LANES)])
    rest = dot(table[pl.ds(0, rows), :], window[:, pl.ds((fields + chosen[0]) * LANES, n * LANES)])
    inner = pl.ds(LANES, rows)
    hi = [window[inner, f * LANES : (f + 1) * LANES] for f in chosen]
    lo = [window[inner, (fields + f) * LANES : (fields + f + 1) * LANES] for f in chosen]
    v = dot(jnp.concatenate([jnp.concatenate([a, b], axis=1) for a, b in zip(hi, lo)], axis=0), wa[...])
    m = columns(mt, element, points)
    for i, f in enumerate(chosen):
        at = slice(i * LANES, (i + 1) * LANES)
        own = slice(i * rows, (i + 1) * rows)
        tend = heads[:rows, at] + heads[rows:, at] + rest[:, at] + v[own, :LANES] + v[own, LANES:]
        store(f, hi[i].astype(F32) + lo[i].astype(F32) + m * tend)


def prepare(metric, vertical, wa, mt):
    mt[...] = turned(metric[...])
    hi, lo = split(vertical[...].T)
    wa[pl.ds(0, LANES), pl.ds(0, LANES)] = hi
    wa[pl.ds(LANES, LANES), pl.ds(0, LANES)] = hi
    wa[pl.ds(0, LANES), pl.ds(LANES, LANES)] = lo
    wa[pl.ds(LANES, LANES), pl.ds(LANES, LANES)] = jnp.zeros((LANES, LANES), BF16)


def put_flux(ft, flux):
    for f in range(flux.shape[0]):
        ft[f] = turned(-0.5 * flux[f])


def edge_windows(dom, xhl, x, from_core, from_chip):
    fields = from_core.shape[0]
    rows = x.shape[0]
    side = 3 * LANES
    xhl[pl.ds(LANES, side), :] = x[pl.ds(0, side), :]
    xhl[pl.ds(4 * LANES, side), :] = x[pl.ds(rows - side, side), :]
    for f in range(fields):
        left, right = take_in(dom, from_core, from_chip, f)
        put_split(xhl, pl.ds(0, LANES), f, fields, left)
        put_split(xhl, pl.ds(7 * LANES, LANES), f, fields, right)


def edge_kernel(
    ocean, dom, elem, base, xt, from_core, from_chip, enbr, coupling, stiffness, metric, vertical, flux,
    o, nbr, diff, sea, overt, held,
    u, to_core, to_chip, fresh,
    table, cx, nt, xhl, hv, wa, mt, ft, ov, ext, res, vert, o_sem, r_sem,
):
    del held
    fields, points = flux.shape[0], flux.shape[1]
    blocks = xt.shape[0] // (2 * LANES)
    sides = enbr.shape[0]

    @pl.when(ocean[0] == 0)
    def _():
        prepare_table(elem, enbr, coupling, stiffness, cx, nt)
        for i in range(2):
            build_table(i * (blocks - 1), table, i, cx, nt, sides, points)
        prepare(metric, vertical, wa, mt)
        put_flux(ft, flux)
        edge_windows(dom, xhl, xt, from_core, from_chip)
        last_lane = lax.broadcasted_iota(jnp.int32, (2 * LANES, LANES), 1) == LANES - 1
        for i in range(2):
            b = i * (blocks - 1)
            element = b * 2 * GROUP

            def store(f, value):
                value = value + jnp.where(last_lane, columns(ft.at[f], element, points), 0.0)
                put_split(u, pl.ds(i * 2 * LANES, 2 * LANES), f, fields, value)
                hv[i, f] = value[:LANES] if i == 0 else value[LANES:]

            advance(
                xhl.at[pl.ds(i * 4 * LANES, 4 * LANES)], table.at[i], wa, mt, element, points, store, range(fields)
            )
        hand_out(dom, hv, to_core, to_chip)

    @pl.when(ocean[0] != 0)
    def _():
        load = pltpu.make_async_copy(o, ov, o_sem.at[0])
        load.start()
        ocean_part(dom, base, load, from_core, from_chip, nbr, diff, sea, overt, fresh, ov, ext, res, vert, r_sem)


def edge_step(
    ocean_flag, dom, elem, base, xt, from_core, from_chip, enbr, coupling, stiffness, metric, vertical, flux,
    ocean, nbr, diff, sea, overt, fresh,
):
    width = xt.shape[1]
    points = stiffness.shape[0]
    sides = enbr.shape[0]
    fields = flux.shape[0]
    olev, cells = ocean.shape[1], ocean.shape[2]
    halo = jax.ShapeDtypeStruct((fields, LANES, LANES), F32)
    return pl.pallas_call(
        edge_kernel,
        out_shape=(
            jax.ShapeDtypeStruct((4 * LANES, width), BF16),
            halo,
            halo,
            jax.ShapeDtypeStruct(ocean.shape, F32),
        ),
        in_specs=[SMEM] * 4 + [VMEM] * 9 + [HBM] + [VMEM] * 4 + [HBM],
        out_specs=(VMEM, VMEM, VMEM, HBM),
        input_output_aliases={18: 3},
        scratch_shapes=[
            pltpu.VMEM((2, 4 * LANES, 4 * LANES), BF16),
            pltpu.VMEM(((sides + 1) * points, LANES), F32),
            pltpu.VMEM((LANES, LANES), F32),
            pltpu.VMEM((8 * LANES, width), BF16),
            pltpu.VMEM((2, fields, LANES, LANES), F32),
            pltpu.VMEM((2 * LANES, 2 * LANES), BF16),
            pltpu.VMEM((LANES, LANES), F32),
            pltpu.VMEM((fields, LANES, LANES), F32),
            pltpu.VMEM(ocean.shape, F32),
            pltpu.VMEM((2, fields * olev, cells + 2 * HALO_O), BF16),
            pltpu.VMEM(ocean.shape, F32),
            pltpu.VMEM(ocean.shape, F32),
            pltpu.SemaphoreType.DMA((1,)),
            pltpu.SemaphoreType.DMA((1,)),
        ],
        compiler_params=params(20),
        cost_estimate=cost(4000000000, 3 << 20),
        name="edge_step",
    )(
        ocean_flag, dom, elem, base, xt, from_core, from_chip, enbr, coupling, stiffness, metric, vertical, flux,
        ocean, nbr, diff, sea, overt, fresh,
    )


def inner_kernel(ocean, elem, xt, ue, enbr, coupling, stiffness, metric, vertical, flux, u, table, cx, nt, wa, mt, ft):
    fields, points = flux.shape[0], flux.shape[1]
    sides = enbr.shape[0]
    rows = xt.shape[0]
    blocks = table.shape[0]
    edge = 2 * LANES

    @pl.when(ocean[0] == 0)
    def _():
        prepare_table(elem, enbr, coupling, stiffness, cx, nt)
        for b in range(2):
            build_table(b, table, b, cx, nt, sides, points)
        prepare(metric, vertical, wa, mt)
        put_flux(ft, flux)
        u[pl.ds(0, edge), :] = ue[pl.ds(0, edge), :]
        u[pl.ds(rows - edge, edge), :] = ue[pl.ds(edge, edge), :]
        last_lane = lax.broadcasted_iota(jnp.int32, (edge, LANES), 1) == LANES - 1

        @pl.loop(1, blocks - 1, step=3)
        def _(start_of):
            for i in range(3):
                b = start_of + i
                first = pl.multiple_of(b * edge, edge)
                element = b * 2 * GROUP

                def store(f, value):
                    value = value + jnp.where(last_lane, columns(ft.at[f], element, points), 0.0)
                    put_split(u, pl.ds(first, edge), f, fields, value)

                window = xt.at[pl.ds(pl.multiple_of(first - LANES, LANES), 4 * LANES)]
                advance(window, table.at[b], wa, mt, element, points, store, range(fields))
                build_table(b + 1, table, b + 1, cx, nt, sides, points)


def ocean_part(dom, base, load, from_core, from_chip, nbr, diff, sea, overt, fresh, ov, ext, res, vert, r_sem):
    fields, olev, cells = ov.shape
    sides = nbr.shape[0]
    for f in range(fields):
        rows = pl.ds(f * olev, olev)
        left, right = take_in(dom, from_core, from_chip, f)
        for at, value in ((0, left[:olev]), (HALO_O + cells, right[:olev])):
            hi, lo = split(value)
            ext[0, rows, pl.ds(at, HALO_O)] = hi
            ext[1, rows, pl.ds(at, HALO_O)] = lo
    vhi, vlo = split(overt[...])
    both = jnp.concatenate([vhi, vlo], axis=0)
    load.wait()
    for f in range(fields):
        rows = pl.ds(f * olev, olev)
        hi, lo = split(ov[f])
        ext[0, rows, pl.ds(HALO_O, cells)] = hi
        ext[1, rows, pl.ds(HALO_O, cells)] = lo
        v = dot(both, hi)
        vert[f] = v[:olev] + v[olev:] + dot(vhi, lo)

    @pl.loop(0, cells // LANES)
    def _(b):
        first = pl.multiple_of(b * LANES, LANES)
        here = pl.ds(first, LANES)
        begin = base[0] + first - HALO_O
        place = lax.broadcasted_iota(jnp.int32, (3 * LANES, LANES), 0)
        table = jnp.zeros((3 * LANES, LANES), F32)
        held = jnp.zeros((1, LANES), F32)
        for k in range(sides):
            d = diff[k, :, here]
            held = held + d
            table = table + jnp.where(place == nbr[k, :, here] - begin, d, 0.0)
        hi, lo = split(table)
        window = pl.ds(first, 3 * LANES)
        heads = dot(ext[0, :, window], jnp.concatenate([hi, lo], axis=1))
        lap = heads[:, :LANES] + heads[:, LANES:] + dot(ext[1, :, window], hi)
        wet = sea[:, here] == 1
        for f in range(fields):
            own = ov[f, :, here]
            new = own + (lap[f * olev : (f + 1) * olev] - held * own) + vert[f, :, here]
            res[f, :, here] = jnp.where(wet, new, own)

    out = pltpu.make_async_copy(res, fresh, r_sem.at[0])
    out.start()
    out.wait()


def inner_step(ocean_flag, elem, xt, ue, enbr, coupling, stiffness, metric, vertical, flux):
    rows, width = xt.shape
    fields, points = flux.shape[0], flux.shape[1]
    sides = enbr.shape[0]
    blocks = rows // (2 * LANES)
    return pl.pallas_call(
        inner_kernel,
        out_shape=(
            jax.ShapeDtypeStruct((rows, width), BF16),
            jax.ShapeDtypeStruct((blocks, 4 * LANES, 4 * LANES), BF16),
        ),
        in_specs=[SMEM, SMEM] + [VMEM] * 8,
        out_specs=(VMEM, VMEM),
        scratch_shapes=[
            pltpu.VMEM(((sides + 1) * points, LANES), F32),
            pltpu.VMEM((LANES, LANES), F32),
            pltpu.VMEM((2 * LANES, 2 * LANES), BF16),
            pltpu.VMEM((LANES, LANES), F32),
            pltpu.VMEM((fields, LANES, LANES), F32),
        ],
        compiler_params=params(12),
        cost_estimate=cost(10_000_000_000, 10 << 20),
        name="inner_step",
    )(ocean_flag, elem, xt, ue, enbr, coupling, stiffness, metric, vertical, flux)


def flux_kernel(ocean, dom, owner, block, source, *refs):
    n_tops = len(refs) - 12
    tops = refs[:n_tops]
    weights, coef, sv, flux, sent, fresh, tv, wcat, surf, fl, zv, z_sem = refs[n_tops:]
    pairs = weights.shape[0]
    points, fields = coef.shape[0], flux.shape[0]
    ocean_blocks = sent.shape[0] // n_tops
    chips = n_tops // 2

    @pl.when(ocean[0] == 0)
    def _():
        zv[...] = jnp.zeros_like(zv)
        zeros = copies([(zv, fresh.at[f]) for f in range(fields)], z_sem)
        start(zeros)
        surf[...] = jnp.zeros_like(surf)
        sent[...] = jnp.zeros_like(sent)
        chip, core = dom[0] // 2, dom[0] % 2

        def doubled(rows):
            hi, lo = split(rows)
            eight = jnp.concatenate([hi.astype(F32), lo.astype(F32)], axis=0).astype(BF16)
            return jnp.concatenate([eight, eight], axis=1)

        @pl.loop(0, pairs, unroll=4)
        def _(r):
            hi, lo = split(weights[r])
            wcat[r, :, pl.ds(0, BLK)] = hi
            wcat[r, :, pl.ds(BLK, BLK)] = lo

        for i in range(n_tops):
            tv[i] = tops[i][...]
        for r in range(pairs):
            at = pl.multiple_of(block[r] * BLK, BLK)
            which = owner[r]
            slot = ((which // 2) ^ chip) + jnp.where(which % 2 == core, 0, chips)
            rows = doubled(tv[slot, :, pl.ds(at, BLK)])
            out = dot_t(rows, wcat[r])
            surf[source[r]] += out[:fields] + out[fields:]

        for p in range(points):
            value = coef[pl.ds(p, 1), :] * (sv[:, p, :] - surf[p])
            fl[p] = value
            flux[:, p, :] = value

        for r in range(pairs):
            rows = doubled(fl[source[r]])
            both = jnp.concatenate([wcat[r, :, pl.ds(0, BLK)], wcat[r, :, pl.ds(BLK, BLK)]], axis=0)
            out = dot(rows, both)
            sent[owner[r] * ocean_blocks + block[r]] += out[:fields] + out[fields:]
        wait(zeros)


def fluxes(ocean_flag, dom, owner, block, source, tops, weights, coef, surface, ocean_shape, ocean_blocks):
    fields, points, elems = surface.shape
    pairs = weights.shape[0]
    n = len(tops)
    return pl.pallas_call(
        flux_kernel,
        out_shape=(
            jax.ShapeDtypeStruct((fields, points, elems), F32),
            jax.ShapeDtypeStruct((n * ocean_blocks, fields, BLK), F32),
            jax.ShapeDtypeStruct(ocean_shape, F32),
        ),
        in_specs=[SMEM] * 5 + [VMEM] * (n + 3),
        out_specs=(VMEM, VMEM, HBM),
        scratch_shapes=[
            pltpu.VMEM((n,) + tops[0].shape, F32),
            pltpu.VMEM((pairs, BLK, 2 * BLK), BF16),
            pltpu.VMEM((points, fields, BLK), F32),
            pltpu.VMEM((points, fields, BLK), F32),
            pltpu.VMEM(ocean_shape[1:], F32),
            pltpu.SemaphoreType.DMA((fields,)),
        ],
        compiler_params=params(8),
        cost_estimate=cost(2_500_000_000, 2 << 20),
        name="fluxes",
    )(ocean_flag, dom, owner, block, source, *tops, weights, coef, surface)


def second_kernel(ocean, dom, u, from_core, from_chip, table, metric, vertical, flux, held, out, xhl, wa, mt, xv, ov, o_sem):
    del held
    fields, points = flux.shape[0], flux.shape[1]
    rows, levels = xv.shape[1], xv.shape[2]
    blocks = table.shape[0]
    edge = 2 * LANES

    @pl.when(ocean[0] == 0)
    def _():
        prepare(metric, vertical, wa, mt)
        edge_windows(dom, xhl, u, from_core, from_chip)

        def step(b, window):
            first = b * edge if isinstance(b, int) else pl.multiple_of(b * edge, edge)

            def store(f, value):
                xv[f, pl.ds(first, edge), :] = value

            advance(window, table.at[b], wa, mt, b * 2 * GROUP, points, store, range(fields))

        @pl.loop(1, blocks - 1, step=3)
        def _(start_of):
            for i in range(3):
                b = start_of + i
                step(b, u.at[pl.ds(pl.multiple_of(b * edge - LANES, LANES), 4 * LANES)])

        step(0, xhl.at[pl.ds(0, 4 * LANES)])
        step(blocks - 1, xhl.at[pl.ds(4 * LANES, 4 * LANES)])
        outs = copies([(ov.at[f], out.at[f]) for f in range(fields)], o_sem)
        for f in range(fields):
            for p in range(points):
                cols = [xv[f, pl.ds(g * LANES + p * GROUP, GROUP), :] for g in range(LANES // GROUP)]
                ov[f, pl.ds(p, LANES, stride=points), :] = jnp.concatenate(cols, axis=0).T
            last = pl.ds((levels - 1) * points, points)
            ov[f, last, :] = ov[f, last, :] - 0.5 * flux[f]
            outs[f].start()
        wait(outs)


def second_step(ocean_flag, dom, u, from_core, from_chip, table, metric, vertical, flux, zeroed, levels):
    fields, points = flux.shape[0], flux.shape[1]
    rows, width = u.shape
    return pl.pallas_call(
        second_kernel,
        out_shape=jax.ShapeDtypeStruct((fields, levels * points, LANES), F32),
        in_specs=[SMEM, SMEM] + [VMEM] * 7 + [HBM],
        out_specs=HBM,
        input_output_aliases={9: 0},
        scratch_shapes=[
            pltpu.VMEM((8 * LANES, width), BF16),
            pltpu.VMEM((2 * LANES, 2 * LANES), BF16),
            pltpu.VMEM((LANES, LANES), F32),
            pltpu.VMEM((fields, rows, levels), F32),
            pltpu.VMEM((fields, levels * points, LANES), F32),
            pltpu.SemaphoreType.DMA((fields,)),
        ],
        compiler_params=params(20),
        cost_estimate=cost(10000000000, 12 << 20),
        name="second_step",
    )(ocean_flag, dom, u, from_core, from_chip, table, metric, vertical, flux, zeroed)


def blank_kernel(out):
    del out


def blank(shape):
    return pl.pallas_call(
        blank_kernel, out_shape=jax.ShapeDtypeStruct(shape, F32), out_specs=HBM, compiler_params=params(4), cost_estimate=cost(0, 1024), name="blank"
    )()


def top_kernel(ocean, o, top, tv, sem):
    fields = top.shape[0]

    @pl.when(ocean[0] != 0)
    def _():
        loads = copies([(o.at[f, pl.ds(0, 8)], tv.at[f]) for f in range(fields)], sem)
        start(loads)
        wait(loads)
        for f in range(fields):
            top[pl.ds(f, 1), :] = tv[f, pl.ds(0, 1), :]


def top_rows(ocean_flag, ocean):
    fields, olev, cells = ocean.shape
    return pl.pallas_call(
        top_kernel,
        out_shape=jax.ShapeDtypeStruct((fields, cells), F32),
        in_specs=[SMEM, ANY],
        out_specs=VMEM,
        scratch_shapes=[pltpu.VMEM((fields, 8, cells), F32), pltpu.SemaphoreType.DMA((fields,))],
        compiler_params=params(TURN),
        cost_estimate=cost(0, 1 << 16),
        name="top_rows",
    )(ocean_flag, ocean)


def gather_kernel(dom, *refs):
    parts, (keep, give) = refs[:-2], refs[-2:]
    half, per = keep.shape[0], keep.shape[1]
    for core, out in ((0, keep), (1, give)):
        for s in range(half):
            at = pl.ds((dom[0] ^ (2 * s + core)) * per, per)
            total = parts[0][at]
            for part in parts[1:]:
                total = total + part[at]
            out[s] = total


def gather_sent(dom, parts, n_dom):
    total, fields, blk = parts[0].shape
    shape = jax.ShapeDtypeStruct((n_dom // 2, total // n_dom, fields, blk), F32)
    return pl.pallas_call(
        gather_kernel,
        out_shape=(shape, shape),
        in_specs=[SMEM] + [VMEM] * len(parts),
        out_specs=(VMEM, VMEM),
        compiler_params=params(6),
        name="gather_sent",
    )(dom, *parts)


def pair_kernel(same, other, *outs):
    for s, out in enumerate(outs):
        out[...] = same[s] + other[s]


def pair_sums(same, other):
    chips = same.shape[0]
    return pl.pallas_call(
        pair_kernel,
        out_shape=(jax.ShapeDtypeStruct(same.shape[1:], F32),) * chips,
        in_specs=[VMEM, VMEM],
        out_specs=(VMEM,) * chips,
        compiler_params=params(4),
        cost_estimate=cost(0, 1 << 16),
        name="pair_sums",
    )(same, other)


def add_kernel(*refs):
    parts, out = refs[:-1], refs[-1]
    total = parts[0][...]
    for part in parts[1:]:
        total = total + part[...]
    out[...] = total


def add_up(parts):
    return pl.pallas_call(
        add_kernel,
        out_shape=jax.ShapeDtypeStruct(parts[0].shape, F32),
        in_specs=[VMEM] * len(parts),
        out_specs=VMEM,
        compiler_params=params(4),
        cost_estimate=cost(0, 1 << 16),
        name="add_up",
    )(*parts)


def finish_kernel(ocean, fresh, sea, total, out, sv, pv, rows_v, in_sem, out_sem):
    del fresh
    fields, cells = rows_v.shape[0], rows_v.shape[2]

    @pl.when(ocean[0] != 0)
    def _():
        loads = copies([(out.at[f, pl.ds(0, 8)], rows_v.at[f]) for f in range(fields)] + [(total, pv), (sea, sv)], in_sem)
        start(loads)
        wait(loads)
        for b in range(cells // BLK):
            here = pl.ds(b * BLK, BLK)
            part = jnp.where(sv[:, here] == 1, 0.5 * pv[b], 0.0)
            for f in range(fields):
                rows_v[f, pl.ds(0, 1), here] = rows_v[f, pl.ds(0, 1), here] + part[f : f + 1]
        stores = copies([(rows_v.at[f], out.at[f, pl.ds(0, 8)]) for f in range(fields)], out_sem)
        start(stores)
        wait(stores)


def finish(ocean_flag, fresh, total, sea):
    fields, olev, cells = fresh.shape
    return pl.pallas_call(
        finish_kernel,
        out_shape=jax.ShapeDtypeStruct(fresh.shape, F32),
        in_specs=[SMEM, HBM, ANY, ANY],
        out_specs=HBM,
        input_output_aliases={1: 0},
        scratch_shapes=[
            pltpu.VMEM(sea.shape, jnp.int32),
            pltpu.VMEM(total.shape, F32),
            pltpu.VMEM((fields, 8, cells), F32),
            pltpu.SemaphoreType.DMA((fields + 2,)),
            pltpu.SemaphoreType.DMA((fields,)),
        ],
        compiler_params=params(8),
        cost_estimate=cost(0, 1 << 16),
        name="finish_ocean",
    )(ocean_flag, fresh, sea, total)


def local(
    atm_state,
    elem_nbr,
    elem_metric,
    bulk_coef,
    stiffness,
    coupling,
    atm_vertical,
    ocean_state,
    cell_nbr,
    cell_diff,
    ocean_vertical,
    sea_mask,
    pair_owner,
    pair_block,
    pair_src,
    remap_weight,
):
    n_comp = lax.axis_size("comp")
    n_dom = lax.axis_size("dom")
    comp_index = lax.axis_index("comp")
    dom_index = lax.axis_index("dom")
    live = n_comp - 1
    chips = n_dom // 2
    state = atm_state[0]
    ocean = ocean_state[0]
    fields, levels, points, elems = state.shape
    cells = ocean.shape[2]
    ocean_blocks = cells // BLK
    one = lambda value: value.astype(jnp.int32).reshape(1)
    flag = one(comp_index == live)
    comp = one(comp_index)
    dom = one(dom_index)
    elem_base = one((comp_index * n_dom + dom_index) * elems)
    cell_base = one(dom_index * cells)

    both = ("comp", "dom")
    swapped = [(d, d ^ 1) for d in range(n_dom)]
    between = [(i, i + 1) for i in range(1, live * n_dom - 1, 2)]
    atm_chips = between + [(j, i) for i, j in between]
    between = [(live * n_dom + i, live * n_dom + i + 1) for i in range(1, n_dom - 1, 2)]
    all_chips = atm_chips + between + [(j, i) for i, j in between]

    def from_ocean(c):
        return [(live * n_dom + d, c * n_dom + d) for d in range(n_dom)]

    def to_ocean(c):
        return [(j, i) for i, j in from_ocean(c)]

    def among_ocean(pairs):
        return [(live * n_dom + a, live * n_dom + b) for a, b in pairs]

    is_ocean = comp_index == live
    chips = n_dom // 2

    def shifted(by):
        return [(d, d ^ (2 * by)) for d in range(n_dom)]

    top = top_rows(flag, ocean)
    brought = [lax.ppermute(top, both, from_ocean(c)) for c in range(live)]
    xt, to_core, to_chip, surface, zeroed = turn(flag, dom, state, ocean)
    brought, to_core, to_chip = lax.optimization_barrier((brought, to_core, to_chip))
    got = sum(brought)
    got, to_core, to_chip = lax.optimization_barrier((got, to_core, to_chip))
    near = [got] + [lax.ppermute(got, "dom", shifted(s)) for s in range(1, chips)]
    tops = near + [lax.ppermute(part, "dom", swapped) for part in near]
    from_core = lax.ppermute(to_core, "dom", swapped)
    from_chip = lax.ppermute(to_chip, both, all_chips)
    metric = elem_metric[0]

    operators = (elem_nbr[0], coupling.reshape(-1, points), stiffness, metric, atm_vertical)
    flux, sent, fresh = fluxes(
        flag,
        dom,
        pair_owner[0, :, 0],
        pair_block[0],
        pair_src[0],
        tops,
        remap_weight[0],
        bulk_coef[0],
        surface,
        ocean.shape,
        ocean_blocks,
    )
    parts = [lax.ppermute(sent, both, to_ocean(c)) for c in range(live)]
    ue, to_core, to_chip, fresh = edge_step(
        flag,
        dom,
        elem_base,
        cell_base,
        xt,
        from_core,
        from_chip,
        *operators,
        flux,
        ocean,
        cell_nbr[0][:, None],
        cell_diff[0][:, None],
        sea_mask,
        ocean_vertical,
        fresh,
    )
    from_chip2 = lax.ppermute(to_chip, both, atm_chips)
    from_core2 = lax.ppermute(to_core, "dom", swapped)
    u, table = inner_step(flag, elem_base, xt, ue, *operators, flux)
    atm_next = second_step(flag, dom, u, from_core2, from_chip2, table, metric, atm_vertical, flux, zeroed, levels)

    parts, atm_next = lax.optimization_barrier((parts, atm_next))

    def reduce_parts():
        same, other = gather_sent(dom, parts, n_dom)
        pieces = pair_sums(same, lax.ppermute(other, both, among_ocean(swapped)))
        mine = [pieces[0]]
        for s in range(1, chips):
            mine.append(lax.ppermute(pieces[s], both, among_ocean(shifted(s))))
        return add_up(mine)

    total = lax.cond(is_ocean, reduce_parts, lambda: blank((ocean_blocks, fields, BLK)))
    ocean_next = finish(flag, fresh, total, sea_mask)
    return (atm_next.reshape(state.shape)[None], ocean_next[None])


def solution(mesh):
    in_specs = (
        P("comp", None, None, None, "dom"),
        P("comp", None, "dom"),
        P("comp", None, "dom"),
        P("comp", None, "dom"),
        P(),
        P(),
        P(),
        P("comp", None, None, "dom"),
        P("comp", None, "dom"),
        P("comp", None, "dom"),
        P(),
        P("comp", "dom"),
        P("comp", "dom", None),
        P("comp", "dom"),
        P("comp", "dom"),
        P("comp", "dom", None, None),
    )
    out_specs = (P("comp", None, None, None, "dom"), P("comp", None, None, "dom"))
    return jax.shard_map(local, mesh=mesh, in_specs=in_specs, out_specs=out_specs, check_vma=False)
```

time: 55.3 us -> 52 us (0.940)
  Pallas kernels: 26 us -> 23.6 us
  starting transfers between devices: 22.7 us -> 20.7 us
  waiting for transfers between devices: 3.97 us -> 4.77 us
    pallas_call x3 -> x2, Pallas kernels: 3.9 us -> 0.64 us  [the longest x1 0.64 us: top_rows(): pl.pallas_call(top_kernel, out_shape=jax.ShapeDtypeStruct((fields, cells)...]
    ppermute x1, waiting for transfers between devices: 0.01 us -> 3.15 us  [local(): from_chip2 = lax.ppermute(to_chip, both, atm_chips)]
    ppermute x4 -> x0, starting transfers between devices: 2.65 us -> none  [the longest x3 1.99 us: local(): lax.ppermute(pieces[s], both, among_ocean(shifted(s)))]
    ppermute x1, waiting for transfers between devices: 2.21 us -> 0.01 us  [local(): from_chip = lax.ppermute(to_chip, both, all_chips)]
    ppermute x3, waiting for transfers between devices: 1.56 us -> 0.01 us  [local(): lax.ppermute(got, 'dom', shifted(s))]
    pallas_call x1, Pallas kernels: 4.81 us -> 5.75 us  [inner_step(): pl.pallas_call(inner_kernel, out_shape=(jax.ShapeDtypeStruct((rows, width...]
    ppermute x4, waiting for transfers between devices: 0.16 us -> 1.1 us  [local(): tops = near + [lax.ppermute(part, 'dom', swapped) for part in near]]
    ppermute x1, starting transfers between devices: 4.57 us -> 5.5 us  [local(): from_chip = lax.ppermute(to_chip, both, all_chips)]
  transfers between devices with their start and end apart: 21 -> 17, of which waited for: 3 -> 5; matrix products, arithmetic and copies ran while one was open for 0% -> 0% of each run, Pallas kernels for 32% -> 45%
where the time goes in v3:
time: 52 us; the launch traced here: 51.2 us
  Pallas kernels  23.6 us (45%)
  starting transfers between devices  20.7 us (40%)
  waiting for transfers between devices  4.77 us (9%)
  between operations  1.24 us (2%)
  local copies, waits for them, and re-layouts  0.83 us (2%)
    pallas_call x1, Pallas kernels, second_step(): pl.pallas_call(second_kernel, out_shape=jax.ShapeDtypeStruct((fields, lev...  8.03 us
    pallas_call x1, Pallas kernels, inner_step(): pl.pallas_call(inner_kernel, out_shape=(jax.ShapeDtypeStruct((rows, width...  5.75 us
    ppermute x1, starting transfers between devices, local(): from_chip = lax.ppermute(to_chip, both, all_chips)  5.5 us
    pallas_call x1, Pallas kernels, turn(): pl.pallas_call(turn_kernel, out_shape=(jax.ShapeDtypeStruct((rows, 2 * fi...  5.07 us
    ppermute x3, starting transfers between devices, local(): lax.ppermute(got, 'dom', shifted(s))  4.45 us
    ppermute x3, starting transfers between devices, local(): parts = [lax.ppermute(sent, both, to_ocean(c)) for c in range(live)]  3.51 us
    ppermute x1, starting transfers between devices, local(): from_chip2 = lax.ppermute(to_chip, both, atm_chips)  3.37 us
    ppermute x1, waiting for transfers between devices, local(): from_chip2 = lax.ppermute(to_chip, both, atm_chips)  3.15 us
  transfers between devices with their start and end apart: 17, of which 5 were waited for; matrix products, arithmetic and copies ran while one was open for 0% of the time, Pallas kernels for 45%

profile of v3, /device:TPU:4, one launch (start us, length us, event | category | flops | bytes accessed | tf_op | source)
XLA Modules:
  0.0 51.2 jit_solution(1434656319822542066)
XLA Ops:
  0.6 0.0 copy-start.2
  0.7 0.0 copy-start.8
  0.7 0.0 copy-start.12
  0.7 0.0 copy-start.13
  0.7 0.0 copy-start.14
  0.7 0.6 %top_rows.1 = f32[4,1024]{1,0:T(4,128)} custom-call(s32[1]{0:T(128)} %bitcast.ocean, f32[4,80,1024]{2,1,0:T(8,128)} %bitcast.18), custom_call_target="tpu_custom_call" | custom-call | bytes 65536 | tf_op jit(solution)/shard_map/top_rows/pallas_call | solution.py:629
  1.3 0.7 %collective-permute-start.4 = (f32[4,1024]{1,0:T(4,128)}, f32[4,1024]{1,0:T(4,128)S(1)}, u32[]{:S(2)}, u32[]{:S(2)}) collective-permute-start(f32[4,1024]{1,0:T(4,128)} %top_rows.1), channel_id=1, source_target_pairs={{24,0},{25,1},{26,2},{27,3},{28,4},{29,5},{30,6},{31,7}} | collective-permute-start | bytes 49160 | tf_op jit(solution)/shard_map/ppermute | solution.py:803
  2.0 0.7 %collective-permute-start.5 = (f32[4,1024]{1,0:T(4,128)}, f32[4,1024]{1,0:T(4,128)S(1)}, u32[]{:S(2)}, u32[]{:S(2)}) collective-permute-start(f32[4,1024]{1,0:T(4,128)} %top_rows.1), channel_id=1, source_target_pairs={{24,8},{25,9},{26,10},{27,11},{28,12},{29,13},{30,14},{31,15}} | collective-permute-start | bytes 49160 | tf_op jit(solution)/shard_map/ppermute | solution.py:803
  2.7 1.3 %collective-permute-start.6 = (f32[4,1024]{1,0:T(4,128)}, f32[4,1024]{1,0:T(4,128)S(1)}, u32[]{:S(2)}, u32[]{:S(2)}) collective-permute-start(f32[4,1024]{1,0:T(4,128)} %top_rows.1), channel_id=1, source_target_pairs={{24,16},{25,17},{26,18},{27,19},{28,20},{29,21},{30,22},{31,23}} | collective-permute-start | bytes 49160 | tf_op jit(solution)/shard_map/ppermute | solution.py:803
  4.0 5.1 %turn_state.1 = (bf16[2048,1024]{1,0:T(8,128)(2,1)}, f32[4,128,128]{2,1,0:T(8,128)}, f32[4,128,128]{2,1,0:T(8,128)}, f32[4,16,128]{2,1,0:T(8,128)}, f32[4,2048,128]{2,1,0:T(8,128)}) custom-call(s32[1]{0:T(128)} %bitcast.ocean, s32[1]{0:T(128)} %bitcast.1.dom, f32[4,2048,128]{2,1,0:T(8,128)} %bitcast.36, f32[4,80,1024]{2,1,0:T(8,128)} %bitcast.19), custom_call_target="tpu_custom_call" | custom-call | flops 2000000000 | bytes 9437184 | tf_op jit(solution)/shard_map/turn_state/pallas_call | solution.py:136
  9.1 0.0 collective-permute-done.4
  9.1 0.0 collective-permute-done.5
  9.1 0.5 collective-permute-done.6
  9.6 1.8 %collective-permute-start.7 = (f32[4,1024]{1,0:T(4,128)S(1)}, f32[4,1024]{1,0:T(4,128)S(1)}, u32[]{:S(2)}, u32[]{:S(2)}) collective-permute-start(f32[4,1024]{1,0:T(4,128)S(1)} %add_add_fusion.refs_0_), channel_id=1, source_target_pairs={{0,2},{1,3},{2,0},{3,1},{4,6},{5,7},{6,4},{7,5},{8,10},{9,11},{10,... | collective-permute-start | bytes 49160 | tf_op jit(solution)/shard_map/ppermute | solution.py:808
  11.4 2.6 %collective-permute-start.8 = (f32[4,1024]{1,0:T(4,128)S(1)}, f32[4,1024]{1,0:T(4,128)S(1)}, u32[]{:S(2)}, u32[]{:S(2)}) collective-permute-start(f32[4,1024]{1,0:T(4,128)S(1)} %add_add_fusion.refs_0_), channel_id=1, source_target_pairs={{0,4},{1,5},{2,6},{3,7},{4,0},{5,1},{6,2},{7,3},{8,12},{9,13},{10,... | collective-permute-start | bytes 49160 | tf_op jit(solution)/shard_map/ppermute | solution.py:808
  14.0 0.1 collective-permute-start.9
  14.0 0.0 collective-permute-start.10
  14.0 0.5 collective-permute-start.17
  14.6 0.0 collective-permute-done.7.refs_1_
  14.6 5.5 %collective-permute-start.18 = (f32[4,128,128]{2,1,0:T(8,128)}, f32[4,128,128]{2,1,0:T(8,128)S(1)}, u32[]{:S(2)}, u32[]{:S(2)}) collective-permute-start(f32[4,128,128]{2,1,0:T(8,128)} %get-tuple-element.61), channel_id=1, source_target_pairs={{1,2},{3,4},{5,6},{7,8},{9,10},{11,12},{13,14},{15,16},{17,18},{19... | collective-permute-start | bytes 786440 | tf_op jit(solution)/shard_map/ppermute | solution.py:811
  20.1 0.0 collective-permute-done.8.refs_2_
  20.1 0.1 collective-permute-start.11
  20.2 0.0 collective-permute-done.9.refs_3_
  20.2 0.5 collective-permute-start.12
  20.7 0.0 collective-permute-done.10.refs_4_
  20.7 0.1 collective-permute-start.13
  20.7 0.6 %collective-permute-done.11.refs_5_ = f32[4,1024]{1,0:T(4,128)S(1)} collective-permute-done((f32[4,1024]{1,0:T(4,128)S(1)}, f32[4,1024]{1,0:T(4,128)S(1)}, u32[]{:S(2)}, u32[]{:S(2)}) %collective-permute-start.11) | collective-permute-done | bytes 16416 | tf_op jit(solution)/shard_map/ppermute | solution.py:809
  21.3 0.2 collective-permute-done.12.refs_6_
  21.5 0.3 collective-permute-done.13.refs_7_
  21.8 0.0 copy-done.2
  21.8 0.0 copy-done.8
  21.9 0.0 copy-done.12
  21.9 0.0 copy-done.13
  21.9 0.0 copy-done.14
  21.9 0.0 copy-start.16
  21.9 0.7 %copy-done.16 = f32[4,16,128]{2,1,0:T(8,128)S(1)} copy-done((f32[4,16,128]{2,1,0:T(8,128)S(1)}, f32[4,16,128]{2,1,0:T(8,128)}, u32[]{:S(2)}) %copy-start.16) | copy-done | bytes 32792
  22.6 0.0 copy-start.5
  22.7 0.0 copy-start.6
  22.7 0.0 copy-start.7
  22.7 0.0 copy-start.9
  22.7 0.0 copy-start.10
  22.7 0.0 copy-start.11
  22.7 0.0 copy-start.15
  22.7 2.1 %fluxes.1 = (f32[4,16,128]{2,1,0:T(8,128)S(1)}, f32[64,4,128]{2,1,0:T(4,128)S(1)}, f32[4,80,1024]{2,1,0:T(8,128)}) custom-call(s32[1]{0:T(128)} %bitcast.ocean, s32[1]{0:T(128)} %bitcast.1.dom, s32[32]{0:T(128)S(1)} %bitcast.32, s32[32]{0:T(128)S(1)} %bitcast.33, s32[32]{0:T(128)S(1)} %bitcast.34, f32[4,1024]{1,0:T(4,128)S(1)} %add_add_fusion.refs_0_, ...), custom_call_target="tpu_custom_call" | custom-call | flops 2500000000 | bytes 2097152 | tf_op jit(solution)/shard_map/fluxes/pallas_call | solution.py:520
  24.8 0.7 %collective-permute-start.14 = (f32[64,4,128]{2,1,0:T(4,128)S(1)}, f32[64,4,128]{2,1,0:T(4,128)S(1)}, u32[]{:S(2)}, u32[]{:S(2)}) collective-permute-start(f32[64,4,128]{2,1,0:T(4,128)S(1)} %get-tuple-element.58), channel_id=1, source_target_pairs={{0,24},{1,25},{2,26},{3,27},{4,28},{5,29},{6,30},{7,31}} | collective-permute-start | bytes 393224 | tf_op jit(solution)/shard_map/ppermute | solution.py:828
  25.5 0.7 %collective-permute-start.15 = (f32[64,4,128]{2,1,0:T(4,128)S(1)}, f32[64,4,128]{2,1,0:T(4,128)S(1)}, u32[]{:S(2)}, u32[]{:S(2)}) collective-permute-start(f32[64,4,128]{2,1,0:T(4,128)S(1)} %get-tuple-element.58), channel_id=1, source_target_pairs={{8,24},{9,25},{10,26},{11,27},{12,28},{13,29},{14,30},{15,31}} | collective-permute-start | bytes 393224 | tf_op jit(solution)/shard_map/ppermute | solution.py:828
  26.2 2.2 %collective-permute-start.16 = (f32[64,4,128]{2,1,0:T(4,128)S(1)}, f32[64,4,128]{2,1,0:T(4,128)S(1)}, u32[]{:S(2)}, u32[]{:S(2)}) collective-permute-start(f32[64,4,128]{2,1,0:T(4,128)S(1)} %get-tuple-element.58), channel_id=1, source_target_pairs={{16,24},{17,25},{18,26},{19,27},{20,28},{21,29},{22,30},{23,31}} | collective-permute-start | bytes 393224 | tf_op jit(solution)/shard_map/ppermute | solution.py:828
  28.4 0.0 collective-permute-done.17.from_core
  28.4 0.0 collective-permute-done.18.from_chip
  28.4 0.0 copy-done
  28.4 0.0 copy-done.1
  28.4 0.0 copy-done.3
  28.4 0.0 copy-done.4
  28.5 1.9 %edge_step.1 = (bf16[512,1024]{1,0:T(8,128)(2,1)S(1)}, f32[4,128,128]{2,1,0:T(8,128)S(1)}, f32[4,128,128]{2,1,0:T(8,128)S(1)}, f32[4,80,1024]{2,1,0:T(8,128)}) custom-call(s32[1]{0:T(128)} %bitcast.ocean, s32[1]{0:T(128)} %bitcast.1.dom, s32[1]{0:T(128)} %bitcast.9.elem, s32[1]{0:T(128)} %bitcast.10.base, ...), custom_call_target="tpu_custom_call", output_to_operand_aliasing={{3}: (18, {})} | custom-call | flops 4000000000 | bytes 3145728 | tf_op jit(solution)/shard_map/edge_step/pallas_call | solution.py:320
  30.4 0.1 collective-permute-start.19
  30.6 3.4 %collective-permute-start.20 = (f32[4,128,128]{2,1,0:T(8,128)S(1)}, f32[4,128,128]{2,1,0:T(8,128)S(1)}, u32[]{:S(2)}, u32[]{:S(2)}) collective-permute-start(f32[4,128,128]{2,1,0:T(8,128)S(1)} %get-tuple-element.67), channel_id=1, source_target_pairs={{1,2},{3,4},{5,6},{7,8},{9,10},{11,12},{13,14},{15,16},{17,18},{19... | collective-permute-start | bytes 786440 | tf_op jit(solution)/shard_map/ppermute | solution.py:846
  33.9 5.7 %inner_step.1 = (bf16[2048,1024]{1,0:T(8,128)(2,1)S(1)}, bf16[8,512,512]{2,1,0:T(8,128)(2,1)S(1)}) custom-call(s32[1]{0:T(128)} %bitcast.ocean, s32[1]{0:T(128)} %bitcast.9.elem, bf16[2048,1024]{1,0:T(8,128)(2,1)S(1)} %copy-done.15, bf16[512,1024]{1,0:T(8,128)(2,1)S(1)} %get-tuple-element.64.ue, s32[4,128]{1,0:T(4,128)S(1)} %bitcast.31, ...), custom_call_target="tpu_custom_call" | custom-call | flops 10000000000 | bytes 10485760 | tf_op jit(solution)/shard_map/inner_step/pallas_call | solution.py:443
  39.7 0.0 collective-permute-done.19.from_core
  39.7 3.1 %collective-permute-done.20.from_chip = f32[4,128,128]{2,1,0:T(8,128)S(1)} collective-permute-done((f32[4,128,128]{2,1,0:T(8,128)S(1)}, f32[4,128,128]{2,1,0:T(8,128)S(1)}, u32[]{:S(2)}, u32[]{:S(2)}) %collective-permute-start.20) | collective-permute-done | bytes 262176 | tf_op jit(solution)/shard_map/ppermute | solution.py:846
  42.9 8.0 %second_step.1 = f32[4,2048,128]{2,1,0:T(8,128)} custom-call(s32[1]{0:T(128)} %bitcast.ocean, s32[1]{0:T(128)} %bitcast.1.dom, bf16[2048,1024]{1,0:T(8,128)(2,1)S(1)} %get-tuple-element.65.u, f32[4,128,128]{2,1,0:T(8,128)S(1)} %collective-permute-done.19.from_core, ...), custom_call_target="tpu_custom_call", output_to_operand_aliasing={{}: (9, {})} | custom-call | flops 10000000000 | bytes 12582912 | tf_op jit(solution)/shard_map/second_step/pallas_call | solution.py:585
  50.9 0.0 collective-permute-done.14
  50.9 0.0 collective-permute-done.15
  50.9 0.0 collective-permute-done.16
  51.0 0.1 finish_ocean.1
  (14 shorter events, 0.1 us)
Async XLA Ops:
  0.6 21.2 %copy-start.2 = (f32[1,32,128,128]{3,2,1,0:T(8,128)S(1)}, f32[1,32,128,128]{3,2,1,0:T(8,128)}, u32[]{:S(2)}) copy-start(f32[1,32,128,128]{3,2,1,0:T(8,128)} %param.33) | copy-start | bytes 6291460
  0.7 21.2 %copy-start.8 = (f32[1,16,128]{2,1,0:T(8,128)S(1)}, f32[1,16,128]{2,1,0:T(8,128)}, u32[]{:S(2)}) copy-start(f32[1,16,128]{2,1,0:T(8,128)} %param.21) | copy-start | bytes 24580
  0.7 21.2 %copy-start.12 = (s32[1,32,1]{1,2,0:T(1,128)S(1)}, s32[1,32,1]{1,2,0:T(1,128)}, u32[]{:S(2)}) copy-start(s32[1,32,1]{1,2,0:T(1,128)} %param.30) | copy-start | bytes 388
  0.7 21.2 %copy-start.13 = (s32[1,32]{1,0:T(1,128)S(1)}, s32[1,32]{1,0:T(1,128)}, u32[]{:S(2)}) copy-start(s32[1,32]{1,0:T(1,128)} %param.31) | copy-start | bytes 388
  0.7 21.2 %copy-start.14 = (s32[1,32]{1,0:T(1,128)S(1)}, s32[1,32]{1,0:T(1,128)}, u32[]{:S(2)}) copy-start(s32[1,32]{1,0:T(1,128)} %param.32) | copy-start | bytes 388
  1.3 7.7 %collective-permute-start.4 = (f32[4,1024]{1,0:T(4,128)}, f32[4,1024]{1,0:T(4,128)S(1)}, u32[]{:S(2)}, u32[]{:S(2)}) collective-permute-start(f32[4,1024]{1,0:T(4,128)} %top_rows.1), channel_id=1, source_target_pairs={{24,0},{25,1},{26,2},{27,3},{28,4},{29,5},{30,6},{31,7}} | collective-permute-start | bytes 49160 | tf_op jit(solution)/shard_map/ppermute | solution.py:803
  2.0 7.1 %collective-permute-start.5 = (f32[4,1024]{1,0:T(4,128)}, f32[4,1024]{1,0:T(4,128)S(1)}, u32[]{:S(2)}, u32[]{:S(2)}) collective-permute-start(f32[4,1024]{1,0:T(4,128)} %top_rows.1), channel_id=1, source_target_pairs={{24,8},{25,9},{26,10},{27,11},{28,12},{29,13},{30,14},{31,15}} | collective-permute-start | bytes 49160 | tf_op jit(solution)/shard_map/ppermute | solution.py:803
  2.7 6.9 %collective-permute-start.6 = (f32[4,1024]{1,0:T(4,128)}, f32[4,1024]{1,0:T(4,128)S(1)}, u32[]{:S(2)}, u32[]{:S(2)}) collective-permute-start(f32[4,1024]{1,0:T(4,128)} %top_rows.1), channel_id=1, source_target_pairs={{24,16},{25,17},{26,18},{27,19},{28,20},{29,21},{30,22},{31,23}} | collective-permute-start | bytes 49160 | tf_op jit(solution)/shard_map/ppermute | solution.py:803
  9.6 5.0 %collective-permute-start.7 = (f32[4,1024]{1,0:T(4,128)S(1)}, f32[4,1024]{1,0:T(4,128)S(1)}, u32[]{:S(2)}, u32[]{:S(2)}) collective-permute-start(f32[4,1024]{1,0:T(4,128)S(1)} %add_add_fusion.refs_0_), channel_id=1, source_target_pairs={{0,2},{1,3},{2,0},{3,1},{4,6},{5,7},{6,4},{7,5},{8,10},{9,11},{10,... | collective-permute-start | bytes 49160 | tf_op jit(solution)/shard_map/ppermute | solution.py:808
  11.4 8.7 %collective-permute-start.8 = (f32[4,1024]{1,0:T(4,128)S(1)}, f32[4,1024]{1,0:T(4,128)S(1)}, u32[]{:S(2)}, u32[]{:S(2)}) collective-permute-start(f32[4,1024]{1,0:T(4,128)S(1)} %add_add_fusion.refs_0_), channel_id=1, source_target_pairs={{0,4},{1,5},{2,6},{3,7},{4,0},{5,1},{6,2},{7,3},{8,12},{9,13},{10,... | collective-permute-start | bytes 49160 | tf_op jit(solution)/shard_map/ppermute | solution.py:808
  14.0 6.2 %collective-permute-start.9 = (f32[4,1024]{1,0:T(4,128)S(1)}, f32[4,1024]{1,0:T(4,128)S(1)}, u32[]{:S(2)}, u32[]{:S(2)}) collective-permute-start(f32[4,1024]{1,0:T(4,128)S(1)} %add_add_fusion.refs_0_), channel_id=1, source_target_pairs={{0,6},{1,7},{2,4},{3,5},{4,2},{5,3},{6,0},{7,1},{8,14},{9,15},{10,... | collective-permute-start | bytes 49160 | tf_op jit(solution)/shard_map/ppermute | solution.py:808
  14.0 6.6 %collective-permute-start.10 = (f32[4,1024]{1,0:T(4,128)S(1)}, f32[4,1024]{1,0:T(4,128)S(1)}, u32[]{:S(2)}, u32[]{:S(2)}) collective-permute-start(f32[4,1024]{1,0:T(4,128)S(1)} %add_add_fusion.refs_0_), channel_id=1, source_target_pairs={{0,1},{1,0},{2,3},{3,2},{4,5},{5,4},{6,7},{7,6},{8,9},{9,8},{10,11... | collective-permute-start | bytes 49160 | tf_op jit(solution)/shard_map/ppermute | solution.py:809
  14.0 14.3 %collective-permute-start.17 = (f32[4,128,128]{2,1,0:T(8,128)}, f32[4,128,128]{2,1,0:T(8,128)S(1)}, u32[]{:S(2)}, u32[]{:S(2)}) collective-permute-start(f32[4,128,128]{2,1,0:T(8,128)} %get-tuple-element.60), channel_id=1, source_target_pairs={{0,1},{1,0},{2,3},{3,2},{4,5},{5,4},{6,7},{7,6},{8,9},{9,8},{10,11... | collective-permute-start | bytes 786440 | tf_op jit(solution)/shard_map/ppermute | solution.py:810
  14.6 13.8 %collective-permute-start.18 = (f32[4,128,128]{2,1,0:T(8,128)}, f32[4,128,128]{2,1,0:T(8,128)S(1)}, u32[]{:S(2)}, u32[]{:S(2)}) collective-permute-start(f32[4,128,128]{2,1,0:T(8,128)} %get-tuple-element.61), channel_id=1, source_target_pairs={{1,2},{3,4},{5,6},{7,8},{9,10},{11,12},{13,14},{15,16},{17,18},{19... | collective-permute-start | bytes 786440 | tf_op jit(solution)/shard_map/ppermute | solution.py:811
  20.1 1.2 %collective-permute-start.11 = (f32[4,1024]{1,0:T(4,128)S(1)}, f32[4,1024]{1,0:T(4,128)S(1)}, u32[]{:S(2)}, u32[]{:S(2)}) collective-permute-start(f32[4,1024]{1,0:T(4,128)S(1)} %collective-permute-done.7.refs_1_), channel_id=1, source_target_pairs={{0,1},{1,0},{2,3},{3,2},{4,5},{5,4},{6,7},{7,6},{8,9},{9,8},{10,11... | collective-permute-start | bytes 49160 | tf_op jit(solution)/shard_map/ppermute | solution.py:809
  20.2 1.3 %collective-permute-start.12 = (f32[4,1024]{1,0:T(4,128)S(1)}, f32[4,1024]{1,0:T(4,128)S(1)}, u32[]{:S(2)}, u32[]{:S(2)}) collective-permute-start(f32[4,1024]{1,0:T(4,128)S(1)} %collective-permute-done.8.refs_2_), channel_id=1, source_target_pairs={{0,1},{1,0},{2,3},{3,2},{4,5},{5,4},{6,7},{7,6},{8,9},{9,8},{10,11... | collective-permute-start | bytes 49160 | tf_op jit(solution)/shard_map/ppermute | solution.py:809
  20.7 1.2 %collective-permute-start.13 = (f32[4,1024]{1,0:T(4,128)S(1)}, f32[4,1024]{1,0:T(4,128)S(1)}, u32[]{:S(2)}, u32[]{:S(2)}) collective-permute-start(f32[4,1024]{1,0:T(4,128)S(1)} %collective-permute-done.9.refs_3_), channel_id=1, source_target_pairs={{0,1},{1,0},{2,3},{3,2},{4,5},{5,4},{6,7},{7,6},{8,9},{9,8},{10,11... | collective-permute-start | bytes 49160 | tf_op jit(solution)/shard_map/ppermute | solution.py:809
  21.9 0.8 %copy-start.16 = (f32[4,16,128]{2,1,0:T(8,128)S(1)}, f32[4,16,128]{2,1,0:T(8,128)}, u32[]{:S(2)}) copy-start(f32[4,16,128]{2,1,0:T(8,128)} %get-tuple-element.57.refs_10_) | copy-start | bytes 98308
  22.6 5.8 %copy-start = (f32[1,4,80,1024]{3,2,1,0:T(8,128)S(1)}, f32[1,4,80,1024]{3,2,1,0:T(8,128)}, u32[]{:S(2)}) copy-start(f32[1,4,80,1024]{3,2,1,0:T(8,128)} %param.25) | copy-start | bytes 3932164
  22.6 5.8 %copy-start.1 = (s32[1,1024]{1,0:T(1,128)S(1)}, s32[1,1024]{1,0:T(1,128)}, u32[]{:S(2)}) copy-start(s32[1,1024]{1,0:T(1,128)} %sea.3) | copy-start | bytes 12292
  22.6 5.8 %copy-start.3 = (f32[128,128]{1,0:T(8,128)S(1)}, f32[128,128]{1,0:T(8,128)}, u32[]{:S(2)}) copy-start(f32[128,128]{1,0:T(8,128)} %vertical.5) | copy-start | bytes 196612
  22.6 5.8 %copy-start.4 = (f32[80,80]{1,0:T(8,128)S(1)}, f32[80,80]{1,0:T(8,128)}, u32[]{:S(2)}) copy-start(f32[80,80]{1,0:T(8,128)} %overt.1) | copy-start | bytes 76804
  22.6 5.8 %copy-start.5 = (f32[4,16,16]{2,1,0:T(8,128)S(1)}, f32[4,16,16]{2,1,0:T(8,128)}, u32[]{:S(2)}) copy-start(f32[4,16,16]{2,1,0:T(8,128)} %param.23) | copy-start | bytes 12292
  22.7 5.8 %copy-start.6 = (s32[1,6,1024]{2,0,1:T(1,128)S(1)}, s32[1,6,1024]{2,0,1:T(1,128)}, u32[]{:S(2)}) copy-start(s32[1,6,1024]{2,0,1:T(1,128)} %param.26) | copy-start | bytes 73732
  22.7 5.8 %copy-start.7 = (f32[1,6,1024]{2,0,1:T(1,128)S(1)}, f32[1,6,1024]{2,0,1:T(1,128)}, u32[]{:S(2)}) copy-start(f32[1,6,1024]{2,0,1:T(1,128)} %param.27) | copy-start | bytes 73732
  22.7 5.8 %copy-start.9 = (f32[16,16]{1,0:T(8,128)S(1)}, f32[16,16]{1,0:T(8,128)}, u32[]{:S(2)}) copy-start(f32[16,16]{1,0:T(8,128)} %stiffness.3) | copy-start | bytes 3076
  22.7 5.8 %copy-start.10 = (f32[1,16,128]{2,1,0:T(8,128)S(1)}, f32[1,16,128]{2,1,0:T(8,128)}, u32[]{:S(2)}) copy-start(f32[1,16,128]{2,1,0:T(8,128)} %param.20) | copy-start | bytes 24580
  22.7 5.8 %copy-start.11 = (s32[1,4,128]{2,1,0:T(4,128)S(1)}, s32[1,4,128]{2,1,0:T(4,128)}, u32[]{:S(2)}) copy-start(s32[1,4,128]{2,1,0:T(4,128)} %param.19) | copy-start | bytes 6148
  22.7 5.8 %copy-start.15 = (bf16[2048,1024]{1,0:T(8,128)(2,1)S(1)}, bf16[2048,1024]{1,0:T(8,128)(2,1)}, u32[]{:S(2)}) copy-start(bf16[2048,1024]{1,0:T(8,128)(2,1)} %get-tuple-element.59.xt) | copy-start | bytes 12582916
  24.8 26.1 %collective-permute-start.14 = (f32[64,4,128]{2,1,0:T(4,128)S(1)}, f32[64,4,128]{2,1,0:T(4,128)S(1)}, u32[]{:S(2)}, u32[]{:S(2)}) collective-permute-start(f32[64,4,128]{2,1,0:T(4,128)S(1)} %get-tuple-element.58), channel_id=1, source_target_pairs={{0,24},{1,25},{2,26},{3,27},{4,28},{5,29},{6,30},{7,31}} | collective-permute-start | bytes 393224 | tf_op jit(solution)/shard_map/ppermute | solution.py:828
  25.5 25.4 %collective-permute-start.15 = (f32[64,4,128]{2,1,0:T(4,128)S(1)}, f32[64,4,128]{2,1,0:T(4,128)S(1)}, u32[]{:S(2)}, u32[]{:S(2)}) collective-permute-start(f32[64,4,128]{2,1,0:T(4,128)S(1)} %get-tuple-element.58), channel_id=1, source_target_pairs={{8,24},{9,25},{10,26},{11,27},{12,28},{13,29},{14,30},{15,31}} | collective-permute-start | bytes 393224 | tf_op jit(solution)/shard_map/ppermute | solution.py:828
  26.2 24.7 %collective-permute-start.16 = (f32[64,4,128]{2,1,0:T(4,128)S(1)}, f32[64,4,128]{2,1,0:T(4,128)S(1)}, u32[]{:S(2)}, u32[]{:S(2)}) collective-permute-start(f32[64,4,128]{2,1,0:T(4,128)S(1)} %get-tuple-element.58), channel_id=1, source_target_pairs={{16,24},{17,25},{18,26},{19,27},{20,28},{21,29},{22,30},{23,31}} | collective-permute-start | bytes 393224 | tf_op jit(solution)/shard_map/ppermute | solution.py:828
  30.4 9.3 %collective-permute-start.19 = (f32[4,128,128]{2,1,0:T(8,128)S(1)}, f32[4,128,128]{2,1,0:T(8,128)S(1)}, u32[]{:S(2)}, u32[]{:S(2)}) collective-permute-start(f32[4,128,128]{2,1,0:T(8,128)S(1)} %get-tuple-element.66), channel_id=1, source_target_pairs={{0,1},{1,0},{2,3},{3,2},{4,5},{5,4},{6,7},{7,6},{8,9},{9,8},{10,11... | collective-permute-start | bytes 786440 | tf_op jit(solution)/shard_map/ppermute | solution.py:847
  30.6 12.3 %collective-permute-start.20 = (f32[4,128,128]{2,1,0:T(8,128)S(1)}, f32[4,128,128]{2,1,0:T(8,128)S(1)}, u32[]{:S(2)}, u32[]{:S(2)}) collective-permute-start(f32[4,128,128]{2,1,0:T(8,128)S(1)} %get-tuple-element.67), channel_id=1, source_target_pairs={{1,2},{3,4},{5,6},{7,8},{9,10},{11,12},{13,14},{15,16},{17,18},{19... | collective-permute-start | bytes 786440 | tf_op jit(solution)/shard_map/ppermute | solution.py:846

commit v4 on v3

--- a/solution.py
+++ b/solution.py
@@ -79,7 +79,7 @@
     return jnp.where(first, b, a), jnp.where(first, a, b)
 
 
-def turn_kernel(ocean, dom, x, o, xt, to_core, to_chip, surface, zeroed, xv, tv, hv, in_sem, out_sem, o_sem, z_sem):
+def turn_kernel(ocean, dom, x, o, xt, to_core, to_chip, surface, xv, tv, hv, in_sem, out_sem, o_sem):
     fields, points = xv.shape[0], 16
     olev, cells = o.shape[1], o.shape[2]
     groups = LANES // GROUP
@@ -115,18 +115,14 @@
 
     @pl.when(ocean[0] != 0)
     def _():
-        xv[0] = jnp.zeros_like(xv[0])
-        zeros = copies([(xv.at[0], zeroed.at[f]) for f in range(fields)], z_sem)
         pairs = []
         for f in range(fields):
             pairs.append((o.at[f, :, pl.ds(0, HALO_O)], hv.at[0, f, pl.ds(0, olev)]))
             pairs.append((o.at[f, :, pl.ds(cells - HALO_O, HALO_O)], hv.at[1, f, pl.ds(0, olev)]))
         loads = copies(pairs, o_sem)
         start(loads)
-        start(zeros)
         wait(loads)
         hand_out(dom, hv, to_core, to_chip)
-        wait(zeros)
 
 
 def turn(ocean_flag, dom, state, ocean):
@@ -140,10 +136,9 @@
             halo,
             halo,
             jax.ShapeDtypeStruct((fields, points, elems), F32),
-            jax.ShapeDtypeStruct((fields, levels * points, elems), F32),
         ),
         in_specs=[SMEM, SMEM, ANY, ANY],
-        out_specs=(ANY, VMEM, VMEM, VMEM, HBM),
+        out_specs=(ANY, VMEM, VMEM, VMEM),
         scratch_shapes=[
             pltpu.VMEM((fields, levels * points, elems), F32),
             pltpu.VMEM((rows, 2 * fields * LANES), BF16),
@@ -151,7 +146,6 @@
             pltpu.SemaphoreType.DMA((fields,)),
             pltpu.SemaphoreType.DMA((fields, 2)),
             pltpu.SemaphoreType.DMA((2 * fields,)),
-            pltpu.SemaphoreType.DMA((fields,)),
         ],
         compiler_params=params(TURN),
         cost_estimate=cost(2000000000, 9 << 20),
@@ -269,8 +263,8 @@
 def edge_kernel(
     ocean, dom, elem, base, xt, from_core, from_chip, enbr, coupling, stiffness, metric, vertical, flux,
     o, nbr, diff, sea, overt, held,
-    u, to_core, to_chip, fresh,
-    table, cx, nt, xhl, hv, wa, mt, ft, ov, ext, res, vert, o_sem, r_sem,
+    u, to_core, to_chip, fresh, zeroed,
+    table, cx, nt, xhl, hv, wa, mt, ft, ov, ext, res, vert, zv, o_sem, r_sem, z_sem,
 ):
     del held
     fields, points = flux.shape[0], flux.shape[1]
@@ -304,7 +298,11 @@
     def _():
         load = pltpu.make_async_copy(o, ov, o_sem.at[0])
         load.start()
+        zv[...] = jnp.zeros_like(zv)
+        zeros = copies([(zv, zeroed.at[f]) for f in range(fields)], z_sem)
+        start(zeros)
         ocean_part(dom, base, load, from_core, from_chip, nbr, diff, sea, overt, fresh, ov, ext, res, vert, r_sem)
+        wait(zeros)
 
 
 def edge_step(
@@ -324,9 +322,10 @@
             halo,
             halo,
             jax.ShapeDtypeStruct(ocean.shape, F32),
+            jax.ShapeDtypeStruct((fields,) + xt.shape[:1] + (LANES,), F32),
         ),
         in_specs=[SMEM] * 4 + [VMEM] * 9 + [HBM] + [VMEM] * 4 + [HBM],
-        out_specs=(VMEM, VMEM, VMEM, HBM),
+        out_specs=(VMEM, VMEM, VMEM, HBM, HBM),
         input_output_aliases={18: 3},
         scratch_shapes=[
             pltpu.VMEM((2, 4 * LANES, 4 * LANES), BF16),
@@ -341,8 +340,10 @@
             pltpu.VMEM((2, fields * olev, cells + 2 * HALO_O), BF16),
             pltpu.VMEM(ocean.shape, F32),
             pltpu.VMEM(ocean.shape, F32),
+            pltpu.VMEM(xt.shape[:1] + (LANES,), F32),
             pltpu.SemaphoreType.DMA((1,)),
             pltpu.SemaphoreType.DMA((1,)),
+            pltpu.SemaphoreType.DMA((fields,)),
         ],
         compiler_params=params(20),
         cost_estimate=cost(4000000000, 3 << 20),
@@ -353,7 +354,7 @@
     )
 
 
-def inner_kernel(ocean, elem, xt, ue, enbr, coupling, stiffness, metric, vertical, flux, u, table, cx, nt, wa, mt, ft):
+def inner_kernel(ocean, elem, xt, ue, enbr, coupling, stiffness, metric, vertical, flux, u, table, xv, cx, nt, wa, mt, ft):
     fields, points = flux.shape[0], flux.shape[1]
     sides = enbr.shape[0]
     rows = xt.shape[0]
@@ -385,6 +386,18 @@
                 window = xt.at[pl.ds(pl.multiple_of(first - LANES, LANES), 4 * LANES)]
                 advance(window, table.at[b], wa, mt, element, points, store, range(fields))
                 build_table(b + 1, table, b + 1, cx, nt, sides, points)
+
+        @pl.loop(1, blocks - 1, step=3)
+        def _(start_of):
+            for i in range(3):
+                b = start_of + i
+                first = pl.multiple_of(b * edge, edge)
+
+                def store(f, value):
+                    xv[f, pl.ds(first, edge), :] = value
+
+                window = u.at[pl.ds(pl.multiple_of(first - LANES, LANES), 4 * LANES)]
+                advance(window, table.at[b], wa, mt, b * 2 * GROUP, points, store, range(fields))
 
 
 def ocean_part(dom, base, load, from_core, from_chip, nbr, diff, sea, overt, fresh, ov, ext, res, vert, r_sem):
@@ -445,9 +458,10 @@
         out_shape=(
             jax.ShapeDtypeStruct((rows, width), BF16),
             jax.ShapeDtypeStruct((blocks, 4 * LANES, 4 * LANES), BF16),
+            jax.ShapeDtypeStruct((fields, rows, LANES), F32),
         ),
         in_specs=[SMEM, SMEM] + [VMEM] * 8,
-        out_specs=(VMEM, VMEM),
+        out_specs=(VMEM, VMEM, VMEM),
         scratch_shapes=[
             pltpu.VMEM(((sides + 1) * points, LANES), F32),
             pltpu.VMEM((LANES, LANES), F32),
@@ -462,9 +476,9 @@
 
 
 def flux_kernel(ocean, dom, owner, block, source, *refs):
-    n_tops = len(refs) - 12
+    n_tops = len(refs) - 14
     tops = refs[:n_tops]
-    weights, coef, sv, flux, sent, fresh, tv, wcat, surf, fl, zv, z_sem = refs[n_tops:]
+    weights, coef, surface, flux, sent, fresh, sv, tv, wcat, surf, fl, zv, z_sem, s_sem = refs[n_tops:]
     pairs = weights.shape[0]
     points, fields = coef.shape[0], flux.shape[0]
     ocean_blocks = sent.shape[0] // n_tops
@@ -472,6 +486,8 @@
 
     @pl.when(ocean[0] == 0)
     def _():
+        load = pltpu.make_async_copy(surface, sv, s_sem)
+        load.start()
         zv[...] = jnp.zeros_like(zv)
         zeros = copies([(zv, fresh.at[f]) for f in range(fields)], z_sem)
         start(zeros)
@@ -500,6 +516,7 @@
             out = dot_t(rows, wcat[r])
             surf[source[r]] += out[:fields] + out[fields:]
 
+        load.wait()
         for p in range(points):
             value = coef[pl.ds(p, 1), :] * (sv[:, p, :] - surf[p])
             fl[p] = value
@@ -524,15 +541,17 @@
             jax.ShapeDtypeStruct((n * ocean_blocks, fields, BLK), F32),
             jax.ShapeDtypeStruct(ocean_shape, F32),
         ),
-        in_specs=[SMEM] * 5 + [VMEM] * (n + 3),
+        in_specs=[SMEM] * 5 + [VMEM] * (n + 2) + [ANY],
         out_specs=(VMEM, VMEM, HBM),
         scratch_shapes=[
+            pltpu.VMEM((fields, points, elems), F32),
             pltpu.VMEM((n,) + tops[0].shape, F32),
             pltpu.VMEM((pairs, BLK, 2 * BLK), BF16),
             pltpu.VMEM((points, fields, BLK), F32),
             pltpu.VMEM((points, fields, BLK), F32),
             pltpu.VMEM(ocean_shape[1:], F32),
             pltpu.SemaphoreType.DMA((fields,)),
+            pltpu.SemaphoreType.DMA,
         ],
         compiler_params=params(8),
         cost_estimate=cost(2_500_000_000, 2 << 20),
@@ -540,38 +559,38 @@
     )(ocean_flag, dom, owner, block, source, *tops, weights, coef, surface)
 
 
-def second_kernel(ocean, dom, u, from_core, from_chip, table, metric, vertical, flux, held, out, xhl, wa, mt, xv, ov, o_sem):
+def second_kernel(
+    ocean, dom, xv, u, from_core, from_chip, table, metric, vertical, flux, held, out, xhl, wa, mt, xe, ov, o_sem
+):
     del held
     fields, points = flux.shape[0], flux.shape[1]
-    rows, levels = xv.shape[1], xv.shape[2]
     blocks = table.shape[0]
+    levels = xv.shape[2]
+    groups = LANES // GROUP
     edge = 2 * LANES
 
     @pl.when(ocean[0] == 0)
     def _():
         prepare(metric, vertical, wa, mt)
         edge_windows(dom, xhl, u, from_core, from_chip)
-
-        def step(b, window):
-            first = b * edge if isinstance(b, int) else pl.multiple_of(b * edge, edge)
+        for i in range(2):
+            b = i * (blocks - 1)
 
             def store(f, value):
-                xv[f, pl.ds(first, edge), :] = value
-
-            advance(window, table.at[b], wa, mt, b * 2 * GROUP, points, store, range(fields))
-
-        @pl.loop(1, blocks - 1, step=3)
-        def _(start_of):
-            for i in range(3):
-                b = start_of + i
-                step(b, u.at[pl.ds(pl.multiple_of(b * edge - LANES, LANES), 4 * LANES)])
-
-        step(0, xhl.at[pl.ds(0, 4 * LANES)])
-        step(blocks - 1, xhl.at[pl.ds(4 * LANES, 4 * LANES)])
+                xe[f, pl.ds(i * edge, edge), :] = value
+
+            advance(
+                xhl.at[pl.ds(i * 4 * LANES, 4 * LANES)], table.at[b], wa, mt, b * 2 * GROUP, points, store, range(fields)
+            )
         outs = copies([(ov.at[f], out.at[f]) for f in range(fields)], o_sem)
         for f in range(fields):
             for p in range(points):
-                cols = [xv[f, pl.ds(g * LANES + p * GROUP, GROUP), :] for g in range(LANES // GROUP)]
+                cols = []
+                for g in range(groups):
+                    if 2 <= g < groups - 2:
+                        cols.append(xv[f, pl.ds(g * LANES + p * GROUP, GROUP), :])
+                    else:
+                        cols.append(xe[f, pl.ds((g % (groups - 4)) * LANES + p * GROUP, GROUP), :])
                 ov[f, pl.ds(p, LANES, stride=points), :] = jnp.concatenate(cols, axis=0).T
             last = pl.ds((levels - 1) * points, points)
             ov[f, last, :] = ov[f, last, :] - 0.5 * flux[f]
@@ -579,27 +598,28 @@
         wait(outs)
 
 
-def second_step(ocean_flag, dom, u, from_core, from_chip, table, metric, vertical, flux, zeroed, levels):
-    fields, points = flux.shape[0], flux.shape[1]
-    rows, width = u.shape
+def second_step(ocean_flag, dom, xv, u, from_core, from_chip, table, metric, vertical, flux, zeroed):
+    fields, rows, levels = xv.shape
+    points = flux.shape[1]
+    width = u.shape[1]
     return pl.pallas_call(
         second_kernel,
         out_shape=jax.ShapeDtypeStruct((fields, levels * points, LANES), F32),
-        in_specs=[SMEM, SMEM] + [VMEM] * 7 + [HBM],
+        in_specs=[SMEM, SMEM] + [VMEM] * 8 + [HBM],
         out_specs=HBM,
-        input_output_aliases={9: 0},
+        input_output_aliases={10: 0},
         scratch_shapes=[
             pltpu.VMEM((8 * LANES, width), BF16),
             pltpu.VMEM((2 * LANES, 2 * LANES), BF16),
             pltpu.VMEM((LANES, LANES), F32),
-            pltpu.VMEM((fields, rows, levels), F32),
+            pltpu.VMEM((fields, 4 * LANES, levels), F32),
             pltpu.VMEM((fields, levels * points, LANES), F32),
             pltpu.SemaphoreType.DMA((fields,)),
         ],
         compiler_params=params(20),
-        cost_estimate=cost(10000000000, 12 << 20),
+        cost_estimate=cost(10_000_000_000, 12 << 20),
         name="second_step",
-    )(ocean_flag, dom, u, from_core, from_chip, table, metric, vertical, flux, zeroed)
+    )(ocean_flag, dom, xv, u, from_core, from_chip, table, metric, vertical, flux, zeroed)
 
 
 def blank_kernel(out):
@@ -790,9 +810,6 @@
     def to_ocean(c):
         return [(j, i) for i, j in from_ocean(c)]
 
-    def among_ocean(pairs):
-        return [(live * n_dom + a, live * n_dom + b) for a, b in pairs]
-
     is_ocean = comp_index == live
     chips = n_dom // 2
 
@@ -801,7 +818,7 @@
 
     top = top_rows(flag, ocean)
     brought = [lax.ppermute(top, both, from_ocean(c)) for c in range(live)]
-    xt, to_core, to_chip, surface, zeroed = turn(flag, dom, state, ocean)
+    xt, to_core, to_chip, surface = turn(flag, dom, state, ocean)
     brought, to_core, to_chip = lax.optimization_barrier((brought, to_core, to_chip))
     got = sum(brought)
     got, to_core, to_chip = lax.optimization_barrier((got, to_core, to_chip))
@@ -826,7 +843,7 @@
         ocean_blocks,
     )
     parts = [lax.ppermute(sent, both, to_ocean(c)) for c in range(live)]
-    ue, to_core, to_chip, fresh = edge_step(
+    ue, to_core, to_chip, fresh, zeroed = edge_step(
         flag,
         dom,
         elem_base,
@@ -845,17 +862,19 @@
     )
     from_chip2 = lax.ppermute(to_chip, both, atm_chips)
     from_core2 = lax.ppermute(to_core, "dom", swapped)
-    u, table = inner_step(flag, elem_base, xt, ue, *operators, flux)
-    atm_next = second_step(flag, dom, u, from_core2, from_chip2, table, metric, atm_vertical, flux, zeroed, levels)
+    u, table, xv = inner_step(flag, elem_base, xt, ue, *operators, flux)
+    atm_next = second_step(
+        flag, dom, xv, u, from_core2, from_chip2, table, metric, atm_vertical, flux, zeroed
+    )
 
     parts, atm_next = lax.optimization_barrier((parts, atm_next))
 
     def reduce_parts():
         same, other = gather_sent(dom, parts, n_dom)
-        pieces = pair_sums(same, lax.ppermute(other, both, among_ocean(swapped)))
+        pieces = pair_sums(same, lax.ppermute(other, "dom", swapped))
         mine = [pieces[0]]
         for s in range(1, chips):
-            mine.append(lax.ppermute(pieces[s], both, among_ocean(shifted(s))))
+            mine.append(lax.ppermute(pieces[s], "dom", shifted(s)))
         return add_up(mine)
 
     total = lax.cond(is_ocean, reduce_parts, lambda: blank((ocean_blocks, fields, BLK)))

time: 52 us -> 48.4 us (0.931)
  waiting for transfers between devices: 4.77 us -> 1.92 us
    pallas_call x1, Pallas kernels: 5.75 us -> 9.52 us  [inner_step(): pl.pallas_call(inner_kernel, out_shape=(jax.ShapeDtypeStruct((rows, width...]
    pallas_call x1, Pallas kernels: 8.03 us -> 4.36 us  [second_step(): pl.pallas_call(second_kernel, out_shape=jax.ShapeDtypeStruct((fields, lev...]
    ppermute x1, waiting for transfers between devices: 3.15 us -> 0.01 us  [local(): from_chip2 = lax.ppermute(to_chip, both, atm_chips)]
    ppermute x3, starting transfers between devices: 3.51 us -> 2.64 us  [local(): parts = [lax.ppermute(sent, both, to_ocean(c)) for c in range(live)]]
  transfers between devices with their start and end apart: 17 -> 17, of which waited for: 5 -> 5; matrix products, arithmetic and copies ran while one was open for 0% -> 0% of each run, Pallas kernels for 45% -> 48%
where the time goes in v4:
time: 48.4 us; the launch traced here: 48 us
  Pallas kernels  23.8 us (49%)
  starting transfers between devices  20.2 us (42%)
  waiting for transfers between devices  1.92 us (4%)
  between operations  1.22 us (3%)
  local copies, waits for them, and re-layouts  0.83 us (2%)
    pallas_call x1, Pallas kernels, inner_step(): pl.pallas_call(inner_kernel, out_shape=(jax.ShapeDtypeStruct((rows, width...  9.52 us
    ppermute x1, starting transfers between devices, local(): from_chip = lax.ppermute(to_chip, both, all_chips)  5.42 us
    pallas_call x1, Pallas kernels, turn(): pl.pallas_call(turn_kernel, out_shape=(jax.ShapeDtypeStruct((rows, 2 * fi...  4.99 us
    ppermute x3, starting transfers between devices, local(): lax.ppermute(got, 'dom', shifted(s))  4.45 us
    pallas_call x1, Pallas kernels, second_step(): pl.pallas_call(second_kernel, out_shape=jax.ShapeDtypeStruct((fields, lev...  4.36 us
    ppermute x1, starting transfers between devices, local(): from_chip2 = lax.ppermute(to_chip, both, atm_chips)  3.84 us
    ppermute x3, starting transfers between devices, local(): parts = [lax.ppermute(sent, both, to_ocean(c)) for c in range(live)]  2.64 us
    ppermute x3, starting transfers between devices, local(): brought = [lax.ppermute(top, both, from_ocean(c)) for c in range(live)]  2.62 us
  transfers between devices with their start and end apart: 17, of which 5 were waited for; matrix products, arithmetic and copies ran while one was open for 0% of the time, Pallas kernels for 48%

profile of v4, /device:TPU:4, one launch (start us, length us, event | category | flops | bytes accessed | tf_op | source)
XLA Modules:
  0.0 48.0 jit_solution(13634425119155119300)
XLA Ops:
  0.6 0.0 copy-start.2
  0.7 0.0 copy-start.8
  0.7 0.0 copy-start.12
  0.7 0.0 copy-start.13
  0.7 0.0 copy-start.14
  0.7 0.7 %top_rows.1 = f32[4,1024]{1,0:T(4,128)} custom-call(s32[1]{0:T(128)} %bitcast.ocean, f32[4,80,1024]{2,1,0:T(8,128)} %bitcast.18), custom_call_target="tpu_custom_call" | custom-call | bytes 65536 | tf_op jit(solution)/shard_map/top_rows/pallas_call | solution.py:649
  1.4 0.7 %collective-permute-start.4 = (f32[4,1024]{1,0:T(4,128)}, f32[4,1024]{1,0:T(4,128)S(1)}, u32[]{:S(2)}, u32[]{:S(2)}) collective-permute-start(f32[4,1024]{1,0:T(4,128)} %top_rows.1), channel_id=1, source_target_pairs={{24,0},{25,1},{26,2},{27,3},{28,4},{29,5},{30,6},{31,7}} | collective-permute-start | bytes 49160 | tf_op jit(solution)/shard_map/ppermute | solution.py:820
  2.0 0.7 %collective-permute-start.5 = (f32[4,1024]{1,0:T(4,128)}, f32[4,1024]{1,0:T(4,128)S(1)}, u32[]{:S(2)}, u32[]{:S(2)}) collective-permute-start(f32[4,1024]{1,0:T(4,128)} %top_rows.1), channel_id=1, source_target_pairs={{24,8},{25,9},{26,10},{27,11},{28,12},{29,13},{30,14},{31,15}} | collective-permute-start | bytes 49160 | tf_op jit(solution)/shard_map/ppermute | solution.py:820
  2.7 1.3 %collective-permute-start.6 = (f32[4,1024]{1,0:T(4,128)}, f32[4,1024]{1,0:T(4,128)S(1)}, u32[]{:S(2)}, u32[]{:S(2)}) collective-permute-start(f32[4,1024]{1,0:T(4,128)} %top_rows.1), channel_id=1, source_target_pairs={{24,16},{25,17},{26,18},{27,19},{28,20},{29,21},{30,22},{31,23}} | collective-permute-start | bytes 49160 | tf_op jit(solution)/shard_map/ppermute | solution.py:820
  4.0 5.0 %turn_state.1 = (bf16[2048,1024]{1,0:T(8,128)(2,1)}, f32[4,128,128]{2,1,0:T(8,128)}, f32[4,128,128]{2,1,0:T(8,128)}, f32[4,16,128]{2,1,0:T(8,128)}) custom-call(s32[1]{0:T(128)} %bitcast.ocean, s32[1]{0:T(128)} %bitcast.1.dom, f32[4,2048,128]{2,1,0:T(8,128)} %bitcast.36, f32[4,80,1024]{2,1,0:T(8,128)} %bitcast.19), custom_call_target="tpu_custom_call" | custom-call | flops 2000000000 | bytes 9437184 | tf_op jit(solution)/shard_map/turn_state/pallas_call | solution.py:132
  9.0 0.0 collective-permute-done.4
  9.0 0.0 collective-permute-done.5
  9.0 0.6 %collective-permute-done.6 = f32[4,1024]{1,0:T(4,128)S(1)} collective-permute-done((f32[4,1024]{1,0:T(4,128)}, f32[4,1024]{1,0:T(4,128)S(1)}, u32[]{:S(2)}, u32[]{:S(2)}) %collective-permute-start.6) | collective-permute-done | bytes 16416 | tf_op jit(solution)/shard_map/ppermute | solution.py:820
  9.6 1.8 %collective-permute-start.7 = (f32[4,1024]{1,0:T(4,128)S(1)}, f32[4,1024]{1,0:T(4,128)S(1)}, u32[]{:S(2)}, u32[]{:S(2)}) collective-permute-start(f32[4,1024]{1,0:T(4,128)S(1)} %add_add_fusion.refs_0_), channel_id=1, source_target_pairs={{0,2},{1,3},{2,0},{3,1},{4,6},{5,7},{6,4},{7,5},{8,10},{9,11},{10,... | collective-permute-start | bytes 49160 | tf_op jit(solution)/shard_map/ppermute | solution.py:825
  11.4 2.6 %collective-permute-start.8 = (f32[4,1024]{1,0:T(4,128)S(1)}, f32[4,1024]{1,0:T(4,128)S(1)}, u32[]{:S(2)}, u32[]{:S(2)}) collective-permute-start(f32[4,1024]{1,0:T(4,128)S(1)} %add_add_fusion.refs_0_), channel_id=1, source_target_pairs={{0,4},{1,5},{2,6},{3,7},{4,0},{5,1},{6,2},{7,3},{8,12},{9,13},{10,... | collective-permute-start | bytes 49160 | tf_op jit(solution)/shard_map/ppermute | solution.py:825
  14.0 0.1 collective-permute-start.9
  14.1 0.0 collective-permute-start.10
  14.1 0.5 %collective-permute-start.17 = (f32[4,128,128]{2,1,0:T(8,128)}, f32[4,128,128]{2,1,0:T(8,128)S(1)}, u32[]{:S(2)}, u32[]{:S(2)}) collective-permute-start(f32[4,128,128]{2,1,0:T(8,128)} %get-tuple-element.61), channel_id=1, source_target_pairs={{0,1},{1,0},{2,3},{3,2},{4,5},{5,4},{6,7},{7,6},{8,9},{9,8},{10,11... | collective-permute-start | bytes 786440 | tf_op jit(solution)/shard_map/ppermute | solution.py:827
  14.6 0.0 collective-permute-done.7.refs_1_
  14.6 5.4 %collective-permute-start.18 = (f32[4,128,128]{2,1,0:T(8,128)}, f32[4,128,128]{2,1,0:T(8,128)S(1)}, u32[]{:S(2)}, u32[]{:S(2)}) collective-permute-start(f32[4,128,128]{2,1,0:T(8,128)} %get-tuple-element.62), channel_id=1, source_target_pairs={{1,2},{3,4},{5,6},{7,8},{9,10},{11,12},{13,14},{15,16},{17,18},{19... | collective-permute-start | bytes 786440 | tf_op jit(solution)/shard_map/ppermute | solution.py:828
  20.0 0.0 collective-permute-done.8.refs_2_
  20.0 0.1 collective-permute-start.11
  20.1 0.0 collective-permute-done.9.refs_3_
  20.1 0.5 %collective-permute-start.12 = (f32[4,1024]{1,0:T(4,128)S(1)}, f32[4,1024]{1,0:T(4,128)S(1)}, u32[]{:S(2)}, u32[]{:S(2)}) collective-permute-start(f32[4,1024]{1,0:T(4,128)S(1)} %collective-permute-done.8.refs_2_), channel_id=1, source_target_pairs={{0,1},{1,0},{2,3},{3,2},{4,5},{5,4},{6,7},{7,6},{8,9},{9,8},{10,11... | collective-permute-start | bytes 49160 | tf_op jit(solution)/shard_map/ppermute | solution.py:826
  20.6 0.0 collective-permute-done.10.refs_4_
  20.6 0.1 collective-permute-start.13
  20.7 0.6 %collective-permute-done.11.refs_5_ = f32[4,1024]{1,0:T(4,128)S(1)} collective-permute-done((f32[4,1024]{1,0:T(4,128)S(1)}, f32[4,1024]{1,0:T(4,128)S(1)}, u32[]{:S(2)}, u32[]{:S(2)}) %collective-permute-start.11) | collective-permute-done | bytes 16416 | tf_op jit(solution)/shard_map/ppermute | solution.py:826
  21.3 0.2 collective-permute-done.12.refs_6_
  21.4 0.3 collective-permute-done.13.refs_7_
  21.8 0.0 copy-done.2
  21.8 0.0 copy-done.8
  21.8 0.0 copy-done.12
  21.8 0.0 copy-done.13
  21.8 0.0 copy-done.14
  21.8 0.0 copy-start.16
  21.8 0.7 %copy-done.16 = f32[4,16,128]{2,1,0:T(8,128)S(1)} copy-done((f32[4,16,128]{2,1,0:T(8,128)S(1)}, f32[4,16,128]{2,1,0:T(8,128)}, u32[]{:S(2)}) %copy-start.16) | copy-done | bytes 32792
  22.6 0.0 copy-start.5
  22.6 0.0 copy-start.6
  22.6 0.0 copy-start.7
  22.6 0.0 copy-start.9
  22.6 0.0 copy-start.10
  22.6 0.0 copy-start.11
  22.6 0.0 copy-start.15
  22.7 2.2 %fluxes.1 = (f32[4,16,128]{2,1,0:T(8,128)S(1)}, f32[64,4,128]{2,1,0:T(4,128)S(1)}, f32[4,80,1024]{2,1,0:T(8,128)}) custom-call(s32[1]{0:T(128)} %bitcast.ocean, s32[1]{0:T(128)} %bitcast.1.dom, s32[32]{0:T(128)S(1)} %bitcast.32, s32[32]{0:T(128)S(1)} %bitcast.33, s32[32]{0:T(128)S(1)} %bitcast.34, f32[4,1024]{1,0:T(4,128)S(1)} %add_add_fusion.refs_0_, ...), custom_call_target="tpu_custom_call" | custom-call | flops 2500000000 | bytes 2097152 | tf_op jit(solution)/shard_map/fluxes/pallas_call | solution.py:537
  24.9 0.7 %collective-permute-start.14 = (f32[64,4,128]{2,1,0:T(4,128)S(1)}, f32[64,4,128]{2,1,0:T(4,128)S(1)}, u32[]{:S(2)}, u32[]{:S(2)}) collective-permute-start(f32[64,4,128]{2,1,0:T(4,128)S(1)} %get-tuple-element.59), channel_id=1, source_target_pairs={{0,24},{1,25},{2,26},{3,27},{4,28},{5,29},{6,30},{7,31}} | collective-permute-start | bytes 393224 | tf_op jit(solution)/shard_map/ppermute | solution.py:845
  25.5 0.7 %collective-permute-start.15 = (f32[64,4,128]{2,1,0:T(4,128)S(1)}, f32[64,4,128]{2,1,0:T(4,128)S(1)}, u32[]{:S(2)}, u32[]{:S(2)}) collective-permute-start(f32[64,4,128]{2,1,0:T(4,128)S(1)} %get-tuple-element.59), channel_id=1, source_target_pairs={{8,24},{9,25},{10,26},{11,27},{12,28},{13,29},{14,30},{15,31}} | collective-permute-start | bytes 393224 | tf_op jit(solution)/shard_map/ppermute | solution.py:845
  26.2 1.3 %collective-permute-start.16 = (f32[64,4,128]{2,1,0:T(4,128)S(1)}, f32[64,4,128]{2,1,0:T(4,128)S(1)}, u32[]{:S(2)}, u32[]{:S(2)}) collective-permute-start(f32[64,4,128]{2,1,0:T(4,128)S(1)} %get-tuple-element.59), channel_id=1, source_target_pairs={{16,24},{17,25},{18,26},{19,27},{20,28},{21,29},{22,30},{23,31}} | collective-permute-start | bytes 393224 | tf_op jit(solution)/shard_map/ppermute | solution.py:845
  27.5 0.0 collective-permute-done.17.from_core
  27.5 0.2 collective-permute-done.18.from_chip
  27.7 0.0 copy-done
  27.7 0.0 copy-done.1
  27.7 0.0 copy-done.3
  27.8 0.0 copy-done.4
  27.8 2.0 %edge_step.1 = (bf16[512,1024]{1,0:T(8,128)(2,1)S(1)}, f32[4,128,128]{2,1,0:T(8,128)S(1)}, f32[4,128,128]{2,1,0:T(8,128)S(1)}, f32[4,80,1024]{2,1,0:T(8,128)}, f32[4,2048,128]{2,1,0:T(8,128)}) custom-call(s32[1]{0:T(128)} %bitcast.ocean, s32[1]{0:T(128)} %bitcast.1.dom, s32[1]{0:T(128)} %bitcast.9.elem, ...), custom_call_target="tpu_custom_call", output_to_operand_aliasing={{3}: (18, {})} | custom-call | flops 4000000000 | bytes 3145728 | tf_op jit(solution)/shard_map/edge_step/pallas_call | solution.py:318
  29.8 0.1 collective-permute-start.19
  29.9 3.8 %collective-permute-start.20 = (f32[4,128,128]{2,1,0:T(8,128)S(1)}, f32[4,128,128]{2,1,0:T(8,128)S(1)}, u32[]{:S(2)}, u32[]{:S(2)}) collective-permute-start(f32[4,128,128]{2,1,0:T(8,128)S(1)} %get-tuple-element.69), channel_id=1, source_target_pairs={{1,2},{3,4},{5,6},{7,8},{9,10},{11,12},{13,14},{15,16},{17,18},{19... | collective-permute-start | bytes 786440 | tf_op jit(solution)/shard_map/ppermute | solution.py:863
  33.7 9.5 %inner_step.1 = (bf16[2048,1024]{1,0:T(8,128)(2,1)S(1)}, bf16[8,512,512]{2,1,0:T(8,128)(2,1)S(1)}, f32[4,2048,128]{2,1,0:T(8,128)S(1)}) custom-call(s32[1]{0:T(128)} %bitcast.ocean, s32[1]{0:T(128)} %bitcast.9.elem, bf16[2048,1024]{1,0:T(8,128)(2,1)S(1)} %copy-done.15, bf16[512,1024]{1,0:T(8,128)(2,1)S(1)} %get-tuple-element.65.ue, s32[4,128]{1,0:T(4,128)S(1)} %bitcast.31, ...), custom_call_target="tpu_custom_call" | custom-call | flops 10000000000 | bytes 10485760 | tf_op jit(solution)/shard_map/inner_step/pallas_call | solution.py:456
  43.3 0.0 collective-permute-done.19.from_core
  43.3 0.0 collective-permute-done.20.from_chip
  43.3 4.4 %second_step.1 = f32[4,2048,128]{2,1,0:T(8,128)} custom-call(s32[1]{0:T(128)} %bitcast.ocean, s32[1]{0:T(128)} %bitcast.1.dom, f32[4,2048,128]{2,1,0:T(8,128)S(1)} %get-tuple-element.66.xv, bf16[2048,1024]{1,0:T(8,128)(2,1)S(1)} %get-tuple-element.67.u, f32[4,128,128]{2,1,0:T(8,128)S(1)} %collective-permute-done.19.from_core, ...), custom_call_target="tpu_custom_call", output_to_operand_aliasing={{}: (10, {})} | custom-call | flops 10000000000 | bytes 12582912 | tf_op jit(solution)/shard_map/second_step/pallas_call | solution.py:605
  47.6 0.0 collective-permute-done.14
  47.7 0.0 collective-permute-done.15
  47.7 0.0 collective-permute-done.16
  47.7 0.1 finish_ocean.1
  (14 shorter events, 0.1 us)
Async XLA Ops:
  0.6 21.1 %copy-start.2 = (f32[1,32,128,128]{3,2,1,0:T(8,128)S(1)}, f32[1,32,128,128]{3,2,1,0:T(8,128)}, u32[]{:S(2)}) copy-start(f32[1,32,128,128]{3,2,1,0:T(8,128)} %param.33) | copy-start | bytes 6291460
  0.7 21.1 %copy-start.8 = (f32[1,16,128]{2,1,0:T(8,128)S(1)}, f32[1,16,128]{2,1,0:T(8,128)}, u32[]{:S(2)}) copy-start(f32[1,16,128]{2,1,0:T(8,128)} %param.21) | copy-start | bytes 24580
  0.7 21.1 %copy-start.12 = (s32[1,32,1]{1,2,0:T(1,128)S(1)}, s32[1,32,1]{1,2,0:T(1,128)}, u32[]{:S(2)}) copy-start(s32[1,32,1]{1,2,0:T(1,128)} %param.30) | copy-start | bytes 388
  0.7 21.1 %copy-start.13 = (s32[1,32]{1,0:T(1,128)S(1)}, s32[1,32]{1,0:T(1,128)}, u32[]{:S(2)}) copy-start(s32[1,32]{1,0:T(1,128)} %param.31) | copy-start | bytes 388
  0.7 21.1 %copy-start.14 = (s32[1,32]{1,0:T(1,128)S(1)}, s32[1,32]{1,0:T(1,128)}, u32[]{:S(2)}) copy-start(s32[1,32]{1,0:T(1,128)} %param.32) | copy-start | bytes 388
  1.4 7.6 %collective-permute-start.4 = (f32[4,1024]{1,0:T(4,128)}, f32[4,1024]{1,0:T(4,128)S(1)}, u32[]{:S(2)}, u32[]{:S(2)}) collective-permute-start(f32[4,1024]{1,0:T(4,128)} %top_rows.1), channel_id=1, source_target_pairs={{24,0},{25,1},{26,2},{27,3},{28,4},{29,5},{30,6},{31,7}} | collective-permute-start | bytes 49160 | tf_op jit(solution)/shard_map/ppermute | solution.py:820
  2.0 7.0 %collective-permute-start.5 = (f32[4,1024]{1,0:T(4,128)}, f32[4,1024]{1,0:T(4,128)S(1)}, u32[]{:S(2)}, u32[]{:S(2)}) collective-permute-start(f32[4,1024]{1,0:T(4,128)} %top_rows.1), channel_id=1, source_target_pairs={{24,8},{25,9},{26,10},{27,11},{28,12},{29,13},{30,14},{31,15}} | collective-permute-start | bytes 49160 | tf_op jit(solution)/shard_map/ppermute | solution.py:820
  2.7 6.9 %collective-permute-start.6 = (f32[4,1024]{1,0:T(4,128)}, f32[4,1024]{1,0:T(4,128)S(1)}, u32[]{:S(2)}, u32[]{:S(2)}) collective-permute-start(f32[4,1024]{1,0:T(4,128)} %top_rows.1), channel_id=1, source_target_pairs={{24,16},{25,17},{26,18},{27,19},{28,20},{29,21},{30,22},{31,23}} | collective-permute-start | bytes 49160 | tf_op jit(solution)/shard_map/ppermute | solution.py:820
  9.6 5.0 %collective-permute-start.7 = (f32[4,1024]{1,0:T(4,128)S(1)}, f32[4,1024]{1,0:T(4,128)S(1)}, u32[]{:S(2)}, u32[]{:S(2)}) collective-permute-start(f32[4,1024]{1,0:T(4,128)S(1)} %add_add_fusion.refs_0_), channel_id=1, source_target_pairs={{0,2},{1,3},{2,0},{3,1},{4,6},{5,7},{6,4},{7,5},{8,10},{9,11},{10,... | collective-permute-start | bytes 49160 | tf_op jit(solution)/shard_map/ppermute | solution.py:825
  11.4 8.6 %collective-permute-start.8 = (f32[4,1024]{1,0:T(4,128)S(1)}, f32[4,1024]{1,0:T(4,128)S(1)}, u32[]{:S(2)}, u32[]{:S(2)}) collective-permute-start(f32[4,1024]{1,0:T(4,128)S(1)} %add_add_fusion.refs_0_), channel_id=1, source_target_pairs={{0,4},{1,5},{2,6},{3,7},{4,0},{5,1},{6,2},{7,3},{8,12},{9,13},{10,... | collective-permute-start | bytes 49160 | tf_op jit(solution)/shard_map/ppermute | solution.py:825
  14.0 6.1 %collective-permute-start.9 = (f32[4,1024]{1,0:T(4,128)S(1)}, f32[4,1024]{1,0:T(4,128)S(1)}, u32[]{:S(2)}, u32[]{:S(2)}) collective-permute-start(f32[4,1024]{1,0:T(4,128)S(1)} %add_add_fusion.refs_0_), channel_id=1, source_target_pairs={{0,6},{1,7},{2,4},{3,5},{4,2},{5,3},{6,0},{7,1},{8,14},{9,15},{10,... | collective-permute-start | bytes 49160 | tf_op jit(solution)/shard_map/ppermute | solution.py:825
  14.1 6.5 %collective-permute-start.10 = (f32[4,1024]{1,0:T(4,128)S(1)}, f32[4,1024]{1,0:T(4,128)S(1)}, u32[]{:S(2)}, u32[]{:S(2)}) collective-permute-start(f32[4,1024]{1,0:T(4,128)S(1)} %add_add_fusion.refs_0_), channel_id=1, source_target_pairs={{0,1},{1,0},{2,3},{3,2},{4,5},{5,4},{6,7},{7,6},{8,9},{9,8},{10,11... | collective-permute-start | bytes 49160 | tf_op jit(solution)/shard_map/ppermute | solution.py:826
  14.1 13.5 %collective-permute-start.17 = (f32[4,128,128]{2,1,0:T(8,128)}, f32[4,128,128]{2,1,0:T(8,128)S(1)}, u32[]{:S(2)}, u32[]{:S(2)}) collective-permute-start(f32[4,128,128]{2,1,0:T(8,128)} %get-tuple-element.61), channel_id=1, source_target_pairs={{0,1},{1,0},{2,3},{3,2},{4,5},{5,4},{6,7},{7,6},{8,9},{9,8},{10,11... | collective-permute-start | bytes 786440 | tf_op jit(solution)/shard_map/ppermute | solution.py:827
  14.6 13.2 %collective-permute-start.18 = (f32[4,128,128]{2,1,0:T(8,128)}, f32[4,128,128]{2,1,0:T(8,128)S(1)}, u32[]{:S(2)}, u32[]{:S(2)}) collective-permute-start(f32[4,128,128]{2,1,0:T(8,128)} %get-tuple-element.62), channel_id=1, source_target_pairs={{1,2},{3,4},{5,6},{7,8},{9,10},{11,12},{13,14},{15,16},{17,18},{19... | collective-permute-start | bytes 786440 | tf_op jit(solution)/shard_map/ppermute | solution.py:828
  20.0 1.2 %collective-permute-start.11 = (f32[4,1024]{1,0:T(4,128)S(1)}, f32[4,1024]{1,0:T(4,128)S(1)}, u32[]{:S(2)}, u32[]{:S(2)}) collective-permute-start(f32[4,1024]{1,0:T(4,128)S(1)} %collective-permute-done.7.refs_1_), channel_id=1, source_target_pairs={{0,1},{1,0},{2,3},{3,2},{4,5},{5,4},{6,7},{7,6},{8,9},{9,8},{10,11... | collective-permute-start | bytes 49160 | tf_op jit(solution)/shard_map/ppermute | solution.py:826
  20.1 1.3 %collective-permute-start.12 = (f32[4,1024]{1,0:T(4,128)S(1)}, f32[4,1024]{1,0:T(4,128)S(1)}, u32[]{:S(2)}, u32[]{:S(2)}) collective-permute-start(f32[4,1024]{1,0:T(4,128)S(1)} %collective-permute-done.8.refs_2_), channel_id=1, source_target_pairs={{0,1},{1,0},{2,3},{3,2},{4,5},{5,4},{6,7},{7,6},{8,9},{9,8},{10,11... | collective-permute-start | bytes 49160 | tf_op jit(solution)/shard_map/ppermute | solution.py:826
  20.6 1.2 %collective-permute-start.13 = (f32[4,1024]{1,0:T(4,128)S(1)}, f32[4,1024]{1,0:T(4,128)S(1)}, u32[]{:S(2)}, u32[]{:S(2)}) collective-permute-start(f32[4,1024]{1,0:T(4,128)S(1)} %collective-permute-done.9.refs_3_), channel_id=1, source_target_pairs={{0,1},{1,0},{2,3},{3,2},{4,5},{5,4},{6,7},{7,6},{8,9},{9,8},{10,11... | collective-permute-start | bytes 49160 | tf_op jit(solution)/shard_map/ppermute | solution.py:826
  21.8 0.8 %copy-start.16 = (f32[4,16,128]{2,1,0:T(8,128)S(1)}, f32[4,16,128]{2,1,0:T(8,128)}, u32[]{:S(2)}) copy-start(f32[4,16,128]{2,1,0:T(8,128)} %get-tuple-element.58.refs_10_) | copy-start | bytes 98308
  22.6 5.2 %copy-start = (f32[1,4,80,1024]{3,2,1,0:T(8,128)S(1)}, f32[1,4,80,1024]{3,2,1,0:T(8,128)}, u32[]{:S(2)}) copy-start(f32[1,4,80,1024]{3,2,1,0:T(8,128)} %param.25) | copy-start | bytes 3932164
  22.6 5.2 %copy-start.1 = (s32[1,1024]{1,0:T(1,128)S(1)}, s32[1,1024]{1,0:T(1,128)}, u32[]{:S(2)}) copy-start(s32[1,1024]{1,0:T(1,128)} %sea.3) | copy-start | bytes 12292
  22.6 5.2 %copy-start.3 = (f32[128,128]{1,0:T(8,128)S(1)}, f32[128,128]{1,0:T(8,128)}, u32[]{:S(2)}) copy-start(f32[128,128]{1,0:T(8,128)} %vertical.5) | copy-start | bytes 196612
  22.6 5.2 %copy-start.4 = (f32[80,80]{1,0:T(8,128)S(1)}, f32[80,80]{1,0:T(8,128)}, u32[]{:S(2)}) copy-start(f32[80,80]{1,0:T(8,128)} %overt.1) | copy-start | bytes 76804
  22.6 5.2 %copy-start.5 = (f32[4,16,16]{2,1,0:T(8,128)S(1)}, f32[4,16,16]{2,1,0:T(8,128)}, u32[]{:S(2)}) copy-start(f32[4,16,16]{2,1,0:T(8,128)} %param.23) | copy-start | bytes 12292
  22.6 5.2 %copy-start.6 = (s32[1,6,1024]{2,0,1:T(1,128)S(1)}, s32[1,6,1024]{2,0,1:T(1,128)}, u32[]{:S(2)}) copy-start(s32[1,6,1024]{2,0,1:T(1,128)} %param.26) | copy-start | bytes 73732
  22.6 5.2 %copy-start.7 = (f32[1,6,1024]{2,0,1:T(1,128)S(1)}, f32[1,6,1024]{2,0,1:T(1,128)}, u32[]{:S(2)}) copy-start(f32[1,6,1024]{2,0,1:T(1,128)} %param.27) | copy-start | bytes 73732
  22.6 5.2 %copy-start.9 = (f32[16,16]{1,0:T(8,128)S(1)}, f32[16,16]{1,0:T(8,128)}, u32[]{:S(2)}) copy-start(f32[16,16]{1,0:T(8,128)} %stiffness.3) | copy-start | bytes 3076
  22.6 5.2 %copy-start.10 = (f32[1,16,128]{2,1,0:T(8,128)S(1)}, f32[1,16,128]{2,1,0:T(8,128)}, u32[]{:S(2)}) copy-start(f32[1,16,128]{2,1,0:T(8,128)} %param.20) | copy-start | bytes 24580
  22.6 5.2 %copy-start.11 = (s32[1,4,128]{2,1,0:T(4,128)S(1)}, s32[1,4,128]{2,1,0:T(4,128)}, u32[]{:S(2)}) copy-start(s32[1,4,128]{2,1,0:T(4,128)} %param.19) | copy-start | bytes 6148
  22.6 5.2 %copy-start.15 = (bf16[2048,1024]{1,0:T(8,128)(2,1)S(1)}, bf16[2048,1024]{1,0:T(8,128)(2,1)}, u32[]{:S(2)}) copy-start(bf16[2048,1024]{1,0:T(8,128)(2,1)} %get-tuple-element.60.xt) | copy-start | bytes 12582916
  24.9 22.8 %collective-permute-start.14 = (f32[64,4,128]{2,1,0:T(4,128)S(1)}, f32[64,4,128]{2,1,0:T(4,128)S(1)}, u32[]{:S(2)}, u32[]{:S(2)}) collective-permute-start(f32[64,4,128]{2,1,0:T(4,128)S(1)} %get-tuple-element.59), channel_id=1, source_target_pairs={{0,24},{1,25},{2,26},{3,27},{4,28},{5,29},{6,30},{7,31}} | collective-permute-start | bytes 393224 | tf_op jit(solution)/shard_map/ppermute | solution.py:845
  25.5 22.1 %collective-permute-start.15 = (f32[64,4,128]{2,1,0:T(4,128)S(1)}, f32[64,4,128]{2,1,0:T(4,128)S(1)}, u32[]{:S(2)}, u32[]{:S(2)}) collective-permute-start(f32[64,4,128]{2,1,0:T(4,128)S(1)} %get-tuple-element.59), channel_id=1, source_target_pairs={{8,24},{9,25},{10,26},{11,27},{12,28},{13,29},{14,30},{15,31}} | collective-permute-start | bytes 393224 | tf_op jit(solution)/shard_map/ppermute | solution.py:845
  26.2 21.5 %collective-permute-start.16 = (f32[64,4,128]{2,1,0:T(4,128)S(1)}, f32[64,4,128]{2,1,0:T(4,128)S(1)}, u32[]{:S(2)}, u32[]{:S(2)}) collective-permute-start(f32[64,4,128]{2,1,0:T(4,128)S(1)} %get-tuple-element.59), channel_id=1, source_target_pairs={{16,24},{17,25},{18,26},{19,27},{20,28},{21,29},{22,30},{23,31}} | collective-permute-start | bytes 393224 | tf_op jit(solution)/shard_map/ppermute | solution.py:845
  29.8 13.5 %collective-permute-start.19 = (f32[4,128,128]{2,1,0:T(8,128)S(1)}, f32[4,128,128]{2,1,0:T(8,128)S(1)}, u32[]{:S(2)}, u32[]{:S(2)}) collective-permute-start(f32[4,128,128]{2,1,0:T(8,128)S(1)} %get-tuple-element.68), channel_id=1, source_target_pairs={{0,1},{1,0},{2,3},{3,2},{4,5},{5,4},{6,7},{7,6},{8,9},{9,8},{10,11... | collective-permute-start | bytes 786440 | tf_op jit(solution)/shard_map/ppermute | solution.py:864
  29.9 13.4 %collective-permute-start.20 = (f32[4,128,128]{2,1,0:T(8,128)S(1)}, f32[4,128,128]{2,1,0:T(8,128)S(1)}, u32[]{:S(2)}, u32[]{:S(2)}) collective-permute-start(f32[4,128,128]{2,1,0:T(8,128)S(1)} %get-tuple-element.69), channel_id=1, source_target_pairs={{1,2},{3,4},{5,6},{7,8},{9,10},{11,12},{13,14},{15,16},{17,18},{19... | collective-permute-start | bytes 786440 | tf_op jit(solution)/shard_map/ppermute | solution.py:863

commit v5 on v4

--- a/solution.py
+++ b/solution.py
@@ -372,32 +372,24 @@
         u[pl.ds(rows - edge, edge), :] = ue[pl.ds(edge, edge), :]
         last_lane = lax.broadcasted_iota(jnp.int32, (edge, LANES), 1) == LANES - 1
 
-        @pl.loop(1, blocks - 1, step=3)
-        def _(start_of):
-            for i in range(3):
-                b = start_of + i
-                first = pl.multiple_of(b * edge, edge)
-                element = b * 2 * GROUP
-
-                def store(f, value):
-                    value = value + jnp.where(last_lane, columns(ft.at[f], element, points), 0.0)
-                    put_split(u, pl.ds(first, edge), f, fields, value)
-
-                window = xt.at[pl.ds(pl.multiple_of(first - LANES, LANES), 4 * LANES)]
-                advance(window, table.at[b], wa, mt, element, points, store, range(fields))
-                build_table(b + 1, table, b + 1, cx, nt, sides, points)
-
-        @pl.loop(1, blocks - 1, step=3)
-        def _(start_of):
-            for i in range(3):
-                b = start_of + i
-                first = pl.multiple_of(b * edge, edge)
-
-                def store(f, value):
-                    xv[f, pl.ds(first, edge), :] = value
-
-                window = u.at[pl.ds(pl.multiple_of(first - LANES, LANES), 4 * LANES)]
-                advance(window, table.at[b], wa, mt, b * 2 * GROUP, points, store, range(fields))
+        for b in range(1, blocks - 1):
+            element = b * 2 * GROUP
+
+            def store(f, value):
+                value = value + jnp.where(last_lane, columns(ft.at[f], element, points), 0.0)
+                put_split(u, pl.ds(b * edge, edge), f, fields, value)
+
+            build_table(b + 1, table, b + 1, cx, nt, sides, points)
+            window = xt.at[pl.ds(b * edge - LANES, 4 * LANES)]
+            advance(window, table.at[b], wa, mt, element, points, store, range(fields))
+
+        for b in range(1, blocks - 1):
+
+            def store(f, value):
+                xv[f, pl.ds(b * edge, edge), :] = value
+
+            window = u.at[pl.ds(b * edge - LANES, 4 * LANES)]
+            advance(window, table.at[b], wa, mt, b * 2 * GROUP, points, store, range(fields))
 
 
 def ocean_part(dom, base, load, from_core, from_chip, nbr, diff, sea, overt, fresh, ov, ext, res, vert, r_sem):

time: 48.4 us -> 47.7 us (0.986)
  Pallas kernels: 23.8 us -> 23 us
    pallas_call x1, Pallas kernels: 9.52 us -> 8.98 us  [inner_step(): pl.pallas_call(inner_kernel, out_shape=(jax.ShapeDtypeStruct((rows, width...]
  transfers between devices with their start and end apart: 17 -> 17, of which waited for: 5 -> 5; matrix products, arithmetic and copies ran while one was open for 0% -> 0% of each run, Pallas kernels for 48% -> 47%
where the time goes in v5:
time: 47.7 us; the launch traced here: 47.2 us
  Pallas kernels  23 us (48%)
  starting transfers between devices  20.2 us (42%)
  waiting for transfers between devices  1.92 us (4%)
  between operations  1.22 us (3%)
  local copies, waits for them, and re-layouts  0.83 us (2%)
    pallas_call x1, Pallas kernels, inner_step(): pl.pallas_call(inner_kernel, out_shape=(jax.ShapeDtypeStruct((rows, width...  8.98 us
    ppermute x1, starting transfers between devices, local(): from_chip = lax.ppermute(to_chip, both, all_chips)  5.42 us
    pallas_call x1, Pallas kernels, turn(): pl.pallas_call(turn_kernel, out_shape=(jax.ShapeDtypeStruct((rows, 2 * fi...  4.99 us
    ppermute x3, starting transfers between devices, local(): lax.ppermute(got, 'dom', shifted(s))  4.45 us
    pallas_call x1, Pallas kernels, second_step(): pl.pallas_call(second_kernel, out_shape=jax.ShapeDtypeStruct((fields, lev...  4.18 us
    ppermute x1, starting transfers between devices, local(): from_chip2 = lax.ppermute(to_chip, both, atm_chips)  3.84 us
    ppermute x3, starting transfers between devices, local(): parts = [lax.ppermute(sent, both, to_ocean(c)) for c in range(live)]  2.64 us
    ppermute x3, starting transfers between devices, local(): brought = [lax.ppermute(top, both, from_ocean(c)) for c in range(live)]  2.62 us
  transfers between devices with their start and end apart: 17, of which 5 were waited for; matrix products, arithmetic and copies ran while one was open for 0% of the time, Pallas kernels for 47%

profile of v5, /device:TPU:4, one launch (start us, length us, event | category | flops | bytes accessed | tf_op | source)
XLA Modules:
  0.0 47.2 jit_solution(16000102979451010212)
XLA Ops:
  0.6 0.0 copy-start.2
  0.7 0.0 copy-start.8
  0.7 0.0 copy-start.12
  0.7 0.0 copy-start.13
  0.7 0.0 copy-start.14
  0.7 0.7 %top_rows.1 = f32[4,1024]{1,0:T(4,128)} custom-call(s32[1]{0:T(128)} %bitcast.ocean, f32[4,80,1024]{2,1,0:T(8,128)} %bitcast.18), custom_call_target="tpu_custom_call" | custom-call | bytes 65536 | tf_op jit(solution)/shard_map/top_rows/pallas_call | solution.py:641
  1.4 0.7 %collective-permute-start.4 = (f32[4,1024]{1,0:T(4,128)}, f32[4,1024]{1,0:T(4,128)S(1)}, u32[]{:S(2)}, u32[]{:S(2)}) collective-permute-start(f32[4,1024]{1,0:T(4,128)} %top_rows.1), channel_id=1, source_target_pairs={{24,0},{25,1},{26,2},{27,3},{28,4},{29,5},{30,6},{31,7}} | collective-permute-start | bytes 49160 | tf_op jit(solution)/shard_map/ppermute | solution.py:812
  2.0 0.7 %collective-permute-start.5 = (f32[4,1024]{1,0:T(4,128)}, f32[4,1024]{1,0:T(4,128)S(1)}, u32[]{:S(2)}, u32[]{:S(2)}) collective-permute-start(f32[4,1024]{1,0:T(4,128)} %top_rows.1), channel_id=1, source_target_pairs={{24,8},{25,9},{26,10},{27,11},{28,12},{29,13},{30,14},{31,15}} | collective-permute-start | bytes 49160 | tf_op jit(solution)/shard_map/ppermute | solution.py:812
  2.7 1.3 %collective-permute-start.6 = (f32[4,1024]{1,0:T(4,128)}, f32[4,1024]{1,0:T(4,128)S(1)}, u32[]{:S(2)}, u32[]{:S(2)}) collective-permute-start(f32[4,1024]{1,0:T(4,128)} %top_rows.1), channel_id=1, source_target_pairs={{24,16},{25,17},{26,18},{27,19},{28,20},{29,21},{30,22},{31,23}} | collective-permute-start | bytes 49160 | tf_op jit(solution)/shard_map/ppermute | solution.py:812
  4.0 5.0 %turn_state.1 = (bf16[2048,1024]{1,0:T(8,128)(2,1)}, f32[4,128,128]{2,1,0:T(8,128)}, f32[4,128,128]{2,1,0:T(8,128)}, f32[4,16,128]{2,1,0:T(8,128)}) custom-call(s32[1]{0:T(128)} %bitcast.ocean, s32[1]{0:T(128)} %bitcast.1.dom, f32[4,2048,128]{2,1,0:T(8,128)} %bitcast.36, f32[4,80,1024]{2,1,0:T(8,128)} %bitcast.19), custom_call_target="tpu_custom_call" | custom-call | flops 2000000000 | bytes 9437184 | tf_op jit(solution)/shard_map/turn_state/pallas_call | solution.py:132
  9.0 0.0 collective-permute-done.4
  9.0 0.0 collective-permute-done.5
  9.0 0.6 %collective-permute-done.6 = f32[4,1024]{1,0:T(4,128)S(1)} collective-permute-done((f32[4,1024]{1,0:T(4,128)}, f32[4,1024]{1,0:T(4,128)S(1)}, u32[]{:S(2)}, u32[]{:S(2)}) %collective-permute-start.6) | collective-permute-done | bytes 16416 | tf_op jit(solution)/shard_map/ppermute | solution.py:812
  9.6 1.8 %collective-permute-start.7 = (f32[4,1024]{1,0:T(4,128)S(1)}, f32[4,1024]{1,0:T(4,128)S(1)}, u32[]{:S(2)}, u32[]{:S(2)}) collective-permute-start(f32[4,1024]{1,0:T(4,128)S(1)} %add_add_fusion.refs_0_), channel_id=1, source_target_pairs={{0,2},{1,3},{2,0},{3,1},{4,6},{5,7},{6,4},{7,5},{8,10},{9,11},{10,... | collective-permute-start | bytes 49160 | tf_op jit(solution)/shard_map/ppermute | solution.py:817
  11.4 2.6 %collective-permute-start.8 = (f32[4,1024]{1,0:T(4,128)S(1)}, f32[4,1024]{1,0:T(4,128)S(1)}, u32[]{:S(2)}, u32[]{:S(2)}) collective-permute-start(f32[4,1024]{1,0:T(4,128)S(1)} %add_add_fusion.refs_0_), channel_id=1, source_target_pairs={{0,4},{1,5},{2,6},{3,7},{4,0},{5,1},{6,2},{7,3},{8,12},{9,13},{10,... | collective-permute-start | bytes 49160 | tf_op jit(solution)/shard_map/ppermute | solution.py:817
  14.0 0.1 collective-permute-start.9
  14.1 0.0 collective-permute-start.10
  14.1 0.5 %collective-permute-start.17 = (f32[4,128,128]{2,1,0:T(8,128)}, f32[4,128,128]{2,1,0:T(8,128)S(1)}, u32[]{:S(2)}, u32[]{:S(2)}) collective-permute-start(f32[4,128,128]{2,1,0:T(8,128)} %get-tuple-element.61), channel_id=1, source_target_pairs={{0,1},{1,0},{2,3},{3,2},{4,5},{5,4},{6,7},{7,6},{8,9},{9,8},{10,11... | collective-permute-start | bytes 786440 | tf_op jit(solution)/shard_map/ppermute | solution.py:819
  14.6 0.0 collective-permute-done.7.refs_1_
  14.6 5.4 %collective-permute-start.18 = (f32[4,128,128]{2,1,0:T(8,128)}, f32[4,128,128]{2,1,0:T(8,128)S(1)}, u32[]{:S(2)}, u32[]{:S(2)}) collective-permute-start(f32[4,128,128]{2,1,0:T(8,128)} %get-tuple-element.62), channel_id=1, source_target_pairs={{1,2},{3,4},{5,6},{7,8},{9,10},{11,12},{13,14},{15,16},{17,18},{19... | collective-permute-start | bytes 786440 | tf_op jit(solution)/shard_map/ppermute | solution.py:820
  20.0 0.0 collective-permute-done.8.refs_2_
  20.0 0.1 collective-permute-start.11
  20.1 0.0 collective-permute-done.9.refs_3_
  20.1 0.5 %collective-permute-start.12 = (f32[4,1024]{1,0:T(4,128)S(1)}, f32[4,1024]{1,0:T(4,128)S(1)}, u32[]{:S(2)}, u32[]{:S(2)}) collective-permute-start(f32[4,1024]{1,0:T(4,128)S(1)} %collective-permute-done.8.refs_2_), channel_id=1, source_target_pairs={{0,1},{1,0},{2,3},{3,2},{4,5},{5,4},{6,7},{7,6},{8,9},{9,8},{10,11... | collective-permute-start | bytes 49160 | tf_op jit(solution)/shard_map/ppermute | solution.py:818
  20.6 0.0 collective-permute-done.10.refs_4_
  20.6 0.1 collective-permute-start.13
  20.7 0.6 %collective-permute-done.11.refs_5_ = f32[4,1024]{1,0:T(4,128)S(1)} collective-permute-done((f32[4,1024]{1,0:T(4,128)S(1)}, f32[4,1024]{1,0:T(4,128)S(1)}, u32[]{:S(2)}, u32[]{:S(2)}) %collective-permute-start.11) | collective-permute-done | bytes 16416 | tf_op jit(solution)/shard_map/ppermute | solution.py:818
  21.3 0.2 collective-permute-done.12.refs_6_
  21.4 0.3 collective-permute-done.13.refs_7_
  21.8 0.0 copy-done.2
  21.8 0.0 copy-done.8
  21.8 0.0 copy-done.12
  21.8 0.0 copy-done.13
  21.8 0.0 copy-done.14
  21.8 0.0 copy-start.16
  21.8 0.7 %copy-done.16 = f32[4,16,128]{2,1,0:T(8,128)S(1)} copy-done((f32[4,16,128]{2,1,0:T(8,128)S(1)}, f32[4,16,128]{2,1,0:T(8,128)}, u32[]{:S(2)}) %copy-start.16) | copy-done | bytes 32792
  22.6 0.0 copy-start.5
  22.6 0.0 copy-start.6
  22.6 0.0 copy-start.7
  22.6 0.0 copy-start.9
  22.6 0.0 copy-start.10
  22.6 0.0 copy-start.11
  22.6 0.0 copy-start.15
  22.7 2.2 %fluxes.1 = (f32[4,16,128]{2,1,0:T(8,128)S(1)}, f32[64,4,128]{2,1,0:T(4,128)S(1)}, f32[4,80,1024]{2,1,0:T(8,128)}) custom-call(s32[1]{0:T(128)} %bitcast.ocean, s32[1]{0:T(128)} %bitcast.1.dom, s32[32]{0:T(128)S(1)} %bitcast.32, s32[32]{0:T(128)S(1)} %bitcast.33, s32[32]{0:T(128)S(1)} %bitcast.34, f32[4,1024]{1,0:T(4,128)S(1)} %add_add_fusion.refs_0_, ...), custom_call_target="tpu_custom_call" | custom-call | flops 2500000000 | bytes 2097152 | tf_op jit(solution)/shard_map/fluxes/pallas_call | solution.py:529
  24.9 0.7 %collective-permute-start.14 = (f32[64,4,128]{2,1,0:T(4,128)S(1)}, f32[64,4,128]{2,1,0:T(4,128)S(1)}, u32[]{:S(2)}, u32[]{:S(2)}) collective-permute-start(f32[64,4,128]{2,1,0:T(4,128)S(1)} %get-tuple-element.59), channel_id=1, source_target_pairs={{0,24},{1,25},{2,26},{3,27},{4,28},{5,29},{6,30},{7,31}} | collective-permute-start | bytes 393224 | tf_op jit(solution)/shard_map/ppermute | solution.py:837
  25.5 0.7 %collective-permute-start.15 = (f32[64,4,128]{2,1,0:T(4,128)S(1)}, f32[64,4,128]{2,1,0:T(4,128)S(1)}, u32[]{:S(2)}, u32[]{:S(2)}) collective-permute-start(f32[64,4,128]{2,1,0:T(4,128)S(1)} %get-tuple-element.59), channel_id=1, source_target_pairs={{8,24},{9,25},{10,26},{11,27},{12,28},{13,29},{14,30},{15,31}} | collective-permute-start | bytes 393224 | tf_op jit(solution)/shard_map/ppermute | solution.py:837
  26.2 1.3 %collective-permute-start.16 = (f32[64,4,128]{2,1,0:T(4,128)S(1)}, f32[64,4,128]{2,1,0:T(4,128)S(1)}, u32[]{:S(2)}, u32[]{:S(2)}) collective-permute-start(f32[64,4,128]{2,1,0:T(4,128)S(1)} %get-tuple-element.59), channel_id=1, source_target_pairs={{16,24},{17,25},{18,26},{19,27},{20,28},{21,29},{22,30},{23,31}} | collective-permute-start | bytes 393224 | tf_op jit(solution)/shard_map/ppermute | solution.py:837
  27.5 0.0 collective-permute-done.17.from_core
  27.5 0.2 collective-permute-done.18.from_chip
  27.7 0.0 copy-done
  27.7 0.0 copy-done.1
  27.7 0.0 copy-done.3
  27.8 0.0 copy-done.4
  27.8 2.0 %edge_step.1 = (bf16[512,1024]{1,0:T(8,128)(2,1)S(1)}, f32[4,128,128]{2,1,0:T(8,128)S(1)}, f32[4,128,128]{2,1,0:T(8,128)S(1)}, f32[4,80,1024]{2,1,0:T(8,128)}, f32[4,2048,128]{2,1,0:T(8,128)}) custom-call(s32[1]{0:T(128)} %bitcast.ocean, s32[1]{0:T(128)} %bitcast.1.dom, s32[1]{0:T(128)} %bitcast.9.elem, ...), custom_call_target="tpu_custom_call", output_to_operand_aliasing={{3}: (18, {})} | custom-call | flops 4000000000 | bytes 3145728 | tf_op jit(solution)/shard_map/edge_step/pallas_call | solution.py:318
  29.8 0.1 collective-permute-start.19
  29.9 3.8 %collective-permute-start.20 = (f32[4,128,128]{2,1,0:T(8,128)S(1)}, f32[4,128,128]{2,1,0:T(8,128)S(1)}, u32[]{:S(2)}, u32[]{:S(2)}) collective-permute-start(f32[4,128,128]{2,1,0:T(8,128)S(1)} %get-tuple-element.69), channel_id=1, source_target_pairs={{1,2},{3,4},{5,6},{7,8},{9,10},{11,12},{13,14},{15,16},{17,18},{19... | collective-permute-start | bytes 786440 | tf_op jit(solution)/shard_map/ppermute | solution.py:855
  33.7 9.0 %inner_step.1 = (bf16[2048,1024]{1,0:T(8,128)(2,1)S(1)}, bf16[8,512,512]{2,1,0:T(8,128)(2,1)S(1)}, f32[4,2048,128]{2,1,0:T(8,128)S(1)}) custom-call(s32[1]{0:T(128)} %bitcast.ocean, s32[1]{0:T(128)} %bitcast.9.elem, bf16[2048,1024]{1,0:T(8,128)(2,1)S(1)} %copy-done.15, bf16[512,1024]{1,0:T(8,128)(2,1)S(1)} %get-tuple-element.65.ue, s32[4,128]{1,0:T(4,128)S(1)} %bitcast.31, ...), custom_call_target="tpu_custom_call" | custom-call | flops 10000000000 | bytes 10485760 | tf_op jit(solution)/shard_map/inner_step/pallas_call | solution.py:448
  42.7 0.0 collective-permute-done.19.from_core
  42.7 0.0 collective-permute-done.20.from_chip
  42.7 4.2 %second_step.1 = f32[4,2048,128]{2,1,0:T(8,128)} custom-call(s32[1]{0:T(128)} %bitcast.ocean, s32[1]{0:T(128)} %bitcast.1.dom, f32[4,2048,128]{2,1,0:T(8,128)S(1)} %get-tuple-element.66.xv, bf16[2048,1024]{1,0:T(8,128)(2,1)S(1)} %get-tuple-element.67.u, f32[4,128,128]{2,1,0:T(8,128)S(1)} %collective-permute-done.19.from_core, ...), custom_call_target="tpu_custom_call", output_to_operand_aliasing={{}: (10, {})} | custom-call | flops 10000000000 | bytes 12582912 | tf_op jit(solution)/shard_map/second_step/pallas_call | solution.py:597
  46.9 0.0 collective-permute-done.14
  46.9 0.0 collective-permute-done.15
  46.9 0.0 collective-permute-done.16
  47.0 0.1 finish_ocean.1
  (14 shorter events, 0.1 us)
Async XLA Ops:
  0.6 21.1 %copy-start.2 = (f32[1,32,128,128]{3,2,1,0:T(8,128)S(1)}, f32[1,32,128,128]{3,2,1,0:T(8,128)}, u32[]{:S(2)}) copy-start(f32[1,32,128,128]{3,2,1,0:T(8,128)} %param.33) | copy-start | bytes 6291460
  0.7 21.1 %copy-start.8 = (f32[1,16,128]{2,1,0:T(8,128)S(1)}, f32[1,16,128]{2,1,0:T(8,128)}, u32[]{:S(2)}) copy-start(f32[1,16,128]{2,1,0:T(8,128)} %param.21) | copy-start | bytes 24580
  0.7 21.1 %copy-start.12 = (s32[1,32,1]{1,2,0:T(1,128)S(1)}, s32[1,32,1]{1,2,0:T(1,128)}, u32[]{:S(2)}) copy-start(s32[1,32,1]{1,2,0:T(1,128)} %param.30) | copy-start | bytes 388
  0.7 21.1 %copy-start.13 = (s32[1,32]{1,0:T(1,128)S(1)}, s32[1,32]{1,0:T(1,128)}, u32[]{:S(2)}) copy-start(s32[1,32]{1,0:T(1,128)} %param.31) | copy-start | bytes 388
  0.7 21.1 %copy-start.14 = (s32[1,32]{1,0:T(1,128)S(1)}, s32[1,32]{1,0:T(1,128)}, u32[]{:S(2)}) copy-start(s32[1,32]{1,0:T(1,128)} %param.32) | copy-start | bytes 388
  1.4 7.6 %collective-permute-start.4 = (f32[4,1024]{1,0:T(4,128)}, f32[4,1024]{1,0:T(4,128)S(1)}, u32[]{:S(2)}, u32[]{:S(2)}) collective-permute-start(f32[4,1024]{1,0:T(4,128)} %top_rows.1), channel_id=1, source_target_pairs={{24,0},{25,1},{26,2},{27,3},{28,4},{29,5},{30,6},{31,7}} | collective-permute-start | bytes 49160 | tf_op jit(solution)/shard_map/ppermute | solution.py:812
  2.0 7.0 %collective-permute-start.5 = (f32[4,1024]{1,0:T(4,128)}, f32[4,1024]{1,0:T(4,128)S(1)}, u32[]{:S(2)}, u32[]{:S(2)}) collective-permute-start(f32[4,1024]{1,0:T(4,128)} %top_rows.1), channel_id=1, source_target_pairs={{24,8},{25,9},{26,10},{27,11},{28,12},{29,13},{30,14},{31,15}} | collective-permute-start | bytes 49160 | tf_op jit(solution)/shard_map/ppermute | solution.py:812
  2.7 6.9 %collective-permute-start.6 = (f32[4,1024]{1,0:T(4,128)}, f32[4,1024]{1,0:T(4,128)S(1)}, u32[]{:S(2)}, u32[]{:S(2)}) collective-permute-start(f32[4,1024]{1,0:T(4,128)} %top_rows.1), channel_id=1, source_target_pairs={{24,16},{25,17},{26,18},{27,19},{28,20},{29,21},{30,22},{31,23}} | collective-permute-start | bytes 49160 | tf_op jit(solution)/shard_map/ppermute | solution.py:812
  9.6 5.0 %collective-permute-start.7 = (f32[4,1024]{1,0:T(4,128)S(1)}, f32[4,1024]{1,0:T(4,128)S(1)}, u32[]{:S(2)}, u32[]{:S(2)}) collective-permute-start(f32[4,1024]{1,0:T(4,128)S(1)} %add_add_fusion.refs_0_), channel_id=1, source_target_pairs={{0,2},{1,3},{2,0},{3,1},{4,6},{5,7},{6,4},{7,5},{8,10},{9,11},{10,... | collective-permute-start | bytes 49160 | tf_op jit(solution)/shard_map/ppermute | solution.py:817
  11.4 8.6 %collective-permute-start.8 = (f32[4,1024]{1,0:T(4,128)S(1)}, f32[4,1024]{1,0:T(4,128)S(1)}, u32[]{:S(2)}, u32[]{:S(2)}) collective-permute-start(f32[4,1024]{1,0:T(4,128)S(1)} %add_add_fusion.refs_0_), channel_id=1, source_target_pairs={{0,4},{1,5},{2,6},{3,7},{4,0},{5,1},{6,2},{7,3},{8,12},{9,13},{10,... | collective-permute-start | bytes 49160 | tf_op jit(solution)/shard_map/ppermute | solution.py:817
  14.0 6.1 %collective-permute-start.9 = (f32[4,1024]{1,0:T(4,128)S(1)}, f32[4,1024]{1,0:T(4,128)S(1)}, u32[]{:S(2)}, u32[]{:S(2)}) collective-permute-start(f32[4,1024]{1,0:T(4,128)S(1)} %add_add_fusion.refs_0_), channel_id=1, source_target_pairs={{0,6},{1,7},{2,4},{3,5},{4,2},{5,3},{6,0},{7,1},{8,14},{9,15},{10,... | collective-permute-start | bytes 49160 | tf_op jit(solution)/shard_map/ppermute | solution.py:817
  14.1 6.5 %collective-permute-start.10 = (f32[4,1024]{1,0:T(4,128)S(1)}, f32[4,1024]{1,0:T(4,128)S(1)}, u32[]{:S(2)}, u32[]{:S(2)}) collective-permute-start(f32[4,1024]{1,0:T(4,128)S(1)} %add_add_fusion.refs_0_), channel_id=1, source_target_pairs={{0,1},{1,0},{2,3},{3,2},{4,5},{5,4},{6,7},{7,6},{8,9},{9,8},{10,11... | collective-permute-start | bytes 49160 | tf_op jit(solution)/shard_map/ppermute | solution.py:818
  14.1 13.5 %collective-permute-start.17 = (f32[4,128,128]{2,1,0:T(8,128)}, f32[4,128,128]{2,1,0:T(8,128)S(1)}, u32[]{:S(2)}, u32[]{:S(2)}) collective-permute-start(f32[4,128,128]{2,1,0:T(8,128)} %get-tuple-element.61), channel_id=1, source_target_pairs={{0,1},{1,0},{2,3},{3,2},{4,5},{5,4},{6,7},{7,6},{8,9},{9,8},{10,11... | collective-permute-start | bytes 786440 | tf_op jit(solution)/shard_map/ppermute | solution.py:819
  14.6 13.2 %collective-permute-start.18 = (f32[4,128,128]{2,1,0:T(8,128)}, f32[4,128,128]{2,1,0:T(8,128)S(1)}, u32[]{:S(2)}, u32[]{:S(2)}) collective-permute-start(f32[4,128,128]{2,1,0:T(8,128)} %get-tuple-element.62), channel_id=1, source_target_pairs={{1,2},{3,4},{5,6},{7,8},{9,10},{11,12},{13,14},{15,16},{17,18},{19... | collective-permute-start | bytes 786440 | tf_op jit(solution)/shard_map/ppermute | solution.py:820
  20.0 1.2 %collective-permute-start.11 = (f32[4,1024]{1,0:T(4,128)S(1)}, f32[4,1024]{1,0:T(4,128)S(1)}, u32[]{:S(2)}, u32[]{:S(2)}) collective-permute-start(f32[4,1024]{1,0:T(4,128)S(1)} %collective-permute-done.7.refs_1_), channel_id=1, source_target_pairs={{0,1},{1,0},{2,3},{3,2},{4,5},{5,4},{6,7},{7,6},{8,9},{9,8},{10,11... | collective-permute-start | bytes 49160 | tf_op jit(solution)/shard_map/ppermute | solution.py:818
  20.1 1.3 %collective-permute-start.12 = (f32[4,1024]{1,0:T(4,128)S(1)}, f32[4,1024]{1,0:T(4,128)S(1)}, u32[]{:S(2)}, u32[]{:S(2)}) collective-permute-start(f32[4,1024]{1,0:T(4,128)S(1)} %collective-permute-done.8.refs_2_), channel_id=1, source_target_pairs={{0,1},{1,0},{2,3},{3,2},{4,5},{5,4},{6,7},{7,6},{8,9},{9,8},{10,11... | collective-permute-start | bytes 49160 | tf_op jit(solution)/shard_map/ppermute | solution.py:818
  20.6 1.2 %collective-permute-start.13 = (f32[4,1024]{1,0:T(4,128)S(1)}, f32[4,1024]{1,0:T(4,128)S(1)}, u32[]{:S(2)}, u32[]{:S(2)}) collective-permute-start(f32[4,1024]{1,0:T(4,128)S(1)} %collective-permute-done.9.refs_3_), channel_id=1, source_target_pairs={{0,1},{1,0},{2,3},{3,2},{4,5},{5,4},{6,7},{7,6},{8,9},{9,8},{10,11... | collective-permute-start | bytes 49160 | tf_op jit(solution)/shard_map/ppermute | solution.py:818
  21.8 0.8 %copy-start.16 = (f32[4,16,128]{2,1,0:T(8,128)S(1)}, f32[4,16,128]{2,1,0:T(8,128)}, u32[]{:S(2)}) copy-start(f32[4,16,128]{2,1,0:T(8,128)} %get-tuple-element.58.refs_10_) | copy-start | bytes 98308
  22.6 5.2 %copy-start = (f32[1,4,80,1024]{3,2,1,0:T(8,128)S(1)}, f32[1,4,80,1024]{3,2,1,0:T(8,128)}, u32[]{:S(2)}) copy-start(f32[1,4,80,1024]{3,2,1,0:T(8,128)} %param.25) | copy-start | bytes 3932164
  22.6 5.2 %copy-start.1 = (s32[1,1024]{1,0:T(1,128)S(1)}, s32[1,1024]{1,0:T(1,128)}, u32[]{:S(2)}) copy-start(s32[1,1024]{1,0:T(1,128)} %sea.3) | copy-start | bytes 12292
  22.6 5.2 %copy-start.3 = (f32[128,128]{1,0:T(8,128)S(1)}, f32[128,128]{1,0:T(8,128)}, u32[]{:S(2)}) copy-start(f32[128,128]{1,0:T(8,128)} %vertical.5) | copy-start | bytes 196612
  22.6 5.2 %copy-start.4 = (f32[80,80]{1,0:T(8,128)S(1)}, f32[80,80]{1,0:T(8,128)}, u32[]{:S(2)}) copy-start(f32[80,80]{1,0:T(8,128)} %overt.1) | copy-start | bytes 76804
  22.6 5.2 %copy-start.5 = (f32[4,16,16]{2,1,0:T(8,128)S(1)}, f32[4,16,16]{2,1,0:T(8,128)}, u32[]{:S(2)}) copy-start(f32[4,16,16]{2,1,0:T(8,128)} %param.23) | copy-start | bytes 12292
  22.6 5.2 %copy-start.6 = (s32[1,6,1024]{2,0,1:T(1,128)S(1)}, s32[1,6,1024]{2,0,1:T(1,128)}, u32[]{:S(2)}) copy-start(s32[1,6,1024]{2,0,1:T(1,128)} %param.26) | copy-start | bytes 73732
  22.6 5.2 %copy-start.7 = (f32[1,6,1024]{2,0,1:T(1,128)S(1)}, f32[1,6,1024]{2,0,1:T(1,128)}, u32[]{:S(2)}) copy-start(f32[1,6,1024]{2,0,1:T(1,128)} %param.27) | copy-start | bytes 73732
  22.6 5.2 %copy-start.9 = (f32[16,16]{1,0:T(8,128)S(1)}, f32[16,16]{1,0:T(8,128)}, u32[]{:S(2)}) copy-start(f32[16,16]{1,0:T(8,128)} %stiffness.3) | copy-start | bytes 3076
  22.6 5.2 %copy-start.10 = (f32[1,16,128]{2,1,0:T(8,128)S(1)}, f32[1,16,128]{2,1,0:T(8,128)}, u32[]{:S(2)}) copy-start(f32[1,16,128]{2,1,0:T(8,128)} %param.20) | copy-start | bytes 24580
  22.6 5.2 %copy-start.11 = (s32[1,4,128]{2,1,0:T(4,128)S(1)}, s32[1,4,128]{2,1,0:T(4,128)}, u32[]{:S(2)}) copy-start(s32[1,4,128]{2,1,0:T(4,128)} %param.19) | copy-start | bytes 6148
  22.6 5.2 %copy-start.15 = (bf16[2048,1024]{1,0:T(8,128)(2,1)S(1)}, bf16[2048,1024]{1,0:T(8,128)(2,1)}, u32[]{:S(2)}) copy-start(bf16[2048,1024]{1,0:T(8,128)(2,1)} %get-tuple-element.60.xt) | copy-start | bytes 12582916
  24.9 22.1 %collective-permute-start.14 = (f32[64,4,128]{2,1,0:T(4,128)S(1)}, f32[64,4,128]{2,1,0:T(4,128)S(1)}, u32[]{:S(2)}, u32[]{:S(2)}) collective-permute-start(f32[64,4,128]{2,1,0:T(4,128)S(1)} %get-tuple-element.59), channel_id=1, source_target_pairs={{0,24},{1,25},{2,26},{3,27},{4,28},{5,29},{6,30},{7,31}} | collective-permute-start | bytes 393224 | tf_op jit(solution)/shard_map/ppermute | solution.py:837
  25.5 21.4 %collective-permute-start.15 = (f32[64,4,128]{2,1,0:T(4,128)S(1)}, f32[64,4,128]{2,1,0:T(4,128)S(1)}, u32[]{:S(2)}, u32[]{:S(2)}) collective-permute-start(f32[64,4,128]{2,1,0:T(4,128)S(1)} %get-tuple-element.59), channel_id=1, source_target_pairs={{8,24},{9,25},{10,26},{11,27},{12,28},{13,29},{14,30},{15,31}} | collective-permute-start | bytes 393224 | tf_op jit(solution)/shard_map/ppermute | solution.py:837
  26.2 20.7 %collective-permute-start.16 = (f32[64,4,128]{2,1,0:T(4,128)S(1)}, f32[64,4,128]{2,1,0:T(4,128)S(1)}, u32[]{:S(2)}, u32[]{:S(2)}) collective-permute-start(f32[64,4,128]{2,1,0:T(4,128)S(1)} %get-tuple-element.59), channel_id=1, source_target_pairs={{16,24},{17,25},{18,26},{19,27},{20,28},{21,29},{22,30},{23,31}} | collective-permute-start | bytes 393224 | tf_op jit(solution)/shard_map/ppermute | solution.py:837
  29.8 12.9 %collective-permute-start.19 = (f32[4,128,128]{2,1,0:T(8,128)S(1)}, f32[4,128,128]{2,1,0:T(8,128)S(1)}, u32[]{:S(2)}, u32[]{:S(2)}) collective-permute-start(f32[4,128,128]{2,1,0:T(8,128)S(1)} %get-tuple-element.68), channel_id=1, source_target_pairs={{0,1},{1,0},{2,3},{3,2},{4,5},{5,4},{6,7},{7,6},{8,9},{9,8},{10,11... | collective-permute-start | bytes 786440 | tf_op jit(solution)/shard_map/ppermute | solution.py:856
  29.9 12.8 %collective-permute-start.20 = (f32[4,128,128]{2,1,0:T(8,128)S(1)}, f32[4,128,128]{2,1,0:T(8,128)S(1)}, u32[]{:S(2)}, u32[]{:S(2)}) collective-permute-start(f32[4,128,128]{2,1,0:T(8,128)S(1)} %get-tuple-element.69), channel_id=1, source_target_pairs={{1,2},{3,4},{5,6},{7,8},{9,10},{11,12},{13,14},{15,16},{17,18},{19... | collective-permute-start | bytes 786440 | tf_op jit(solution)/shard_map/ppermute | solution.py:855
